TPU v7x, 32 devices: a whole 2x2x4 slice. The times are simulated.
32 devices in a mesh: seq: 16 (over z, y, x), rep: 2 (over core).
Axes of the slice: x: 2, y: 2, z: 4, core: 2. Of those that a mesh axis runs over, the one named last changes fastest.
Arguments:
- block_in: bfloat16 [2, 2048, 2048], P('rep', 'seq'), may hold values from -6 to 6
- cotangent: bfloat16 [2, 2048, 2048], P('rep', 'seq'), may hold values from -6 to 6
- domain_ids: int32 [2], replicated, may hold values from 0 to 2
- domain_weight: float32 [3], replicated, may hold values from 0.5 to 2
- lower_bound: float32 [2048], P('seq'), may hold values from 0 to 0.9998
- in_w: float32 [2048, 6144], P(('seq', 'rep')), may hold values from -0.125 to 0.125
- out_w: float32 [2048, 2048], P(('seq', 'rep')), may hold values from -0.125 to 0.125
- glu_w: float32 [2048, 11264], P(('seq', 'rep')), may hold values from -0.125 to 0.125
- down_w: float32 [5632, 2048], P(('seq', 'rep')), may hold values from -0.078125 to 0.078125
- gains: float32 [3, 2048], P(None, ('seq', 'rep')), may hold values from 0.8 to 6
- in_m: float32 [2048, 6144], P(('seq', 'rep')), may hold values from -9.1552734e-05 to 9.1552734e-05
- out_m: float32 [2048, 2048], P(('seq', 'rep')), may hold values from -9.1552734e-05 to 9.1552734e-05
- glu_m: float32 [2048, 11264], P(('seq', 'rep')), may hold values from -9.1552734e-05 to 9.1552734e-05
- down_m: float32 [5632, 2048], P(('seq', 'rep')), may hold values from -9.1552734e-05 to 9.1552734e-05
- gain_m: float32 [3, 2048], P(None, ('seq', 'rep')), may hold values from -9.1552734e-05 to 9.1552734e-05
- in_v: float32 [2048, 6144], P(('seq', 'rep')), may hold values from 5.8381244e-10 to 7.784165e-09
- out_v: float32 [2048, 2048], P(('seq', 'rep')), may hold values from 5.8381244e-10 to 7.784165e-09
- glu_v: float32 [2048, 11264], P(('seq', 'rep')), may hold values from 5.8381244e-10 to 7.784165e-09
- down_v: float32 [5632, 2048], P(('seq', 'rep')), may hold values from 5.8381244e-10 to 7.784165e-09
- gain_v: float32 [3, 2048], P(None, ('seq', 'rep')), may hold values from 5.8381244e-10 to 7.784165e-09
Outputs:
- block_out: bfloat16 [2, 2048, 2048], P('rep', 'seq')
- grad_block: float32 [2, 2048, 2048], P('rep', 'seq')
- in_new: float32 [2048, 6144], P(('seq', 'rep'))
- out_new: float32 [2048, 2048], P(('seq', 'rep'))
- glu_new: float32 [2048, 11264], P(('seq', 'rep'))
- down_new: float32 [5632, 2048], P(('seq', 'rep'))
- gain_new: float32 [3, 2048], P(None, ('seq', 'rep'))
- in_m_new: float32 [2048, 6144], P(('seq', 'rep'))
- out_m_new: float32 [2048, 2048], P(('seq', 'rep'))
- glu_m_new: float32 [2048, 11264], P(('seq', 'rep'))
- down_m_new: float32 [5632, 2048], P(('seq', 'rep'))
- gain_m_new: float32 [3, 2048], P(None, ('seq', 'rep'))
- in_v_new: float32 [2048, 6144], P(('seq', 'rep'))
- out_v_new: float32 [2048, 2048], P(('seq', 'rep'))
- glu_v_new: float32 [2048, 11264], P(('seq', 'rep'))
- down_v_new: float32 [5632, 2048], P(('seq', 'rep'))
- gain_v_new: float32 [3, 2048], P(None, ('seq', 'rep'))
- grad_norm: float32 [], replicated
All inputs are finite; a program needn't handle non-finite values.
Results may differ from a plain program's by a relative error of at most 0.012.
The roundings to bfloat16 on the way count: a program that leaves them out, or rounds other values in their place, can miss the bound.
Values may be sent and summed in bfloat16 or wider, within the bound.
No kernel may reach another device: no remote copies, remote signals or barrier semaphores. Data moves between devices by JAX's collectives and lax.ppermute only.
A program may use at most 344 MiB of HBM per device.

v0:
```python
import jax
import jax.numpy as jnp
from jax import lax
from jax.sharding import PartitionSpec as P

STEP = 10


NORM_EPS = 1e-06
CLIP_LIMIT = 1.0
BETA_FIRST = 0.9
BETA_SECOND = 0.95
ADAM_EPS = 1e-08
MATRIX_RATE = 0.04
GAIN_RATE = 0.4
MATRIX_DECAY = 0.1


def combine_steps(earlier, later):
    return (earlier[0] * later[0], later[0] * earlier[1] + later[1])


def contract(left_side, right_side, left_dim, right_dim):
    return lax.dot_general(
        left_side,
        right_side,
        (((left_dim,), (right_dim,)), ((), ())),
        preferred_element_type=jnp.float32,
    )


def silu_slope(values):
    logistic = jax.nn.sigmoid(values)
    return logistic * (1.0 + values * (1.0 - logistic))


def sequence_weights(domain_ids, domain_weight):
    kinds = domain_weight.shape[0]
    total = domain_ids.shape[0]
    same_kind = (domain_ids[:, None] == domain_ids[None, :]).astype(jnp.float32)
    counts = jnp.sum(same_kind, axis=1)
    onehot = (domain_ids[:, None] == jnp.arange(kinds, dtype=jnp.int32)[None, :]).astype(
        jnp.float32
    )
    chosen = jnp.sum(onehot * domain_weight[None, :], axis=1)
    return chosen * (total / kinds) / counts


def adam_step(weight, first, second_m, grad, factor, rate, decay):
    clipped = grad * factor
    first_new = BETA_FIRST * first + (1.0 - BETA_FIRST) * clipped
    second_new = BETA_SECOND * second_m + (1.0 - BETA_SECOND) * clipped * clipped
    first_hat = first_new / (1.0 - BETA_FIRST**STEP)
    second_hat = second_new / (1.0 - BETA_SECOND**STEP)
    weight_new = weight - rate * (first_hat / (jnp.sqrt(second_hat) + ADAM_EPS) + decay * weight)
    return (first_new, second_new, weight_new)


def squared(values):
    return jnp.sum(values * values)


def on_device(
    block_in,
    cotangent,
    domain_ids,
    domain_weight,
    lower_bound,
    in_w,
    out_w,
    glu_w,
    down_w,
    gains,
    in_m,
    out_m,
    glu_m,
    down_m,
    gain_m,
    in_v,
    out_v,
    glu_v,
    down_v,
    gain_v,
):
    inputs_f = block_in[0].astype(jnp.float32)
    tok_count, width = inputs_f.shape
    span = tok_count * lax.axis_size("seq")
    group_seqs = domain_ids.shape[0] // lax.axis_size("rep")
    seq_length = span // group_seqs
    seq_scale = sequence_weights(domain_ids, domain_weight)
    position = lax.axis_index("seq") * tok_count + jnp.arange(tok_count, dtype=jnp.int32)
    owner_seq = lax.axis_index("rep") * group_seqs + position // seq_length
    pick = (owner_seq[:, None] == jnp.arange(domain_ids.shape[0], dtype=jnp.int32)[None, :]).astype(
        jnp.float32
    )
    row_weight = jnp.sum(pick * seq_scale[None, :], axis=1)
    mix_parts = (in_w.astype(jnp.bfloat16), out_w.astype(jnp.bfloat16), gains.astype(jnp.bfloat16))
    ffn_parts = (glu_w.astype(jnp.bfloat16), down_w.astype(jnp.bfloat16))
    in_b, out_b, gain_b = (
        lax.all_gather(mix_parts[0], ("seq", "rep"), axis=0, tiled=True),
        lax.all_gather(mix_parts[1], ("seq", "rep"), axis=0, tiled=True),
        lax.all_gather(mix_parts[2], ("seq", "rep"), axis=1, tiled=True),
    )
    gain_f = gain_b.astype(jnp.float32)
    scale_one = lax.rsqrt(jnp.mean(inputs_f * inputs_f, axis=1, keepdims=True) + NORM_EPS)
    unit_one = inputs_f * scale_one
    normed = (unit_one * gain_f[0]).astype(jnp.bfloat16)
    projected = contract(in_b, normed, 0, 1)
    streams = projected[: 2 * width].astype(jnp.bfloat16).reshape(2, width, tok_count)
    gate_raw = projected[2 * width :]
    lanes = lax.all_to_all(streams, "seq", split_axis=1, concat_axis=2, tiled=True)
    channels = lanes.shape[1]
    raw_lanes = lanes.astype(jnp.float32).reshape(2, channels, group_seqs, seq_length)
    bound = lower_bound[:, None, None]
    forget_sig = jax.nn.sigmoid(raw_lanes[1])
    forget = bound + (1.0 - bound) * forget_sig
    keep_share = 1.0 - forget
    input_act = jax.nn.silu(raw_lanes[0])
    drive = input_act * keep_share
    _, state = lax.associative_scan(combine_steps, (forget, drive), axis=2)
    state_sent = state.astype(jnp.bfloat16).reshape(channels, span)
    state_back = lax.all_to_all(state_sent, "seq", split_axis=1, concat_axis=0, tiled=True)
    state_f = state_back.astype(jnp.float32)
    scale_mid = lax.rsqrt(jnp.mean(state_f * state_f, axis=0, keepdims=True) + NORM_EPS)
    unit_mid = state_f * scale_mid
    gate_act = jax.nn.silu(gate_raw)
    gain_mid = gain_f[1][:, None]
    gated = (unit_mid * gain_mid * gate_act).astype(jnp.bfloat16)
    resid = inputs_f + contract(gated, out_b, 0, 0)
    scale_two = lax.rsqrt(jnp.mean(resid * resid, axis=1, keepdims=True) + NORM_EPS)
    unit_two = resid * scale_two
    second = (unit_two * gain_f[2]).astype(jnp.bfloat16)
    glu_b, down_b = (
        lax.all_gather(ffn_parts[0], ("seq", "rep"), axis=0, tiled=True),
        lax.all_gather(ffn_parts[1], ("seq", "rep"), axis=0, tiled=True),
    )
    paired = jnp.dot(second, glu_b, preferred_element_type=jnp.float32)
    hidden_width = down_b.shape[0]
    up_gate = paired[:, :hidden_width]
    up_value = paired[:, hidden_width:]
    gate_silu = jax.nn.silu(up_gate)
    hidden = (gate_silu * up_value).astype(jnp.bfloat16)
    output = resid + jnp.dot(hidden, down_b, preferred_element_type=jnp.float32)
    block_out = output.astype(jnp.bfloat16)[None]
    glu_b, down_b = (
        lax.all_gather(ffn_parts[0], ("seq", "rep"), axis=0, tiled=True),
        lax.all_gather(ffn_parts[1], ("seq", "rep"), axis=0, tiled=True),
    )
    grad_output = cotangent[0].astype(jnp.float32) * row_weight[:, None]
    grad_output_b = grad_output.astype(jnp.bfloat16)
    grad_hidden = contract(grad_output_b, down_b, 1, 1)
    grad_up_gate = grad_hidden * up_value * silu_slope(up_gate)
    grad_up_value = grad_hidden * gate_silu
    grad_paired = jnp.concatenate([grad_up_gate, grad_up_value], axis=1).astype(jnp.bfloat16)
    grad_second = contract(grad_paired, glu_b, 1, 1)
    glu_grad = lax.psum_scatter(
        contract(second, grad_paired, 0, 0), ("seq", "rep"), scatter_dimension=0, tiled=True
    )
    down_grad = lax.psum_scatter(
        contract(hidden, grad_output_b, 0, 0), ("seq", "rep"), scatter_dimension=0, tiled=True
    )
    grad_gain_two = jnp.sum(grad_second * unit_two, axis=0)
    weighted_two = grad_second * gain_f[2]
    grad_resid = grad_output + scale_two * (
        weighted_two - unit_two * jnp.mean(weighted_two * unit_two, axis=1, keepdims=True)
    )
    in_b, out_b, gain_b = (
        lax.all_gather(mix_parts[0], ("seq", "rep"), axis=0, tiled=True),
        lax.all_gather(mix_parts[1], ("seq", "rep"), axis=0, tiled=True),
        lax.all_gather(mix_parts[2], ("seq", "rep"), axis=1, tiled=True),
    )
    gain_f = gain_b.astype(jnp.float32)
    gain_mid = gain_f[1][:, None]
    grad_resid_b = grad_resid.astype(jnp.bfloat16)
    grad_gated = contract(out_b, grad_resid_b, 1, 1)
    grad_gain_mid = jnp.sum(grad_gated * unit_mid * gate_act, axis=1)
    grad_gate = grad_gated * unit_mid * gain_mid * silu_slope(gate_raw)
    weighted_mid = grad_gated * gain_mid * gate_act
    grad_state = scale_mid * (
        weighted_mid - unit_mid * jnp.mean(weighted_mid * unit_mid, axis=0, keepdims=True)
    )
    grad_lanes = lax.all_to_all(
        grad_state.astype(jnp.bfloat16), "seq", split_axis=0, concat_axis=1, tiled=True
    )
    grad_h = grad_lanes.astype(jnp.float32).reshape(channels, group_seqs, seq_length)
    carry_rate = jnp.concatenate([forget[..., 1:], jnp.zeros_like(forget[..., :1])], axis=2)
    _, carried = lax.associative_scan(combine_steps, (carry_rate, grad_h), reverse=True, axis=2)
    previous = jnp.concatenate([jnp.zeros_like(state[..., :1]), state[..., :-1]], axis=2)
    grad_forget = carried * (previous - input_act)
    grad_in_raw = carried * keep_share * silu_slope(raw_lanes[0])
    grad_forget_raw = grad_forget * (1.0 - bound) * forget_sig * (1.0 - forget_sig)
    grad_streams = (
        jnp.stack([grad_in_raw, grad_forget_raw]).astype(jnp.bfloat16).reshape(2, channels, span)
    )
    grad_back = lax.all_to_all(grad_streams, "seq", split_axis=2, concat_axis=1, tiled=True)
    grad_proj = jnp.concatenate(
        [grad_back.reshape(2 * width, tok_count), grad_gate.astype(jnp.bfloat16)], axis=0
    )
    grad_normed = contract(grad_proj, in_b, 0, 1)
    grad_gain_one = jnp.sum(grad_normed * unit_one, axis=0)
    weighted_one = grad_normed * gain_f[0]
    grad_block = grad_resid + scale_one * (
        weighted_one - unit_one * jnp.mean(weighted_one * unit_one, axis=1, keepdims=True)
    )
    grad_gains = jnp.stack([grad_gain_one, grad_gain_mid, grad_gain_two])
    in_part = contract(normed, grad_proj, 0, 1)
    out_part = contract(gated, grad_resid_b, 1, 0)
    mix_grad = lax.psum_scatter(
        jnp.concatenate([in_part, out_part], axis=1),
        ("seq", "rep"),
        scatter_dimension=0,
        tiled=True,
    )
    in_grad = mix_grad[:, : 3 * width]
    out_grad = mix_grad[:, 3 * width :]
    local_squares = squared(glu_grad) + squared(down_grad) + squared(mix_grad)
    matrix_total, gain_total = lax.psum((local_squares, grad_gains), ("seq", "rep"))
    columns = gains.shape[1]
    gain_grad = lax.dynamic_slice_in_dim(
        gain_total, lax.axis_index(("seq", "rep")) * columns, columns, 1
    )
    squares = matrix_total + squared(gain_total)
    grad_norm = jnp.sqrt(squares)
    factor = jnp.minimum(1.0, CLIP_LIMIT / (grad_norm + 1e-06))
    in_res = adam_step(in_w, in_m, in_v, in_grad, factor, MATRIX_RATE, MATRIX_DECAY)
    out_res = adam_step(out_w, out_m, out_v, out_grad, factor, MATRIX_RATE, MATRIX_DECAY)
    glu_res = adam_step(glu_w, glu_m, glu_v, glu_grad, factor, MATRIX_RATE, MATRIX_DECAY)
    down_res = adam_step(down_w, down_m, down_v, down_grad, factor, MATRIX_RATE, MATRIX_DECAY)
    gain_res = adam_step(gains, gain_m, gain_v, gain_grad, factor, GAIN_RATE, 0.0)
    return (
        block_out,
        grad_block[None],
        in_res[2],
        out_res[2],
        glu_res[2],
        down_res[2],
        gain_res[2],
        in_res[0],
        out_res[0],
        glu_res[0],
        down_res[0],
        gain_res[0],
        in_res[1],
        out_res[1],
        glu_res[1],
        down_res[1],
        gain_res[1],
        grad_norm,
    )


def solution(mesh):
    placed = (
        P("rep", "seq", None),
        P("rep", "seq", None),
        P(),
        P(),
        P("seq"),
        P(("seq", "rep"), None),
        P(("seq", "rep"), None),
        P(("seq", "rep"), None),
        P(("seq", "rep"), None),
        P(None, ("seq", "rep")),
        P(("seq", "rep"), None),
        P(("seq", "rep"), None),
        P(("seq", "rep"), None),
        P(("seq", "rep"), None),
        P(None, ("seq", "rep")),
        P(("seq", "rep"), None),
        P(("seq", "rep"), None),
        P(("seq", "rep"), None),
        P(("seq", "rep"), None),
        P(None, ("seq", "rep")),
    )
    return jax.shard_map(
        on_device,
        mesh=mesh,
        in_specs=placed,
        out_specs=(
            P("rep", "seq", None),
            P("rep", "seq", None),
            P(("seq", "rep"), None),
            P(("seq", "rep"), None),
            P(("seq", "rep"), None),
            P(("seq", "rep"), None),
            P(None, ("seq", "rep")),
            P(("seq", "rep"), None),
            P(("seq", "rep"), None),
            P(("seq", "rep"), None),
            P(("seq", "rep"), None),
            P(None, ("seq", "rep")),
            P(("seq", "rep"), None),
            P(("seq", "rep"), None),
            P(("seq", "rep"), None),
            P(("seq", "rep"), None),
            P(None, ("seq", "rep")),
            P(),
        ),
        check_vma=False,
    )
```

profile of v0, /device:TPU:8, one launch (start us, length us, event | category | flops | bytes accessed | tf_op | source)
XLA Modules:
  0.0 2973.7 jit_solution(3105798549046529913)
XLA Ops:
  7.3 2.5 convert_element_type.109
  14.4 35.5 %all-gather = bf16[32,64,3]{1,2,0:T(4,128)(2,1)S(1)} all-gather(bf16[1,64,3]{1,2,0:T(4,128)(2,1)S(1)} %convert_bitcast_fusion.2), channel_id=1, replica_groups=mesh['seq'=16,'rep'=2] {'seq','rep'}, dimensions={0}, use_global_device_ids=true | all-gather | bytes 12672 | tf_op jit(solution)/shard_map/all_gather | solution.py:102
  50.9 114.7 %all-gather.6.cloned.1.call-done = bf16[2048,6144]{1,0:T(8,128)(2,1)} async-done(((bf16[64,6144]{1,0:T(8,128)(2,1)}), bf16[2048,6144]{1,0:T(8,128)(2,1)}) %all-gather.6.cloned.1.call-update) | async-done | bytes 25165840 | tf_op jit(solution)/shard_map/all_gather | solution.py:100
  165.5 10.1 convolution_bitcast_fusion
  178.4 3.1 copy.106
  181.4 6.1 all-to-all-start
  187.6 37.1 %all-to-all-done = bf16[2,2048,128]{2,0,1:T(2,128)(2,1)S(1)} async-done(((bf16[2,2048,128]{2,0,1:T(2,128)(2,1)}), bf16[2,2048,128]{2,0,1:T(2,128)(2,1)S(1)}, u32[]{:S(2)}, u32[]{:S(2)}) %all-to-all-start) | async-done | bytes 1048608 | tf_op jit(solution)/shard_map/all_to_all | solution.py:111
  229.5 2.6 subtract_multiply_fusion
  244.4 2.4 fusion.82
  246.9 2.5 slice.583
  249.4 2.5 slice.579
  334.1 2.5 slice.578
  356.7 2.6 pad.157
  361.4 5.0 all-to-all-start.1
  367.0 19.1 all-to-all-done.1
  386.3 2.4 multiply_convert_fusion.6
  388.7 7.5 multiply_reduce_fusion.7
  396.2 124.2 %all-gather.10.cloned.1.call-done = bf16[2048,11264]{1,0:T(8,128)(2,1)} async-done(((bf16[64,11264]{1,0:T(8,128)(2,1)}), bf16[2048,11264]{1,0:T(8,128)(2,1)}) %all-gather.10.cloned.1.call-update) | async-done | bytes 46137360 | tf_op jit(solution)/shard_map/all_gather | solution.py:134
  520.4 21.0 fusion.74
  541.3 125.2 %all-gather.12.cloned.1.call-done = bf16[5632,2048]{1,0:T(8,128)(2,1)} async-done(((bf16[176,2048]{1,0:T(8,128)(2,1)}), bf16[5632,2048]{1,0:T(8,128)(2,1)}) %all-gather.12.cloned.1.call-update) | async-done | bytes 23068688 | tf_op jit(solution)/shard_map/all_gather | solution.py:135
  666.6 15.4 multiply_convert_fusion.1
  681.9 19.4 fusion.49
  701.4 23.6 multiply_reduce_fusion.3
  727.4 7.5 multiply_reduce_fusion.4
  737.4 6.3 all-to-all-start.2
  744.8 3.6 slice.661
  748.4 3.6 slice.668
  752.1 3.6 slice.663
  755.7 4.9 slice.662
  760.6 4.7 slice.669
  765.3 4.7 slice.664
  770.1 2.6 slice_add_fusion
  773.8 8.9 reverse.6
  782.6 3.7 slice.745
  786.3 3.7 slice.666
  789.9 3.7 slice.665
  793.6 2.5 fusion.81
  796.1 2.5 slice.675
  798.6 2.5 slice.671
  882.8 2.5 slice.670
  908.3 4.5 pad.178
  912.9 2.6 pad.179
  915.5 2.6 add.633
  918.2 8.9 rev.8
  927.0 2.9 fusion.35
  930.1 9.5 copy.114
  939.6 6.9 all-to-all-start.3
  948.8 8.1 fusion.46
  956.9 26.8 all-to-all-done.3
  988.3 21.2 fusion.37
  1009.4 45.3 %pad_maximum_fusion = f32[2048,8192]{1,0:T(8,128)} fusion(f32[2048,2048]{1,0:T(8,128)} %fusion.46, f32[2048,6144]{1,0:T(8,128)} %fusion.37), kind=kLoop, calls=%fused_computation | loop fusion | flops 16777216 | bytes 134217728 | tf_op jit(solution)/shard_map/concatenate | solution.py:209
  1055.4 34.5 %fusion.4 = f32[2048,11264]{1,0:T(8,128)} fusion(bf16[128,5632]{1,0:T(8,128)(2,1)} %get-tuple-element.44, bf16[128,5632]{1,0:T(8,128)(2,1)} %get-tuple-element.43, f32[128,2048]{1,0:T(8,128)S(1)} %get-tuple-element.104, f32[2048]{0:T(1024)S(1)} %bitcast.150, f32[128]{0:T(128)S(1)} %copy-done.31), kind=kOutput, calls=%fused_computation.23 | convolution fusion | flops 5912133632 | bytes 96215552 | tf_op jit(solution)/shard_map/dot_general | solution.py:24
  1089.9 12.2 fusion.3
  1102.2 13.7 fusion.19
  1115.9 87.6 %reduce-scatter.8.cloned.1.call-done = f32[176,2048]{1,0:T(8,128)} async-done(((f32[5632,2048]{1,0:T(8,128)}), f32[176,2048]{1,0:T(8,128)}) %reduce-scatter.8.cloned.1.call-update) | async-done | bytes 1441808 | tf_op jit(solution)/shard_map/reduce_scatter | solution.py:159
  1205.9 710.5 %reduce-scatter.4.cloned.1.call-done = f32[64,8192]{1,0:T(8,128)} async-done(((f32[2048,8192]{1,0:T(8,128)}), f32[64,8192]{1,0:T(8,128)}) %reduce-scatter.4.cloned.1.call-update) | async-done | bytes 2097168 | tf_op jit(solution)/shard_map/reduce_scatter | solution.py:208
  1916.4 2.7 multiply_reduce_fusion.1
  1919.1 971.2 %reduce-scatter.6.cloned.1.call-done = f32[64,11264]{1,0:T(8,128)} async-done(((f32[2048,11264]{1,0:T(8,128)}), f32[64,11264]{1,0:T(8,128)}) %reduce-scatter.6.cloned.1.call-update) | async-done | bytes 2883600 | tf_op jit(solution)/shard_map/reduce_scatter | solution.py:156
  2890.3 3.2 multiply_reduce_fusion
  2896.8 47.7 %all-reduce.46 = (f32[]{:T(128)}, f32[3,2048]{1,0:T(4,128)S(1)}) all-reduce(f32[]{:T(128)S(6)} %add.638, f32[3,2048]{1,0:T(4,128)S(1)} %pad_maximum_fusion.18), channel_id=1, replica_groups=mesh['seq'=16,'rep'=2] {'seq','rep'}, use_global_device_ids=true, to_apply=%region_15.16 | all-reduce | flops 6145 | bytes 49160 | tf_op jit(solution)/shard_map/psum | solution.py:217
  2947.2 6.0 multiply_subtract_fusion.1
  2953.2 3.0 multiply_subtract_fusion.3
  2956.2 5.1 multiply_subtract_fusion
  2961.3 4.3 multiply_subtract_fusion.2
  (397 shorter events, 254.6 us)
Async XLA Ops:
  7.2 2.7 copy-start.21
  7.2 3.5 copy-start.3
  7.2 158.3 %all-gather.6.cloned.1.call-start = ((), (), s32[]{:S(2)}) async-start(), calls=%async_computation.7 | async-start | bytes 25952256 | tf_op jit(solution)/shard_map/all_gather | solution.py:100
  9.8 378.9 %all-gather.8.cloned.1.call-start = ((), (), s32[]{:S(2)}) async-start(), calls=%async_computation.8 | async-start | bytes 8650752 | tf_op jit(solution)/shard_map/all_gather | solution.py:101
  10.6 509.8 %all-gather.10.cloned.1.call-start = ((), (), s32[]{:S(2)}) async-start(), calls=%async_computation.9 | async-start | bytes 47579136 | tf_op jit(solution)/shard_map/all_gather | solution.py:134
  11.9 2.5 copy-start.37
  11.9 38.1 %copy-start = (bf16[1,128,2048]{2,1,0:T(8,128)(2,1)S(1)}, bf16[1,128,2048]{2,1,0:T(8,128)(2,1)}, u32[]{:S(2)}) copy-start(bf16[1,128,2048]{2,1,0:T(8,128)(2,1)} %param.20) | copy-start | bytes 1572868
  11.9 654.6 %all-gather.12.cloned.1.call-start = ((), (), s32[]{:S(2)}) async-start(), calls=%async_computation.10 | async-start | bytes 23789568 | tf_op jit(solution)/shard_map/all_gather | solution.py:135
  50.3 125.4 %copy-start.34 = (f32[128]{0:T(128)}, f32[128]{0:T(128)S(1)}, u32[]{:S(2)}) copy-start(f32[128]{0:T(128)S(1)} %add_rsqrt_fusion.2) | copy-start | bytes 1540
  175.7 1.8 copy-start.1
  177.5 10.0 copy-start.43
  181.4 43.2 %all-to-all-start = ((bf16[2,2048,128]{2,0,1:T(2,128)(2,1)}), bf16[2,2048,128]{2,0,1:T(2,128)(2,1)S(1)}, u32[]{:S(2)}, u32[]{:S(2)}) async-start(bf16[2,2048,128]{2,0,1:T(2,128)(2,1)} %copy.106), calls=%async_computation | async-start | bytes 2097152 | tf_op jit(solution)/shard_map/all_to_all | solution.py:111
  187.6 41.9 %copy-start.39 = (f32[128]{0:T(128)}, f32[128]{0:T(128)S(1)}, u32[]{:S(2)}) copy-start(f32[128]{0:T(128)S(1)} %broadcast_subtract_fusion) | copy-start | bytes 1540
  228.1 4.0 copy-start.6
  232.1 6.2 copy-start.11
  332.2 15.7 copy-start.24
  332.7 15.1 copy-start.26
  337.1 10.8 copy-start.46
  348.0 4.5 copy-start.18
  349.3 4.4 copy-start.44
  353.7 2.9 copy-start.20
  356.6 29.6 copy-start.9
  356.6 9.9 copy-start.47
  356.6 10.0 copy-start.48
  356.7 29.6 copy-start.32
  361.4 24.6 all-to-all-start.1
  366.4 837.1 %reduce-scatter.8.cloned.1.call-start = ((), (), s32[]{:S(2)}) async-start(), calls=%async_computation.13 | async-start | bytes 47579136 | tf_op jit(solution)/shard_map/reduce_scatter | solution.py:159
  396.2 328.8 %copy-start.30 = (f32[128]{0:T(128)}, f32[128]{0:T(128)S(1)}, u32[]{:S(2)}) copy-start(f32[128]{0:T(128)S(1)} %add_rsqrt_fusion) | copy-start | bytes 1540
  724.9 2.4 copy-start.2
  727.4 7.5 copy-start.7
  737.4 35.3 %all-to-all-start.2 = ((bf16[16,128,128]{1,2,0:T(8,128)(2,1)}), bf16[16,128,128]{1,2,0:T(8,128)(2,1)S(1)}, u32[]{:S(2)}, u32[]{:S(2)}) async-start(bf16[16,128,128]{1,2,0:T(8,128)(2,1)} %bitcast.144), calls=%async_computation.2 | async-start | bytes 1048576 | tf_op jit(solution)/shard_map/all_to_all | solution.py:182
  880.9 16.4 copy-start.25
  881.4 15.9 copy-start.27
  898.1 0.7 copy-start.16
  901.7 5.8 copy-start.45
  907.5 5.4 copy-start.19
  915.5 11.5 copy-start.40
  930.1 18.7 copy-start.8
  930.1 18.7 copy-start.10
  939.6 44.1 %all-to-all-start.3 = ((bf16[2,128,2048]{1,0,2:T(2,128)(2,1)}), bf16[2,128,2048]{1,0,2:T(2,128)(2,1)}, u32[]{:S(2)}, u32[]{:S(2)}) async-start(bf16[2,128,2048]{1,0,2:T(2,128)(2,1)} %copy.114), calls=%async_computation.3 | async-start | bytes 2097152 | tf_op jit(solution)/shard_map/all_to_all | solution.py:195
  946.5 969.9 %reduce-scatter.4.cloned.1.call-start = ((), (), s32[]{:S(2)}) async-start(), calls=%async_computation.11 | async-start | bytes 69206016 | tf_op jit(solution)/shard_map/reduce_scatter | solution.py:208
  956.9 31.4 %copy-start.17 = (bf16[2048,128]{1,0:T(8,128)(2,1)S(1)}, bf16[2048,128]{1,0:T(8,128)(2,1)}, u32[]{:S(2)}) copy-start(bf16[2048,128]{1,0:T(8,128)(2,1)} %copy.117) | copy-start | bytes 1572868
  956.9 31.4 %copy-start.35 = (f32[128]{0:T(128)S(1)}, f32[128]{0:T(128)}, u32[]{:S(2)}) copy-start(f32[128]{0:T(128)} %copy-done.34) | copy-start | bytes 1540
  1054.8 0.6 copy-start.31
  1054.8 1835.5 %reduce-scatter.6.cloned.1.call-start = ((), (), s32[]{:S(2)}) async-start(), calls=%async_computation.12 | async-start | bytes 95158272 | tf_op jit(solution)/shard_map/reduce_scatter | solution.py:156
  1102.1 13.7 copy-start.33
  1102.2 13.7 copy-start.36
  1919.1 1027.3 %copy-start.38 = (f32[3,64]{1,0:T(4,128)S(1)}, f32[3,64]{1,0:T(4,128)}, u32[]{:S(2)}) copy-start(f32[3,64]{1,0:T(4,128)} %param.29) | copy-start | bytes 2308
  1919.1 1027.3 %copy-start.41 = (f32[3,64]{1,0:T(4,128)S(1)}, f32[3,64]{1,0:T(4,128)}, u32[]{:S(2)}) copy-start(f32[3,64]{1,0:T(4,128)} %param.34) | copy-start | bytes 2308
  1919.1 1027.3 %copy-start.42 = (f32[3,64]{1,0:T(4,128)S(1)}, f32[3,64]{1,0:T(4,128)}, u32[]{:S(2)}) copy-start(f32[3,64]{1,0:T(4,128)} %param.39) | copy-start | bytes 2308
  2947.1 6.0 copy-start.22
  2947.1 6.0 copy-start.28
  2947.1 6.0 copy-start.29
  2947.1 9.0 copy-start.5
  2947.1 9.0 copy-start.14
  2947.2 9.0 copy-start.15
  2953.1 3.1 copy-start.4
  2956.2 5.1 copy-start.12
  2956.2 5.1 copy-start.13
  2956.2 5.1 copy-start.23
Sparse Core Ops, SparseCore 0:
  11.5 154.0 all-gather.5
  169.0 87.1 all-gather.7
  259.6 260.7 all-gather.9
  523.6 142.8 all-gather.11
  701.5 501.9 reduce-scatter.7
  1205.8 710.5 reduce-scatter.3
  1918.7 971.5 reduce-scatter.5
where the time goes:
time: 2990 us; the launch traced here: 2970 us
  waiting for transfers between devices  2220 us (74%)
  local copies, waits for them, and re-layouts  269 us (9%)
  matrix products  194 us (6%)
  other arithmetic  166 us (6%)
  blocking collectives  83.2 us (3%)
    reduce_scatter x1, waiting for transfers between devices, on_device(): lax.psum_scatter(contract(second, grad_paired, 0, 0), ('seq', 'rep'), sca...  971 us
    reduce_scatter x1, waiting for transfers between devices, on_device(): lax.psum_scatter(jnp.concatenate([in_part, out_part], axis=1), ('seq', 'r...  710 us
    dot_general x10, matrix products, contract(): lax.dot_general(left_side, right_side, (((left_dim,), (right_dim,)), ((),...  161 us
    all_gather x1, waiting for transfers between devices, on_device(): lax.all_gather(ffn_parts[1], ('seq', 'rep'), axis=0, tiled=True)  125 us
    all_gather x1, waiting for transfers between devices, on_device(): lax.all_gather(ffn_parts[0], ('seq', 'rep'), axis=0, tiled=True)  124 us
    slice x70, local copies, waits for them, and re-layouts, on_device(): lax.associative_scan(combine_steps, (carry_rate, grad_h), reverse=True, a...  115 us
    all_gather x1, waiting for transfers between devices, on_device(): lax.all_gather(mix_parts[0], ('seq', 'rep'), axis=0, tiled=True)  115 us
    slice x67, local copies, waits for them, and re-layouts, on_device(): _, state = lax.associative_scan(combine_steps, (forget, drive), axis=2)  90.9 us
  transfers between devices with their start and end apart: 11, of which 9 were waited for; matrix products, arithmetic and copies ran while one was open for 19% of the time, Pallas kernels for 0%

commit v1 on v0

v1 whole, which is shorter than its diff:
```python
import functools

import jax
import jax.numpy as jnp
import numpy as np
from jax import lax
from jax.experimental import pallas as pl
from jax.experimental.pallas import tpu as pltpu
from jax.sharding import Mesh, PartitionSpec as P

STEP = 10

NORM_EPS = 1e-06
CLIP_LIMIT = 1.0
BETA_FIRST = 0.9
BETA_SECOND = 0.95
ADAM_EPS = 1e-08
MATRIX_RATE = 0.04
GAIN_RATE = 0.4
MATRIX_DECAY = 0.1

LINE = "z"
PLANE = ("y", "x")
CORE = "core"
OWNERS = ("z", "core")


def contract(left_side, right_side, left_dim, right_dim):
    return lax.dot_general(
        left_side,
        right_side,
        (((left_dim,), (right_dim,)), ((), ())),
        preferred_element_type=jnp.float32,
    )


def rounded(values):
    return lax.reduce_precision(values, exponent_bits=8, mantissa_bits=7)


def silu_slope(values):
    logistic = jax.nn.sigmoid(values)
    return logistic * (1.0 + values * (1.0 - logistic))


def sequence_weights(domain_ids, domain_weight):
    kinds = domain_weight.shape[0]
    total = domain_ids.shape[0]
    same_kind = (domain_ids[:, None] == domain_ids[None, :]).astype(jnp.float32)
    counts = jnp.sum(same_kind, axis=1)
    onehot = (domain_ids[:, None] == jnp.arange(kinds, dtype=jnp.int32)[None, :]).astype(
        jnp.float32
    )
    chosen = jnp.sum(onehot * domain_weight[None, :], axis=1)
    return chosen * (total / kinds) / counts


def adam_step(weight, first, second_m, grad, factor, rate, decay):
    clipped = grad * factor
    first_new = BETA_FIRST * first + (1.0 - BETA_FIRST) * clipped
    second_new = BETA_SECOND * second_m + (1.0 - BETA_SECOND) * clipped * clipped
    first_hat = first_new / (1.0 - BETA_FIRST**STEP)
    second_hat = second_new / (1.0 - BETA_SECOND**STEP)
    weight_new = weight - rate * (first_hat / (jnp.sqrt(second_hat) + ADAM_EPS) + decay * weight)
    return (first_new, second_new, weight_new)


def squared(values):
    values = values.astype(jnp.float32)
    return jnp.sum(values * values)


def swap(values, axis, bit):
    size = lax.axis_size(axis)
    return lax.ppermute(values, axis, [(i, i ^ bit) for i in range(size)])


def gather_small(values, axis):
    size = lax.axis_size(axis)
    held = lax.dynamic_update_index_in_dim(
        jnp.zeros((size,) + values.shape, values.dtype), values, lax.axis_index(axis), 0
    )
    bit = 1
    while bit < size:
        held = held + swap(held, axis, bit)
        bit *= 2
    return held


def total_small(values, axes):
    for axis in axes:
        bit = 1
        while bit < lax.axis_size(axis):
            values = values + swap(values, axis, bit)
            bit *= 2
    return values


def gather_plane(values):
    return jnp.concatenate(
        [values] + [swap(values, PLANE, k) for k in range(1, lax.axis_size(PLANE))], axis=0
    )


def total_plane(values):
    size = lax.axis_size(PLANE)
    blocks = values.reshape(size, values.shape[0] // size)
    bit = 1
    while bit < size:
        other = swap(blocks, PLANE, bit)
        blocks = blocks + jnp.stack([other[k ^ bit] for k in range(size)])
        bit *= 2
    return blocks.reshape(values.shape)


def scatter_plane(partial):
    size = lax.axis_size(PLANE)
    rows = partial.shape[0] // size
    total = partial[:rows]
    for k in range(1, size):
        total = total + swap(
            partial[k * rows : (k + 1) * rows].astype(jnp.bfloat16), PLANE, k
        ).astype(jnp.float32)
    return total


def exchange_plane(blocks):
    rank = lax.axis_index(PLANE)
    result = blocks
    for k in range(1, blocks.shape[0]):
        sent = lax.dynamic_index_in_dim(blocks, rank ^ k, 0, keepdims=False)
        result = lax.dynamic_update_index_in_dim(result, swap(sent, PLANE, k), rank ^ k, 0)
    return result


TILE = 8


def gates(proj_ref, rows, width, bound):
    in_raw = proj_ref[rows, 0:width].astype(jnp.bfloat16).astype(jnp.float32)
    forget_raw = proj_ref[rows, width : 2 * width].astype(jnp.bfloat16).astype(jnp.float32)
    forget = bound + (1.0 - bound) * jax.nn.sigmoid(forget_raw)
    return in_raw, forget


def scan_kernel(width, order_ref, proj_ref, bound_ref, state_ref, prod_ref, last_ref):
    blocks = order_ref.shape[0]
    per_block = proj_ref.shape[0] // blocks // TILE
    bound = bound_ref[0:1, :]
    row = lax.broadcasted_iota(jnp.int32, (TILE, width), 0)

    def step(index, carry):
        state_in, prod_in = carry
        tile = order_ref[index // per_block] * per_block + index % per_block
        rows = pl.ds(pl.multiple_of(tile * TILE, TILE), TILE)
        in_raw, forget = gates(proj_ref, rows, width, bound)
        drive = in_raw * jax.nn.sigmoid(in_raw) * (1.0 - forget)
        for shift in (1, 2, 4):
            keep = row >= shift
            drive = jnp.where(keep, forget * pltpu.roll(drive, shift, 0) + drive, drive)
            forget = jnp.where(keep, forget * pltpu.roll(forget, shift, 0), forget)
        state = drive + forget * state_in
        prod = forget * prod_in
        state_ref[rows, :] = state
        prod_ref[rows, :] = prod
        return state[TILE - 1 : TILE, :], prod[TILE - 1 : TILE, :]

    state, prod = lax.fori_loop(
        0,
        blocks * per_block,
        step,
        (jnp.zeros((1, width), jnp.float32), jnp.ones((1, width), jnp.float32)),
    )
    last_ref[0:1, :] = state
    last_ref[1:2, :] = prod


def back_kernel(width, order_ref, proj_ref, bound_ref, grad_ref, carried_ref, prod_ref, last_ref):
    blocks = order_ref.shape[0]
    per_block = proj_ref.shape[0] // blocks // TILE
    count = blocks * per_block
    bound = bound_ref[0:1, :]
    row = lax.broadcasted_iota(jnp.int32, (TILE, width), 0)

    def step(back, carry):
        carried_in, prod_in, forget_next = carry
        index = count - 1 - back
        tile = order_ref[index // per_block] * per_block + index % per_block
        rows = pl.ds(pl.multiple_of(tile * TILE, TILE), TILE)
        _, forget = gates(proj_ref, rows, width, bound)
        rate = jnp.where(row < TILE - 1, pltpu.roll(forget, TILE - 1, 0), forget_next)
        carried = grad_ref[rows, :].astype(jnp.float32)
        for shift in (1, 2, 4):
            keep = row < TILE - shift
            carried = jnp.where(
                keep, rate * pltpu.roll(carried, TILE - shift, 0) + carried, carried
            )
            rate = jnp.where(keep, rate * pltpu.roll(rate, TILE - shift, 0), rate)
        carried = carried + rate * carried_in
        prod = rate * prod_in
        carried_ref[rows, :] = carried
        prod_ref[rows, :] = prod
        return carried[0:1, :], prod[0:1, :], forget[0:1, :]

    ones = jnp.ones((1, width), jnp.float32)
    carried, prod, forget = lax.fori_loop(
        0, count, step, (jnp.zeros((1, width), jnp.float32), ones, ones)
    )
    last_ref[0:1, :] = forget * carried
    last_ref[1:2, :] = forget * prod


def call_scan(kernel, order, *arrays):
    tokens = arrays[0].shape[0]
    width = arrays[1].shape[1]
    vmem = pl.BlockSpec(memory_space=pltpu.VMEM)
    full = jax.ShapeDtypeStruct((tokens, width), jnp.float32)
    return pl.pallas_call(
        functools.partial(kernel, width),
        out_shape=(full, full, jax.ShapeDtypeStruct((2, width), jnp.float32)),
        in_specs=[pl.BlockSpec(memory_space=pltpu.SMEM)] + [vmem] * len(arrays),
        out_specs=(vmem, vmem, vmem),
        compiler_params=pltpu.CompilerParams(vmem_limit_bytes=32 * 1024 * 1024),
    )(order, *arrays)


def on_device(
    block_in,
    cotangent,
    domain_ids,
    domain_weight,
    lower_bound,
    in_w,
    out_w,
    glu_w,
    down_w,
    gains,
    in_m,
    out_m,
    glu_m,
    down_m,
    gain_m,
    in_v,
    out_v,
    glu_v,
    down_v,
    gain_v,
):
    bf16 = jnp.bfloat16
    f32 = jnp.float32
    inputs_f = block_in[0].astype(f32)
    tok, width = inputs_f.shape
    line = lax.axis_size(LINE)
    plane = lax.axis_size(PLANE)
    cores = lax.axis_size(CORE)
    level = lax.axis_index(LINE)
    rank = lax.axis_index(PLANE)
    device = lax.axis_index((LINE,) + PLANE)
    order = jnp.arange(plane, dtype=jnp.int32) ^ rank
    group_seqs = domain_ids.shape[0] // cores
    assert group_seqs == 1
    span = tok * line * plane
    rows = in_w.shape[0]
    chan = lower_bound.shape[0]
    channels = chan * line
    hidden_rows = down_w.shape[0] * cores
    hidden_width = hidden_rows * line

    seq_scale = sequence_weights(domain_ids, domain_weight)
    position = device * tok + jnp.arange(tok, dtype=jnp.int32)
    owner_seq = lax.axis_index(CORE) * group_seqs + position // (span // group_seqs)
    pick = (owner_seq[:, None] == jnp.arange(domain_ids.shape[0], dtype=jnp.int32)[None, :]).astype(
        f32
    )
    row_weight = jnp.sum(pick * seq_scale[None, :], axis=1)

    def feature_swap(values, outer, inner):
        count = values.shape[0]
        return (
            values.reshape(count, line, outer, inner, rows)
            .transpose(0, 1, 3, 2, 4)
            .reshape(count, width)
        )

    in_blocks = (
        in_w.astype(bf16)
        .reshape(rows, 3, line, plane, chan)
        .transpose(3, 0, 1, 2, 4)
        .reshape(plane, rows, 3 * channels)
    )
    in_held = exchange_plane(in_blocks).reshape(plane * rows, 3 * channels)
    in_b = lax.all_gather(in_held, OWNERS, axis=0, tiled=True)
    out_b = lax.all_gather(out_w.astype(bf16), OWNERS, axis=0, tiled=True)
    glu_blocks = (
        glu_w.astype(bf16)
        .reshape(rows, 2, line, plane, hidden_rows)
        .transpose(3, 0, 1, 2, 4)
        .reshape(plane, rows, 2 * hidden_width)
    )
    glu_held = exchange_plane(glu_blocks).reshape(plane * rows, 2 * hidden_width)
    glu_b = lax.all_gather(glu_held, OWNERS, axis=0, tiled=True)
    down_b = lax.all_gather(down_w.astype(bf16), OWNERS, axis=0, tiled=True)

    gain_size = 3 * gains.shape[1]
    packed = jnp.concatenate([rounded(gains).reshape(-1), lower_bound])
    packed = gather_small(packed, LINE)
    bound = packed[:, gain_size:].reshape(1, channels)
    held_gains = gather_small(packed[:, :gain_size], CORE)
    gain_mid = (
        held_gains.reshape(cores, line, 3, gains.shape[1])[:, :, 1]
        .transpose(1, 0, 2)
        .reshape(1, channels)
    )
    held_gains = gather_small(gather_small(held_gains, "x"), "y")
    gain_f = (
        held_gains.reshape(plane, cores, line, 3, gains.shape[1])
        .transpose(3, 2, 0, 1, 4)
        .reshape(3, width)
    )

    grad_output = cotangent[0].astype(f32) * row_weight[:, None]
    grad_output_b = gather_plane(grad_output.astype(bf16))

    scale_one = lax.rsqrt(jnp.mean(inputs_f * inputs_f, axis=1, keepdims=True) + NORM_EPS)
    unit_one = inputs_f * scale_one
    normed = gather_plane(feature_swap((unit_one * gain_f[0]).astype(bf16), plane, cores))
    proj = contract(normed, in_b, 1, 0)
    local_state, local_prod, last = call_scan(scan_kernel, order, proj, bound)
    lasts = gather_small(last, LINE)
    state_in = jnp.zeros((channels,), f32)
    for k in range(line):
        state_in = jnp.where(k < level, lasts[k, 1] * state_in + lasts[k, 0], state_in)
    state = local_state + local_prod * state_in[None, :]
    state_f = rounded(state)
    square_mid = total_plane(jnp.sum(state_f * state_f, axis=1))
    scale_mid = lax.rsqrt(square_mid / width + NORM_EPS)[:, None]
    unit_mid = state_f * scale_mid
    gate_raw = proj[:, 2 * channels :]
    gate_act = jax.nn.silu(gate_raw)
    gated = (unit_mid * gain_mid * gate_act).astype(bf16)
    resid = inputs_f + scatter_plane(contract(gated, out_b, 1, 0))

    scale_two = lax.rsqrt(jnp.mean(resid * resid, axis=1, keepdims=True) + NORM_EPS)
    unit_two = resid * scale_two
    second = gather_plane(feature_swap((unit_two * gain_f[2]).astype(bf16), plane, cores))
    paired = contract(second, glu_b, 1, 0)
    up_gate = paired[:, :hidden_width]
    up_value = paired[:, hidden_width:]
    gate_silu = jax.nn.silu(up_gate)
    hidden = (gate_silu * up_value).astype(bf16)
    output = resid + scatter_plane(contract(hidden, down_b, 1, 0))
    block_out = output.astype(bf16)[None]

    grad_hidden = contract(grad_output_b, down_b, 1, 1)
    grad_paired = jnp.concatenate(
        [grad_hidden * up_value * silu_slope(up_gate), grad_hidden * gate_silu], axis=1
    ).astype(bf16)
    grad_second = feature_swap(scatter_plane(contract(grad_paired, glu_b, 1, 1)), cores, plane)
    glu_part = contract(second, grad_paired, 0, 0).astype(bf16)
    down_part = contract(hidden, grad_output_b, 0, 0).astype(bf16)
    glu_held = lax.psum_scatter(glu_part, OWNERS, scatter_dimension=0, tiled=True)
    down_grad = lax.psum_scatter(down_part, OWNERS, scatter_dimension=0, tiled=True)
    grad_gain_two = jnp.sum(grad_second * unit_two, axis=0)
    weighted_two = grad_second * gain_f[2]
    grad_resid = grad_output + scale_two * (
        weighted_two - unit_two * jnp.mean(weighted_two * unit_two, axis=1, keepdims=True)
    )

    grad_resid_b = gather_plane(grad_resid.astype(bf16))
    grad_gated = contract(grad_resid_b, out_b, 1, 1)
    out_part = contract(gated, grad_resid_b, 0, 0).astype(bf16)
    out_grad = lax.psum_scatter(out_part, OWNERS, scatter_dimension=0, tiled=True)
    grad_gain_mid = jnp.sum(grad_gated * unit_mid * gate_act, axis=0)
    grad_gate = grad_gated * unit_mid * gain_mid * silu_slope(gate_raw)
    weighted_mid = grad_gated * gain_mid * gate_act
    mean_mid = total_plane(jnp.sum(weighted_mid * unit_mid, axis=1)) / width
    grad_state = scale_mid * (weighted_mid - unit_mid * mean_mid[:, None])
    local_carried, local_rate, first = call_scan(
        back_kernel, order, proj, bound, rounded(grad_state)
    )
    firsts = gather_small(first, LINE)
    carried_in = jnp.zeros((channels,), f32)
    for k in range(line - 1, -1, -1):
        carried_in = jnp.where(k > level, firsts[k, 1] * carried_in + firsts[k, 0], carried_in)
    carried = local_carried + local_rate * carried_in[None, :]
    blocked = state.reshape(plane, tok, channels)
    tails = lax.dynamic_update_index_in_dim(
        jnp.zeros((plane, channels), f32), state_in, order[0], 0
    )
    for k in range(1, plane):
        tails = lax.dynamic_update_index_in_dim(
            tails,
            lax.dynamic_index_in_dim(blocked, order[k - 1], 0, keepdims=False)[tok - 1],
            order[k],
            0,
        )
    previous = jnp.concatenate([tails[:, None], blocked[:, :-1]], axis=1).reshape(state.shape)
    in_raw = rounded(proj[:, :channels])
    forget_sig = jax.nn.sigmoid(rounded(proj[:, channels : 2 * channels]))
    forget = bound + (1.0 - bound) * forget_sig
    grad_in_raw = carried * (1.0 - forget) * silu_slope(in_raw)
    grad_forget_raw = (
        carried
        * (previous - jax.nn.silu(in_raw))
        * (1.0 - bound)
        * forget_sig
        * (1.0 - forget_sig)
    )
    grad_proj = jnp.concatenate([grad_in_raw, grad_forget_raw, grad_gate], axis=1).astype(bf16)
    in_part = contract(normed, grad_proj, 0, 0).astype(bf16)
    in_held = lax.psum_scatter(in_part, OWNERS, scatter_dimension=0, tiled=True)
    grad_normed = feature_swap(scatter_plane(contract(grad_proj, in_b, 1, 1)), cores, plane)
    grad_gain_one = jnp.sum(grad_normed * unit_one, axis=0)
    weighted_one = grad_normed * gain_f[0]
    grad_block = grad_resid + scale_one * (
        weighted_one - unit_one * jnp.mean(weighted_one * unit_one, axis=1, keepdims=True)
    )

    glu_grad = (
        exchange_plane(glu_held.reshape(plane, rows, 2 * hidden_width))
        .reshape(plane, rows, 2, line, hidden_rows)
        .transpose(1, 2, 3, 0, 4)
        .reshape(glu_w.shape)
        .astype(f32)
    )
    in_grad = (
        exchange_plane(in_held.reshape(plane, rows, 3 * channels))
        .reshape(plane, rows, 3, line, chan)
        .transpose(1, 2, 3, 0, 4)
        .reshape(in_w.shape)
        .astype(f32)
    )
    out_grad = out_grad.astype(f32)
    down_grad = down_grad.astype(f32)

    mid_row = lax.dynamic_update_index_in_dim(
        jnp.zeros((line, plane, chan), f32), grad_gain_mid.reshape(line, chan), rank, 1
    ).reshape(width)
    everyone = (CORE, "x", "y", LINE)
    gain_total = total_small(jnp.stack([grad_gain_one, mid_row, grad_gain_two]), everyone)
    squares = total_small(
        squared(glu_held) + squared(down_grad) + squared(out_grad) + squared(in_held), everyone
    ) + squared(gain_total)
    columns = gains.shape[1]
    gain_grad = lax.dynamic_slice_in_dim(
        gain_total, (device * cores + lax.axis_index(CORE)) * columns, columns, 1
    )
    grad_norm = jnp.sqrt(squares)
    factor = jnp.minimum(1.0, CLIP_LIMIT / (grad_norm + 1e-06))
    in_res = adam_step(in_w, in_m, in_v, in_grad, factor, MATRIX_RATE, MATRIX_DECAY)
    out_res = adam_step(out_w, out_m, out_v, out_grad, factor, MATRIX_RATE, MATRIX_DECAY)
    glu_res = adam_step(glu_w, glu_m, glu_v, glu_grad, factor, MATRIX_RATE, MATRIX_DECAY)
    down_res = adam_step(down_w, down_m, down_v, down_grad, factor, MATRIX_RATE, MATRIX_DECAY)
    gain_res = adam_step(gains, gain_m, gain_v, gain_grad, factor, GAIN_RATE, 0.0)
    return (
        block_out,
        grad_block[None],
        in_res[2],
        out_res[2],
        glu_res[2],
        down_res[2],
        gain_res[2],
        in_res[0],
        out_res[0],
        glu_res[0],
        down_res[0],
        gain_res[0],
        in_res[1],
        out_res[1],
        glu_res[1],
        down_res[1],
        gain_res[1],
        grad_norm,
    )


def split_mesh(mesh):
    seq, cores = mesh.shape["seq"], mesh.shape["rep"]
    side = 1
    while (2 * side) ** 3 <= seq:
        side *= 2
    return Mesh(
        mesh.devices.reshape(seq // (side * side), side, side, cores), (LINE,) + PLANE + (CORE,)
    )


def solution(mesh):
    tokens = P(CORE, (LINE,) + PLANE, None)
    matrix = P((LINE,) + PLANE + (CORE,), None)
    vectors = P(None, (LINE,) + PLANE + (CORE,))
    state = (matrix, matrix, matrix, matrix, vectors)
    return jax.shard_map(
        on_device,
        mesh=split_mesh(mesh),
        in_specs=(tokens, tokens, P(), P(), P((LINE,) + PLANE)) + state * 3,
        out_specs=(tokens, tokens) + state * 3 + (P(),),
        check_vma=False,
    )
```

time: 2990 us -> 821 us (0.27)
  waiting for transfers between devices: 2220 us -> 460 us
  local copies, waits for them, and re-layouts: 269 us -> 67.8 us
  other arithmetic: 166 us -> 57 us
  matrix products: 194 us -> 88.6 us
  blocking collectives: 83.2 us -> 0 us
  starting transfers between devices: 25.2 us -> 101 us
    reduce_scatter x3 -> x4, waiting for transfers between devices: 1770 us -> 191 us  [the longest x1 109 us: on_device(): lax.psum_scatter(glu_part, OWNERS, scatter_dimension=0, tiled=True)]
    all_gather x4, waiting for transfers between devices: 364 us -> 71.4 us  [the longest x1 49.8 us: on_device(): down_b = lax.all_gather(down_w.astype(bf16), OWNERS, axis=0, tiled=True)]
    slice x141 -> x14, local copies, waits for them, and re-layouts: 209 us -> 3.3 us  [the longest x4 2.63 us: scatter_plane(): partial[k * rows:(k + 1) * rows].astype(jnp.bfloat16)]
    ppermute x0 -> x59, waiting for transfers between devices: none -> 197 us  [swap(): return lax.ppermute(values, axis, [(i, i ^ bit) for i in range(size)])]
    ppermute x0 -> x59, starting transfers between devices: none -> 100 us  [swap(): return lax.ppermute(values, axis, [(i, i ^ bit) for i in range(size)])]
    all_to_all x4 -> x0, waiting for transfers between devices: 83 us -> none  [the longest x1 37.1 us: on_device(): lax.all_to_all(streams, 'seq', split_axis=1, concat_axis=2, tiled=True)]
    dot_general x10 -> x12, matrix products: 161 us -> 88.6 us  [contract(): lax.dot_general(left_side, right_side, (((left_dim,), (right_dim,)), ((),...]
    concatenate x21 -> x2, other arithmetic: 57.5 us -> 0.21 us  [the longest x1 0.13 us: on_device(): jnp.concatenate([tails[:, None], blocked[:, :-1]], axis=1)]
  transfers between devices with their start and end apart: 11 -> 67, of which waited for: 9 -> 50; matrix products, arithmetic and copies ran while one was open for 19% -> 16% of each run, Pallas kernels for 0% -> 0%
where the time goes in v1:
time: 821 us; the launch traced here: 811 us
  waiting for transfers between devices  460 us (56%)
  starting transfers between devices  101 us (12%)
  matrix products  88.6 us (11%)
  local copies, waits for them, and re-layouts  67.8 us (8%)
  other arithmetic  57 us (7%)
  between operations  30.7 us (4%)
    ppermute x59, waiting for transfers between devices, swap(): return lax.ppermute(values, axis, [(i, i ^ bit) for i in range(size)])  197 us
    reduce_scatter x1, waiting for transfers between devices, on_device(): lax.psum_scatter(glu_part, OWNERS, scatter_dimension=0, tiled=True)  109 us
    ppermute x59, starting transfers between devices, swap(): return lax.ppermute(values, axis, [(i, i ^ bit) for i in range(size)])  100 us
    dot_general x12, matrix products, contract(): lax.dot_general(left_side, right_side, (((left_dim,), (right_dim,)), ((),...  88.6 us
    reduce_scatter x1, waiting for transfers between devices, on_device(): lax.psum_scatter(down_part, OWNERS, scatter_dimension=0, tiled=True)  65.1 us
    all_gather x1, waiting for transfers between devices, on_device(): down_b = lax.all_gather(down_w.astype(bf16), OWNERS, axis=0, tiled=True)  49.8 us
    all_gather x1, waiting for transfers between devices, on_device(): glu_b = lax.all_gather(glu_held, OWNERS, axis=0, tiled=True)  21.6 us
    reduce_scatter x1, waiting for transfers between devices, on_device(): lax.psum_scatter(out_part, OWNERS, scatter_dimension=0, tiled=True)  17.3 us
  transfers between devices with their start and end apart: 67, of which 50 were waited for; matrix products, arithmetic and copies ran while one was open for 16% of the time, Pallas kernels for 0%

profile of v1, /device:TPU:8, one launch (start us, length us, event | category | flops | bytes accessed | tf_op | source)
XLA Modules:
  0.0 811.5 jit_solution(11510350280042954862)
XLA Ops:
  14.1 5.5 collective-permute-done.8
  24.3 7.0 collective-permute-done.9
  34.9 4.3 reshape.390
  42.8 6.7 collective-permute-done.21
  49.6 2.5 collective-permute-start.22
  53.1 13.3 %collective-permute-done.22 = bf16[64,2816]{1,0:T(8,128)(2,1)S(1)} collective-permute-done((bf16[64,2816]{1,0:T(8,128)(2,1)S(1)}, bf16[64,2816]{1,0:T(8,128)(2,1)S(1)}, u32[]{:S(2)}, u32[]{:S(2)}) %collective-permute-start.22) | collective-permute-done | bytes 360480 | tf_op jit(solution)/shard_map/ppermute | solution.py:75
  68.3 3.4 collective-permute-done
  71.8 4.4 collective-permute-start.1
  87.6 2.6 collective-permute-start.7
  91.3 12.2 %collective-permute-done.7 = bf16[128,2048]{0,1:T(8,128)(2,1)S(1)} collective-permute-done((bf16[128,2048]{0,1:T(8,128)(2,1)S(1)}, bf16[128,2048]{0,1:T(8,128)(2,1)S(1)}, u32[]{:S(2)}, u32[]{:S(2)}) %collective-permute-start.7) | collective-permute-done | bytes 524320 | tf_op jit(solution)/shard_map/ppermute | solution.py:75
  103.5 9.0 %collective-permute-done.6 = bf16[128,2048]{0,1:T(8,128)(2,1)S(1)} collective-permute-done((bf16[128,2048]{0,1:T(8,128)(2,1)S(1)}, bf16[128,2048]{0,1:T(8,128)(2,1)S(1)}, u32[]{:S(2)}, u32[]{:S(2)}) %collective-permute-start.6) | collective-permute-done | bytes 524320 | tf_op jit(solution)/shard_map/ppermute | solution.py:75
  114.1 6.2 fusion.50.proj_ref
  120.4 3.3 shard_map.331
  129.5 4.9 collective-permute-start.12
  137.1 2.9 multiply_reduce_fusion.7
  149.7 5.0 fusion.105
  159.9 12.1 %collective-permute-done.17 = bf16[128,2048]{1,0:T(8,128)(2,1)} collective-permute-done((bf16[128,2048]{1,0:T(8,128)(2,1)}, bf16[128,2048]{1,0:T(8,128)(2,1)}, u32[]{:S(2)}, u32[]{:S(2)}) %collective-permute-start.17) | collective-permute-done | bytes 524320 | tf_op jit(solution)/shard_map/ppermute | solution.py:75
  172.0 6.6 collective-permute-done.16
  194.6 7.6 collective-permute-done.20
  203.3 10.2 %collective-permute-done.19 = bf16[128,2048]{0,1:T(8,128)(2,1)S(1)} collective-permute-done((bf16[128,2048]{0,1:T(8,128)(2,1)S(1)}, bf16[128,2048]{0,1:T(8,128)(2,1)S(1)}, u32[]{:S(2)}, u32[]{:S(2)}) %collective-permute-start.19) | collective-permute-done | bytes 524320 | tf_op jit(solution)/shard_map/ppermute | solution.py:75
  214.3 21.6 %all-gather.9.cloned.1.call-done = bf16[2048,2816]{1,0:T(8,128)(2,1)} async-done(((bf16[256,2816]{1,0:T(8,128)(2,1)}), bf16[2048,2816]{1,0:T(8,128)(2,1)}) %all-gather.9.cloned.1.call-update) | async-done | bytes 11534352 | tf_op jit(solution)/shard_map/all_gather | solution.py:301
  236.0 11.9 %fusion.49 = f32[512,2816]{1,0:T(8,128)} fusion(bf16[2048,2816]{1,0:T(8,128)(2,1)} %all-gather.9.cloned.1.call-done, bf16[128,2048]{0,1:T(8,128)(2,1)} %copy-done.49, bf16[128,2048]{0,1:T(8,128)(2,1)} %copy-done.51, bf16[128,2048]{0,1:T(8,128)(2,1)} %collective-permute-done.18, bf16[128,2048]{0,1:T(8,128)(2,1)} %bitcast.250), kind=kOutput, calls=%fused_computation.128 | convolution fusion | flops 5913968640 | bytes 19398656 | tf_op jit(solution)/shard_map/dot_general | solution.py:29
  247.9 49.8 %all-gather.11.cloned.1.call-done = bf16[1408,2048]{1,0:T(8,128)(2,1)} async-done(((bf16[176,2048]{1,0:T(8,128)(2,1)}), bf16[1408,2048]{1,0:T(8,128)(2,1)}) %all-gather.11.cloned.1.call-update) | async-done | bytes 5767184 | tf_op jit(solution)/shard_map/all_gather | solution.py:302
  297.7 10.5 %multiply_convert_fusion.1 = (bf16[512,1408]{1,0:T(8,128)(2,1)S(1)}, bf16[512,1408]{1,0:T(8,128)(2,1)}, bf16[512,1408]{1,0:T(8,128)(2,1)S(1)}) fusion(f32[512,2816]{1,0:T(8,128)} %fusion.49, bf16[1408,2048]{1,0:T(8,128)(2,1)} %all-gather.11.cloned.1.call-done, bf16[128,2048]{1,0:T(8,128)(2,1)} %collective-permute-done.29, ...), kind=kOutput, calls=%fused_computation.13 | convolution fusion | flops 2971992064 | bytes 17956864 | tf_op jit(solution)/shard_map/dot_general | solution.py:29
  308.2 10.5 %fusion.106 = (bf16[512,2048]{1,0:T(8,128)(2,1)S(1)}, f32[512,2048]{1,0:T(8,128)S(1)}) fusion(bf16[2048,2816]{1,0:T(8,128)(2,1)} %all-gather.9.cloned.1.call-done, bf16[512,1408]{1,0:T(8,128)(2,1)} %get-tuple-element.62, bf16[512,1408]{1,0:T(8,128)(2,1)S(1)} %get-tuple-element.61), kind=kOutput, calls=%fused_computation.250 | convolution fusion | flops 5912395776 | bytes 20709376 | tf_op jit(solution)/shard_map/dot_general | solution.py:29
  318.9 2.5 collective-permute-start.32
  322.5 5.3 fusion.107
  329.0 2.4 collective-permute-start.26
  332.0 2.7 collective-permute-done.32
  336.2 9.8 %collective-permute-done.31 = bf16[128,2048]{1,0:T(8,128)(2,1)S(1)} collective-permute-done((bf16[128,2048]{1,0:T(8,128)(2,1)S(1)}, bf16[128,2048]{1,0:T(8,128)(2,1)S(1)}, u32[]{:S(2)}, u32[]{:S(2)}) %collective-permute-start.31) | collective-permute-done | bytes 524320 | tf_op jit(solution)/shard_map/ppermute | solution.py:75
  347.3 2.5 copy.75
  352.1 2.5 copy.77
  357.3 10.5 %collective-permute-done.25 = bf16[128,2048]{1,0:T(8,128)(2,1)} collective-permute-done((bf16[128,2048]{1,0:T(8,128)(2,1)}, bf16[128,2048]{1,0:T(8,128)(2,1)}, u32[]{:S(2)}, u32[]{:S(2)}) %collective-permute-start.25) | collective-permute-done | bytes 524320 | tf_op jit(solution)/shard_map/ppermute | solution.py:75
  367.9 3.6 fusion.90
  380.9 6.7 collective-permute-done.35
  387.6 10.1 %collective-permute-done.34 = bf16[128,2048]{1,0:T(8,128)(2,1)} collective-permute-done((bf16[128,2048]{1,0:T(8,128)(2,1)}, bf16[128,2048]{1,0:T(8,128)(2,1)}, u32[]{:S(2)}, u32[]{:S(2)}) %collective-permute-start.34) | collective-permute-done | bytes 524320 | tf_op jit(solution)/shard_map/ppermute | solution.py:75
  397.8 4.1 multiply_reduce_fusion.3
  410.0 3.2 shard_map.332
  413.3 2.6 collective-permute-start.38
  419.4 2.8 collective-permute-done.39
  424.4 5.3 convolution_convert_fusion.2
  430.7 4.1 convolution_convert_fusion.3
  436.4 7.3 convolution_convert_fusion.1
  445.5 10.5 %convolution_convert_fusion = bf16[2048,2816]{1,0:T(8,128)(2,1)} fusion(bf16[512,1408]{1,0:T(8,128)(2,1)} %get-tuple-element.62, bf16[512,1408]{1,0:T(8,128)(2,1)S(1)} %copy-done.58, bf16[128,2048]{0,1:T(8,128)(2,1)S(1)} %copy-done.50, bf16[128,2048]{0,1:T(8,128)(2,1)S(1)} %copy-done.52, bf16[128,2048]{0,1:T(8,128)(2,1)} %collective-permute-done.18, ...), kind=kOutput, calls=%fused_computation | convolution fusion | flops 5925502976 | bytes 16515072 | tf_op jit(solution)/shard_map/dot_general | solution.py:29
  457.4 7.8 fusion.108
  468.9 12.2 %collective-permute-done.42 = bf16[128,2048]{1,0:T(8,128)(2,1)S(1)} collective-permute-done((bf16[128,2048]{1,0:T(8,128)(2,1)S(1)}, bf16[128,2048]{1,0:T(8,128)(2,1)S(1)}, u32[]{:S(2)}, u32[]{:S(2)}) %collective-permute-start.42) | collective-permute-done | bytes 524320 | tf_op jit(solution)/shard_map/ppermute | solution.py:75
  481.1 5.6 collective-permute-done.41
  515.0 17.3 %reduce-scatter.11.cloned.1.call-done = bf16[64,2048]{1,0:T(8,128)(2,1)} async-done(((bf16[512,2048]{1,0:T(8,128)(2,1)}), bf16[64,2048]{1,0:T(8,128)(2,1)}) %reduce-scatter.11.cloned.1.call-update) | async-done | bytes 262160 | tf_op jit(solution)/shard_map/reduce_scatter | solution.py:372
  533.9 65.1 %reduce-scatter.9.cloned.1.call-done = bf16[176,2048]{1,0:T(8,128)(2,1)} async-done(((bf16[1408,2048]{1,0:T(8,128)(2,1)}), bf16[176,2048]{1,0:T(8,128)(2,1)}) %reduce-scatter.9.cloned.1.call-update) | async-done | bytes 720912 | tf_op jit(solution)/shard_map/reduce_scatter | solution.py:362
  601.1 2.5 collective-permute-start.45
  604.3 5.3 collective-permute-done.45
  610.3 108.8 %reduce-scatter.7.cloned.1.call-done = bf16[256,2816]{1,0:T(8,128)(2,1)} async-done(((bf16[2048,2816]{1,0:T(8,128)(2,1)}), bf16[256,2816]{1,0:T(8,128)(2,1)}) %reduce-scatter.7.cloned.1.call-update) | async-done | bytes 1441808 | tf_op jit(solution)/shard_map/reduce_scatter | solution.py:361
  719.1 2.7 multiply_reduce_fusion
  730.3 7.5 collective-permute-start.47
  739.3 2.8 collective-permute-start.48
  743.5 4.1 collective-permute-start.49
  748.4 2.7 collective-permute-start.50
  757.9 5.5 multiply_subtract_fusion.1
  763.3 2.9 multiply_subtract_fusion.2
  772.1 9.5 %collective-permute-done.57 = bf16[64,2816]{1,0:T(8,128)(2,1)S(1)} collective-permute-done((bf16[64,2816]{1,0:T(8,128)(2,1)S(1)}, bf16[64,2816]{1,0:T(8,128)(2,1)S(1)}, u32[]{:S(2)}, u32[]{:S(2)}) %collective-permute-start.57) | collective-permute-done | bytes 360480 | tf_op jit(solution)/shard_map/ppermute | solution.py:75
  783.5 4.2 mul.746
  787.6 3.7 copy.94
  791.3 5.6 mul.748
  797.0 6.3 multiply_subtract_fusion
  (365 shorter events, 165.8 us)
Async XLA Ops:
  7.2 106.9 %all-gather.5.cloned.1.call-start = ((), (), s32[]{:S(2)}) async-start(), calls=%async_computation.4 | async-start | bytes 7077888 | tf_op jit(solution)/shard_map/all_gather | solution.py:292
  12.6 7.0 collective-permute-start.8
  21.4 10.0 %collective-permute-start.9 = (bf16[64,1536]{1,0:T(8,128)(2,1)S(1)}, bf16[64,1536]{1,0:T(8,128)(2,1)S(1)}, u32[]{:S(2)}, u32[]{:S(2)}) collective-permute-start(bf16[64,1536]{1,0:T(8,128)(2,1)S(1)} %get-tuple-element.91), channel_id=1, source_target_pairs={{0,4},{2,6},{4,0},{6,2},{1,5},{3,7},{5,1},{7,3},{8,12},{10,14},{12... | collective-permute-start | bytes 589832 | tf_op jit(solution)/shard_map/ppermute | solution.py:75
  22.9 9.2 %collective-permute-start.10 = (bf16[64,1536]{1,0:T(8,128)(2,1)S(1)}, bf16[64,1536]{1,0:T(8,128)(2,1)S(1)}, u32[]{:S(2)}, u32[]{:S(2)}) collective-permute-start(bf16[64,1536]{1,0:T(8,128)(2,1)S(1)} %get-tuple-element.90), channel_id=1, source_target_pairs={{0,6},{2,4},{4,2},{6,0},{1,7},{3,5},{5,3},{7,1},{8,14},{10,12},{12... | collective-permute-start | bytes 589832 | tf_op jit(solution)/shard_map/ppermute | solution.py:75
  32.8 116.9 %all-gather.7.cloned.1.call-start = ((), (), s32[]{:S(2)}) async-start(), calls=%async_computation.5 | async-start | bytes 2359296 | tf_op jit(solution)/shard_map/all_gather | solution.py:293
  33.6 202.4 %all-gather.9.cloned.1.call-start = ((), (), s32[]{:S(2)}) async-start(), calls=%async_computation.6 | async-start | bytes 12976128 | tf_op jit(solution)/shard_map/all_gather | solution.py:301
  41.3 8.2 %collective-permute-start.21 = (bf16[64,2816]{1,0:T(8,128)(2,1)S(1)}, bf16[64,2816]{1,0:T(8,128)(2,1)S(1)}, u32[]{:S(2)}, u32[]{:S(2)}) collective-permute-start(bf16[64,2816]{1,0:T(8,128)(2,1)S(1)} %dynamic-slice_bitcast_fusion.5), channel_id=1, source_target_pairs={{0,2},{2,0},{4,6},{6,4},{1,3},{3,1},{5,7},{7,5},{8,10},{10,8},{12,... | collective-permute-start | bytes 1081352 | tf_op jit(solution)/shard_map/ppermute | solution.py:75
  49.6 16.9 %collective-permute-start.22 = (bf16[64,2816]{1,0:T(8,128)(2,1)S(1)}, bf16[64,2816]{1,0:T(8,128)(2,1)S(1)}, u32[]{:S(2)}, u32[]{:S(2)}) collective-permute-start(bf16[64,2816]{1,0:T(8,128)(2,1)S(1)} %get-tuple-element.84), channel_id=1, source_target_pairs={{0,4},{2,6},{4,0},{6,2},{1,5},{3,7},{5,1},{7,3},{8,12},{10,14},{12... | collective-permute-start | bytes 1081352 | tf_op jit(solution)/shard_map/ppermute | solution.py:75
  52.1 14.3 %collective-permute-start.23 = (bf16[64,2816]{1,0:T(8,128)(2,1)S(1)}, bf16[64,2816]{1,0:T(8,128)(2,1)S(1)}, u32[]{:S(2)}, u32[]{:S(2)}) collective-permute-start(bf16[64,2816]{1,0:T(8,128)(2,1)S(1)} %get-tuple-element.83), channel_id=1, source_target_pairs={{0,6},{2,4},{4,2},{6,0},{1,7},{3,5},{5,3},{7,1},{8,14},{10,12},{12... | collective-permute-start | bytes 1081352 | tf_op jit(solution)/shard_map/ppermute | solution.py:75
  67.6 230.0 %all-gather.11.cloned.1.call-start = ((), (), s32[]{:S(2)}) async-start(), calls=%async_computation.7 | async-start | bytes 6488064 | tf_op jit(solution)/shard_map/all_gather | solution.py:302
  67.9 3.8 collective-permute-start
  71.8 6.1 collective-permute-start.1
  79.0 426.3 %reduce-scatter.5.cloned.1.call-start = ((), (), s32[]{:S(2)}) async-start(), calls=%async_computation.8 | async-start | bytes 7077888 | tf_op jit(solution)/shard_map/reduce_scatter | solution.py:411
  79.2 3.8 collective-permute-start.3
  83.1 4.0 collective-permute-start.4
  87.6 15.9 %collective-permute-start.7 = (bf16[128,2048]{0,1:T(8,128)(2,1)S(1)}, bf16[128,2048]{0,1:T(8,128)(2,1)S(1)}, u32[]{:S(2)}, u32[]{:S(2)}) collective-permute-start(bf16[128,2048]{0,1:T(8,128)(2,1)S(1)} %bitcast.242), channel_id=1, source_target_pairs={{0,6},{2,4},{4,2},{6,0},{1,7},{3,5},{5,3},{7,1},{8,14},{10,12},{12... | collective-permute-start | bytes 1572872 | tf_op jit(solution)/shard_map/ppermute | solution.py:75
  90.3 22.3 %collective-permute-start.6 = (bf16[128,2048]{0,1:T(8,128)(2,1)S(1)}, bf16[128,2048]{0,1:T(8,128)(2,1)S(1)}, u32[]{:S(2)}, u32[]{:S(2)}) collective-permute-start(bf16[128,2048]{0,1:T(8,128)(2,1)S(1)} %bitcast.243), channel_id=1, source_target_pairs={{0,4},{2,6},{4,0},{6,2},{1,5},{3,7},{5,1},{7,3},{8,12},{10,14},{12... | collective-permute-start | bytes 1572872 | tf_op jit(solution)/shard_map/ppermute | solution.py:75
  90.7 22.1 %collective-permute-start.5 = (bf16[128,2048]{0,1:T(8,128)(2,1)S(1)}, bf16[128,2048]{0,1:T(8,128)(2,1)S(1)}, u32[]{:S(2)}, u32[]{:S(2)}) collective-permute-start(bf16[128,2048]{0,1:T(8,128)(2,1)S(1)} %bitcast.244), channel_id=1, source_target_pairs={{0,2},{2,0},{4,6},{6,4},{1,3},{3,1},{5,7},{7,5},{8,10},{10,8},{12,... | collective-permute-start | bytes 1572872 | tf_op jit(solution)/shard_map/ppermute | solution.py:75
  125.7 3.8 collective-permute-start.11
  129.5 7.5 collective-permute-start.12
  140.0 3.6 collective-permute-start.13
  143.6 3.6 collective-permute-start.14
  155.9 16.1 %collective-permute-start.17 = (bf16[128,2048]{1,0:T(8,128)(2,1)}, bf16[128,2048]{1,0:T(8,128)(2,1)}, u32[]{:S(2)}, u32[]{:S(2)}) collective-permute-start(bf16[128,2048]{1,0:T(8,128)(2,1)} %get-tuple-element.78), channel_id=1, source_target_pairs={{0,6},{2,4},{4,2},{6,0},{1,7},{3,5},{5,3},{7,1},{8,14},{10,12},{12... | collective-permute-start | bytes 1572872 | tf_op jit(solution)/shard_map/ppermute | solution.py:75
  157.6 20.9 %collective-permute-start.16 = (bf16[128,2048]{1,0:T(8,128)(2,1)}, bf16[128,2048]{1,0:T(8,128)(2,1)}, u32[]{:S(2)}, u32[]{:S(2)}) collective-permute-start(bf16[128,2048]{1,0:T(8,128)(2,1)} %get-tuple-element.79), channel_id=1, source_target_pairs={{0,4},{2,6},{4,0},{6,2},{1,5},{3,7},{5,1},{7,3},{8,12},{10,14},{12... | collective-permute-start | bytes 1572872 | tf_op jit(solution)/shard_map/ppermute | solution.py:75
  158.8 20.2 %collective-permute-start.15 = (bf16[128,2048]{1,0:T(8,128)(2,1)}, bf16[128,2048]{1,0:T(8,128)(2,1)}, u32[]{:S(2)}, u32[]{:S(2)}) collective-permute-start(bf16[128,2048]{1,0:T(8,128)(2,1)} %get-tuple-element.77), channel_id=1, source_target_pairs={{0,2},{2,0},{4,6},{6,4},{1,3},{3,1},{5,7},{7,5},{8,10},{10,8},{12,... | collective-permute-start | bytes 1572872 | tf_op jit(solution)/shard_map/ppermute | solution.py:75
  186.4 15.8 %collective-permute-start.20 = (bf16[128,2048]{0,1:T(8,128)(2,1)S(1)}, bf16[128,2048]{0,1:T(8,128)(2,1)S(1)}, u32[]{:S(2)}, u32[]{:S(2)}) collective-permute-start(bf16[128,2048]{0,1:T(8,128)(2,1)S(1)} %bitcast.247), channel_id=1, source_target_pairs={{0,6},{2,4},{4,2},{6,0},{1,7},{3,5},{5,3},{7,1},{8,14},{10,12},{12... | collective-permute-start | bytes 1572872 | tf_op jit(solution)/shard_map/ppermute | solution.py:75
  187.5 26.0 %collective-permute-start.19 = (bf16[128,2048]{0,1:T(8,128)(2,1)S(1)}, bf16[128,2048]{0,1:T(8,128)(2,1)S(1)}, u32[]{:S(2)}, u32[]{:S(2)}) collective-permute-start(bf16[128,2048]{0,1:T(8,128)(2,1)S(1)} %bitcast.248), channel_id=1, source_target_pairs={{0,4},{2,6},{4,0},{6,2},{1,5},{3,7},{5,1},{7,3},{8,12},{10,14},{12... | collective-permute-start | bytes 1572872 | tf_op jit(solution)/shard_map/ppermute | solution.py:75
  189.0 25.3 %collective-permute-start.18 = (bf16[128,2048]{0,1:T(8,128)(2,1)S(1)}, bf16[128,2048]{0,1:T(8,128)(2,1)}, u32[]{:S(2)}, u32[]{:S(2)}) collective-permute-start(bf16[128,2048]{0,1:T(8,128)(2,1)S(1)} %bitcast.249), channel_id=1, source_target_pairs={{0,2},{2,0},{4,6},{6,4},{1,3},{3,1},{5,7},{7,5},{8,10},{10,8},{12,... | collective-permute-start | bytes 1572872 | tf_op jit(solution)/shard_map/ppermute | solution.py:75
  192.1 55.8 %collective-permute-start.29 = (bf16[128,2048]{1,0:T(8,128)(2,1)}, bf16[128,2048]{1,0:T(8,128)(2,1)}, u32[]{:S(2)}, u32[]{:S(2)}) collective-permute-start(bf16[128,2048]{1,0:T(8,128)(2,1)} %fusion.24), channel_id=1, source_target_pairs={{0,6},{2,4},{4,2},{6,0},{1,7},{3,5},{5,3},{7,1},{8,14},{10,12},{12... | collective-permute-start | bytes 1572872 | tf_op jit(solution)/shard_map/ppermute | solution.py:75
  193.1 54.8 %collective-permute-start.28 = (bf16[128,2048]{1,0:T(8,128)(2,1)}, bf16[128,2048]{1,0:T(8,128)(2,1)}, u32[]{:S(2)}, u32[]{:S(2)}) collective-permute-start(bf16[128,2048]{1,0:T(8,128)(2,1)} %fusion.24), channel_id=1, source_target_pairs={{0,4},{2,6},{4,0},{6,2},{1,5},{3,7},{5,1},{7,3},{8,12},{10,14},{12... | collective-permute-start | bytes 1572872 | tf_op jit(solution)/shard_map/ppermute | solution.py:75
  202.2 45.7 %collective-permute-start.27 = (bf16[128,2048]{1,0:T(8,128)(2,1)}, bf16[128,2048]{1,0:T(8,128)(2,1)}, u32[]{:S(2)}, u32[]{:S(2)}) collective-permute-start(bf16[128,2048]{1,0:T(8,128)(2,1)} %fusion.24), channel_id=1, source_target_pairs={{0,2},{2,0},{4,6},{6,4},{1,3},{3,1},{5,7},{7,5},{8,10},{10,8},{12,... | collective-permute-start | bytes 1572872 | tf_op jit(solution)/shard_map/ppermute | solution.py:75
  318.9 15.8 %collective-permute-start.32 = (bf16[128,2048]{1,0:T(8,128)(2,1)S(1)}, bf16[128,2048]{1,0:T(8,128)(2,1)S(1)}, u32[]{:S(2)}, u32[]{:S(2)}) collective-permute-start(bf16[128,2048]{1,0:T(8,128)(2,1)S(1)} %get-tuple-element.72), channel_id=1, source_target_pairs={{0,6},{2,4},{4,2},{6,0},{1,7},{3,5},{5,3},{7,1},{8,14},{10,12},{12... | collective-permute-start | bytes 1572872 | tf_op jit(solution)/shard_map/ppermute | solution.py:75
  321.4 24.6 %collective-permute-start.31 = (bf16[128,2048]{1,0:T(8,128)(2,1)S(1)}, bf16[128,2048]{1,0:T(8,128)(2,1)S(1)}, u32[]{:S(2)}, u32[]{:S(2)}) collective-permute-start(bf16[128,2048]{1,0:T(8,128)(2,1)S(1)} %get-tuple-element.73), channel_id=1, source_target_pairs={{0,4},{2,6},{4,0},{6,2},{1,5},{3,7},{5,1},{7,3},{8,12},{10,14},{12... | collective-permute-start | bytes 1572872 | tf_op jit(solution)/shard_map/ppermute | solution.py:75
  322.0 24.0 %collective-permute-start.30 = (bf16[128,2048]{1,0:T(8,128)(2,1)S(1)}, bf16[128,2048]{1,0:T(8,128)(2,1)S(1)}, u32[]{:S(2)}, u32[]{:S(2)}) collective-permute-start(bf16[128,2048]{1,0:T(8,128)(2,1)S(1)} %get-tuple-element.71), channel_id=1, source_target_pairs={{0,2},{2,0},{4,6},{6,4},{1,3},{3,1},{5,7},{7,5},{8,10},{10,8},{12,... | collective-permute-start | bytes 1572872 | tf_op jit(solution)/shard_map/ppermute | solution.py:75
  329.0 28.3 %collective-permute-start.26 = (bf16[128,2048]{1,0:T(8,128)(2,1)}, bf16[128,2048]{1,0:T(8,128)(2,1)}, u32[]{:S(2)}, u32[]{:S(2)}) collective-permute-start(bf16[128,2048]{1,0:T(8,128)(2,1)} %get-tuple-element.75), channel_id=1, source_target_pairs={{0,6},{2,4},{4,2},{6,0},{1,7},{3,5},{5,3},{7,1},{8,14},{10,12},{12... | collective-permute-start | bytes 1572872 | tf_op jit(solution)/shard_map/ppermute | solution.py:75
  331.4 36.4 %collective-permute-start.25 = (bf16[128,2048]{1,0:T(8,128)(2,1)}, bf16[128,2048]{1,0:T(8,128)(2,1)}, u32[]{:S(2)}, u32[]{:S(2)}) collective-permute-start(bf16[128,2048]{1,0:T(8,128)(2,1)} %get-tuple-element.76), channel_id=1, source_target_pairs={{0,4},{2,6},{4,0},{6,2},{1,5},{3,7},{5,1},{7,3},{8,12},{10,14},{12... | collective-permute-start | bytes 1572872 | tf_op jit(solution)/shard_map/ppermute | solution.py:75
  334.7 33.2 %collective-permute-start.24 = (bf16[128,2048]{1,0:T(8,128)(2,1)}, bf16[128,2048]{1,0:T(8,128)(2,1)}, u32[]{:S(2)}, u32[]{:S(2)}) collective-permute-start(bf16[128,2048]{1,0:T(8,128)(2,1)} %get-tuple-element.74), channel_id=1, source_target_pairs={{0,2},{2,0},{4,6},{6,4},{1,3},{3,1},{5,7},{7,5},{8,10},{10,8},{12,... | collective-permute-start | bytes 1572872 | tf_op jit(solution)/shard_map/ppermute | solution.py:75
  371.5 16.1 %collective-permute-start.35 = (bf16[128,2048]{1,0:T(8,128)(2,1)}, bf16[128,2048]{1,0:T(8,128)(2,1)}, u32[]{:S(2)}, u32[]{:S(2)}) collective-permute-start(bf16[128,2048]{1,0:T(8,128)(2,1)} %get-tuple-element.55), channel_id=1, source_target_pairs={{0,6},{2,4},{4,2},{6,0},{1,7},{3,5},{5,3},{7,1},{8,14},{10,12},{12... | collective-permute-start | bytes 1572872 | tf_op jit(solution)/shard_map/ppermute | solution.py:75
  373.2 24.5 %collective-permute-start.34 = (bf16[128,2048]{1,0:T(8,128)(2,1)}, bf16[128,2048]{1,0:T(8,128)(2,1)}, u32[]{:S(2)}, u32[]{:S(2)}) collective-permute-start(bf16[128,2048]{1,0:T(8,128)(2,1)} %get-tuple-element.55), channel_id=1, source_target_pairs={{0,4},{2,6},{4,0},{6,2},{1,5},{3,7},{5,1},{7,3},{8,12},{10,14},{12... | collective-permute-start | bytes 1572872 | tf_op jit(solution)/shard_map/ppermute | solution.py:75
  374.5 23.3 %collective-permute-start.33 = (bf16[128,2048]{1,0:T(8,128)(2,1)}, bf16[128,2048]{1,0:T(8,128)(2,1)}, u32[]{:S(2)}, u32[]{:S(2)}) collective-permute-start(bf16[128,2048]{1,0:T(8,128)(2,1)} %get-tuple-element.55), channel_id=1, source_target_pairs={{0,2},{2,0},{4,6},{6,4},{1,3},{3,1},{5,7},{7,5},{8,10},{10,8},{12,... | collective-permute-start | bytes 1572872 | tf_op jit(solution)/shard_map/ppermute | solution.py:75
  402.0 3.7 collective-permute-start.36
  405.6 3.6 collective-permute-start.37
  413.3 4.3 collective-permute-start.38
  417.6 4.6 collective-permute-start.39
  429.7 102.5 %reduce-scatter.11.cloned.1.call-start = ((), (), s32[]{:S(2)}) async-start(), calls=%async_computation.11 | async-start | bytes 2359296 | tf_op jit(solution)/shard_map/reduce_scatter | solution.py:372
  434.9 164.2 %reduce-scatter.9.cloned.1.call-start = ((), (), s32[]{:S(2)}) async-start(), calls=%async_computation.10 | async-start | bytes 6488064 | tf_op jit(solution)/shard_map/reduce_scatter | solution.py:362
  443.7 275.3 %reduce-scatter.7.cloned.1.call-start = ((), (), s32[]{:S(2)}) async-start(), calls=%async_computation.9 | async-start | bytes 12976128 | tf_op jit(solution)/shard_map/reduce_scatter | solution.py:361
  465.3 15.8 %collective-permute-start.42 = (bf16[128,2048]{1,0:T(8,128)(2,1)S(1)}, bf16[128,2048]{1,0:T(8,128)(2,1)S(1)}, u32[]{:S(2)}, u32[]{:S(2)}) collective-permute-start(bf16[128,2048]{1,0:T(8,128)(2,1)S(1)} %get-tuple-element.69), channel_id=1, source_target_pairs={{0,6},{2,4},{4,2},{6,0},{1,7},{3,5},{5,3},{7,1},{8,14},{10,12},{12... | collective-permute-start | bytes 1572872 | tf_op jit(solution)/shard_map/ppermute | solution.py:75
  466.9 19.8 %collective-permute-start.41 = (bf16[128,2048]{1,0:T(8,128)(2,1)S(1)}, bf16[128,2048]{1,0:T(8,128)(2,1)S(1)}, u32[]{:S(2)}, u32[]{:S(2)}) collective-permute-start(bf16[128,2048]{1,0:T(8,128)(2,1)S(1)} %get-tuple-element.70), channel_id=1, source_target_pairs={{0,4},{2,6},{4,0},{6,2},{1,5},{3,7},{5,1},{7,3},{8,12},{10,14},{12... | collective-permute-start | bytes 1572872 | tf_op jit(solution)/shard_map/ppermute | solution.py:75
  468.3 18.5 %collective-permute-start.40 = (bf16[128,2048]{1,0:T(8,128)(2,1)S(1)}, bf16[128,2048]{1,0:T(8,128)(2,1)S(1)}, u32[]{:S(2)}, u32[]{:S(2)}) collective-permute-start(bf16[128,2048]{1,0:T(8,128)(2,1)S(1)} %get-tuple-element.68), channel_id=1, source_target_pairs={{0,2},{2,0},{4,6},{6,4},{1,3},{3,1},{5,7},{7,5},{8,10},{10,8},{12,... | collective-permute-start | bytes 1572872 | tf_op jit(solution)/shard_map/ppermute | solution.py:75
  491.8 4.0 collective-permute-start.52
  495.8 4.1 collective-permute-start.53
  499.9 4.0 collective-permute-start.54
  503.9 5.0 collective-permute-start.55
  506.2 5.7 collective-permute-start.43
  513.7 89.9 %collective-permute-start.44 = (bf16[64,1536]{1,0:T(8,128)(2,1)S(1)}, bf16[64,1536]{1,0:T(8,128)(2,1)S(1)}, u32[]{:S(2)}, u32[]{:S(2)}) collective-permute-start(bf16[64,1536]{1,0:T(8,128)(2,1)S(1)} %get-tuple-element.88), channel_id=1, source_target_pairs={{0,4},{2,6},{4,0},{6,2},{1,5},{3,7},{5,1},{7,3},{8,12},{10,14},{12... | collective-permute-start | bytes 589832 | tf_op jit(solution)/shard_map/ppermute | solution.py:75
  601.1 8.5 %collective-permute-start.45 = (bf16[64,1536]{1,0:T(8,128)(2,1)S(1)}, bf16[64,1536]{1,0:T(8,128)(2,1)S(1)}, u32[]{:S(2)}, u32[]{:S(2)}) collective-permute-start(bf16[64,1536]{1,0:T(8,128)(2,1)S(1)} %get-tuple-element.87), channel_id=1, source_target_pairs={{0,6},{2,4},{4,2},{6,0},{1,7},{3,5},{5,3},{7,1},{8,14},{10,12},{12... | collective-permute-start | bytes 589832 | tf_op jit(solution)/shard_map/ppermute | solution.py:75
  724.4 5.3 collective-permute-start.46
  728.2 38.0 %collective-permute-start.56 = (bf16[64,2816]{1,0:T(8,128)(2,1)}, bf16[64,2816]{1,0:T(8,128)(2,1)S(1)}, u32[]{:S(2)}, u32[]{:S(2)}) collective-permute-start(bf16[64,2816]{1,0:T(8,128)(2,1)} %dynamic-slice_bitcast_fusion.2), channel_id=1, source_target_pairs={{0,2},{2,0},{4,6},{6,4},{1,3},{3,1},{5,7},{7,5},{8,10},{10,8},{12,... | collective-permute-start | bytes 1081352 | tf_op jit(solution)/shard_map/ppermute | solution.py:75
  730.3 8.5 %collective-permute-start.47 = (f32[]{:T(128)}, f32[]{:T(128)}, u32[]{:S(2)}, u32[]{:S(2)}) collective-permute-start(f32[]{:T(128)} %add.575), channel_id=1, source_target_pairs={{0,2},{2,0},{1,3},{3,1},{4,6},{6,4},{5,7},{7,5},{8,10},{10,8},{9,1... | collective-permute-start | bytes 20 | tf_op jit(solution)/shard_map/ppermute | solution.py:75
  743.5 4.3 collective-permute-start.49
  748.4 4.5 collective-permute-start.50
  766.4 15.2 %collective-permute-start.57 = (bf16[64,2816]{1,0:T(8,128)(2,1)S(1)}, bf16[64,2816]{1,0:T(8,128)(2,1)S(1)}, u32[]{:S(2)}, u32[]{:S(2)}) collective-permute-start(bf16[64,2816]{1,0:T(8,128)(2,1)S(1)} %get-tuple-element.81), channel_id=1, source_target_pairs={{0,4},{2,6},{4,0},{6,2},{1,5},{3,7},{5,1},{7,3},{8,12},{10,14},{12... | collective-permute-start | bytes 1081352 | tf_op jit(solution)/shard_map/ppermute | solution.py:75
  770.0 11.6 %collective-permute-start.58 = (bf16[64,2816]{1,0:T(8,128)(2,1)S(1)}, bf16[64,2816]{1,0:T(8,128)(2,1)S(1)}, u32[]{:S(2)}, u32[]{:S(2)}) collective-permute-start(bf16[64,2816]{1,0:T(8,128)(2,1)S(1)} %get-tuple-element.80), channel_id=1, source_target_pairs={{0,6},{2,4},{4,2},{6,0},{1,7},{3,5},{5,3},{7,1},{8,14},{10,12},{12... | collective-permute-start | bytes 1081352 | tf_op jit(solution)/shard_map/ppermute | solution.py:75
  (64 other events, 597.0 us)
Sparse Core Ops, SparseCore 0:
  32.9 63.9 all-gather.4
  99.0 29.9 all-gather.6
  131.3 104.6 all-gather.8
  238.0 59.6 all-gather.10
  429.8 66.1 reduce-scatter.4
  498.7 33.4 reduce-scatter.10
  534.5 64.4 reduce-scatter.8
  601.3 117.6 reduce-scatter.6

commit v2 on v1

--- a/solution.py
+++ b/solution.py
@@ -22,7 +22,8 @@
 LINE = "z"
 PLANE = ("y", "x")
 CORE = "core"
-OWNERS = ("z", "core")
+MIXER_OWNERS = ("z", "core")
+GLU_OWNERS = ("y", "x", "core")
 
 
 def contract(left_side, right_side, left_dim, right_dim):
@@ -87,50 +88,144 @@
     return held
 
 
-def total_small(values, axes):
-    for axis in axes:
-        bit = 1
-        while bit < lax.axis_size(axis):
-            values = values + swap(values, axis, bit)
-            bit *= 2
+def total_small(values, groups):
+    for axes in groups:
+        terms = [values] + [swap(values, axes, k) for k in range(1, lax.axis_size(axes))]
+        while len(terms) > 1:
+            terms = [terms[i] + terms[i + 1] for i in range(0, len(terms), 2)]
+        values = terms[0]
     return values
 
 
-def gather_plane(values):
-    return jnp.concatenate(
-        [values] + [swap(values, PLANE, k) for k in range(1, lax.axis_size(PLANE))], axis=0
-    )
-
-
-def total_plane(values):
-    size = lax.axis_size(PLANE)
+def gather_near(values, axes):
+    size = lax.axis_size(axes)
+    direct = [k for k in range(1, size) if axes != LINE or k & (k - 1) == 0]
+    return {0: values} | {k: swap(values, axes, k) for k in direct}
+
+
+def gather_far(blocks, axes):
+    blocks = dict(blocks)
+    for k in range(1, lax.axis_size(axes)):
+        if k not in blocks:
+            blocks[k] = swap(blocks[k ^ (k & -k)], axes, k & -k)
+    return [blocks[k] for k in range(lax.axis_size(axes))]
+
+
+def gather_tokens(values, axes):
+    return jnp.concatenate(gather_far(gather_near(values, axes), axes), axis=0)
+
+
+def scatter_far(partial, axes):
+    size = lax.axis_size(axes)
+    rows = partial.shape[0] // size
+    blocks = {k: partial[k * rows : (k + 1) * rows] for k in range(size)}
+    for k in range(size - 1, 0, -1):
+        if axes == LINE and k & (k - 1):
+            near = k & -k
+            moved = swap(blocks.pop(k).astype(jnp.bfloat16), axes, near)
+            blocks[k ^ near] = blocks[k ^ near] + moved.astype(jnp.float32)
+    return blocks
+
+
+def scatter_near(blocks, axes):
+    total = blocks[0]
+    for k in sorted(blocks, reverse=True)[:-1]:
+        total = total + swap(blocks[k].astype(jnp.bfloat16), axes, k).astype(jnp.float32)
+    return total
+
+
+def scatter_tokens(partial, axes):
+    return scatter_near(scatter_far(partial, axes), axes)
+
+
+def total_tokens(values, axes):
+    size = lax.axis_size(axes)
     blocks = values.reshape(size, values.shape[0] // size)
     bit = 1
     while bit < size:
-        other = swap(blocks, PLANE, bit)
+        other = swap(blocks, axes, bit)
         blocks = blocks + jnp.stack([other[k ^ bit] for k in range(size)])
         bit *= 2
     return blocks.reshape(values.shape)
 
 
-def scatter_plane(partial):
-    size = lax.axis_size(PLANE)
-    rows = partial.shape[0] // size
-    total = partial[:rows]
-    for k in range(1, size):
-        total = total + swap(
-            partial[k * rows : (k + 1) * rows].astype(jnp.bfloat16), PLANE, k
-        ).astype(jnp.float32)
+def core_sums(part, axes):
+    size, cores = lax.axis_size(axes), lax.axis_size(CORE)
+    core = lax.axis_index(CORE)
+    blocks = part.reshape(size, cores, part.shape[0] // (size * cores), part.shape[1])
+    total = lax.dynamic_index_in_dim(blocks, core, 1, keepdims=False).astype(jnp.float32)
+    for k in range(1, cores):
+        sent = lax.dynamic_index_in_dim(blocks, core ^ k, 1, keepdims=False)
+        total = total + swap(sent, CORE, k).astype(jnp.float32)
+    return total.astype(jnp.bfloat16)
+
+
+def rank_sums(blocks, axes):
+    rank = lax.axis_index(axes)
+    total = lax.dynamic_index_in_dim(blocks, rank, 0, keepdims=False).astype(jnp.float32)
+    for k in range(1, lax.axis_size(axes)):
+        sent = lax.dynamic_index_in_dim(blocks, rank ^ k, 0, keepdims=False)
+        total = total + swap(sent, axes, k).astype(jnp.float32)
     return total
 
 
-def exchange_plane(blocks):
-    rank = lax.axis_index(PLANE)
-    result = blocks
-    for k in range(1, blocks.shape[0]):
-        sent = lax.dynamic_index_in_dim(blocks, rank ^ k, 0, keepdims=False)
-        result = lax.dynamic_update_index_in_dim(result, swap(sent, PLANE, k), rank ^ k, 0)
-    return result
+def in_order(blocks, axes):
+    rank = lax.axis_index(axes)
+    blocks = jnp.stack(blocks)
+    return jnp.concatenate(
+        [lax.dynamic_index_in_dim(blocks, rank ^ k, 0) for k in range(blocks.shape[0])], axis=0
+    )
+
+
+def core_pair(values):
+    return in_order([values] + [swap(values, CORE, k) for k in range(1, lax.axis_size(CORE))], CORE)
+
+
+def send_each(blocks, axes):
+    return [blocks[0]] + [swap(blocks[k], axes, k) for k in range(1, len(blocks))]
+
+
+def rank_blocks(blocks, axes):
+    rank = lax.axis_index(axes)
+    return [
+        lax.dynamic_index_in_dim(blocks, rank ^ k, 0, keepdims=False)
+        for k in range(blocks.shape[0])
+    ]
+
+
+def together(*values):
+    return lax.optimization_barrier(values)
+
+
+def split_kernel(groups, order_ref, values_ref, out_ref):
+    count, _, held = out_ref.shape
+    unit = held // groups
+    for k in range(count):
+        for g in range(groups):
+            start = pl.multiple_of((g * count + order_ref[k]) * unit, unit)
+            out_ref[k, :, g * unit : (g + 1) * unit] = values_ref[:, pl.ds(start, unit)].astype(
+                out_ref.dtype
+            )
+
+
+def split_columns(values, groups, order):
+    count = order.shape[0]
+    rows, width = values.shape
+    unit = width // (groups * count)
+    if unit % 128:
+        blocks = values.astype(jnp.bfloat16).reshape(rows, groups, count, unit)
+        blocks = blocks.transpose(2, 0, 1, 3).reshape(count, rows, groups * unit)
+        return jnp.stack(
+            [lax.dynamic_index_in_dim(blocks, order[k], 0, keepdims=False) for k in range(count)]
+        )
+    vmem = pl.BlockSpec(memory_space=pltpu.VMEM)
+    return pl.pallas_call(
+        functools.partial(split_kernel, groups),
+        out_shape=jax.ShapeDtypeStruct((count, rows, groups * unit), jnp.bfloat16),
+        in_specs=[pl.BlockSpec(memory_space=pltpu.SMEM), vmem],
+        out_specs=vmem,
+        compiler_params=pltpu.CompilerParams(vmem_limit_bytes=32 * 1024 * 1024),
+    )(order, values)
 
 
 TILE = 8
@@ -263,8 +358,7 @@
     rows = in_w.shape[0]
     chan = lower_bound.shape[0]
     channels = chan * line
-    hidden_rows = down_w.shape[0] * cores
-    hidden_width = hidden_rows * line
+    hidden_width = down_w.shape[0] * plane * cores
 
     seq_scale = sequence_weights(domain_ids, domain_weight)
     position = device * tok + jnp.arange(tok, dtype=jnp.int32)
@@ -282,24 +376,11 @@
             .reshape(count, width)
         )
 
-    in_blocks = (
-        in_w.astype(bf16)
-        .reshape(rows, 3, line, plane, chan)
-        .transpose(3, 0, 1, 2, 4)
-        .reshape(plane, rows, 3 * channels)
-    )
-    in_held = exchange_plane(in_blocks).reshape(plane * rows, 3 * channels)
-    in_b = lax.all_gather(in_held, OWNERS, axis=0, tiled=True)
-    out_b = lax.all_gather(out_w.astype(bf16), OWNERS, axis=0, tiled=True)
-    glu_blocks = (
-        glu_w.astype(bf16)
-        .reshape(rows, 2, line, plane, hidden_rows)
-        .transpose(3, 0, 1, 2, 4)
-        .reshape(plane, rows, 2 * hidden_width)
-    )
-    glu_held = exchange_plane(glu_blocks).reshape(plane * rows, 2 * hidden_width)
-    glu_b = lax.all_gather(glu_held, OWNERS, axis=0, tiled=True)
-    down_b = lax.all_gather(down_w.astype(bf16), OWNERS, axis=0, tiled=True)
+    line_order = jnp.arange(line, dtype=jnp.int32) ^ level
+    glu_came = send_each(split_columns(glu_w, 2, line_order), LINE)
+    glu_held = in_order(glu_came, LINE).reshape(line * rows, 2 * hidden_width)
+    in_came = send_each(split_columns(in_w, 3 * line, order), PLANE)
+    in_held = in_order(in_came, PLANE).reshape(plane * rows, 3 * channels)
 
     gain_size = 3 * gains.shape[1]
     packed = jnp.concatenate([rounded(gains).reshape(-1), lower_bound])
@@ -318,62 +399,99 @@
         .reshape(3, width)
     )
 
-    grad_output = cotangent[0].astype(f32) * row_weight[:, None]
-    grad_output_b = gather_plane(grad_output.astype(bf16))
+    in_held, glu_held = together(in_held, glu_held)
+    in_b = lax.all_gather(in_held, MIXER_OWNERS, axis=0, tiled=True)
 
     scale_one = lax.rsqrt(jnp.mean(inputs_f * inputs_f, axis=1, keepdims=True) + NORM_EPS)
     unit_one = inputs_f * scale_one
-    normed = gather_plane(feature_swap((unit_one * gain_f[0]).astype(bf16), plane, cores))
+    normed = feature_swap((unit_one * gain_f[0]).astype(bf16), plane, cores)
+    normed = gather_tokens(normed, PLANE)
     proj = contract(normed, in_b, 1, 0)
+
+    glu_held, proj = together(glu_held, proj)
+    glu_rows = lax.all_gather(glu_held, GLU_OWNERS, axis=0, tiled=False)
+    out_pair = core_pair(out_w.astype(bf16))
+    out_blocks = gather_near(out_pair, LINE)
+    proj, out_blocks = together(proj, out_blocks)
+    out_blocks = gather_far(out_blocks, LINE)
     local_state, local_prod, last = call_scan(scan_kernel, order, proj, bound)
     lasts = gather_small(last, LINE)
+    lasts, out_blocks = together(lasts, out_blocks)
     state_in = jnp.zeros((channels,), f32)
     for k in range(line):
         state_in = jnp.where(k < level, lasts[k, 1] * state_in + lasts[k, 0], state_in)
     state = local_state + local_prod * state_in[None, :]
     state_f = rounded(state)
-    square_mid = total_plane(jnp.sum(state_f * state_f, axis=1))
+    square_mid = total_tokens(jnp.sum(state_f * state_f, axis=1), PLANE)
+    out_b = in_order(out_blocks, LINE).reshape(channels, width)
     scale_mid = lax.rsqrt(square_mid / width + NORM_EPS)[:, None]
     unit_mid = state_f * scale_mid
     gate_raw = proj[:, 2 * channels :]
     gate_act = jax.nn.silu(gate_raw)
     gated = (unit_mid * gain_mid * gate_act).astype(bf16)
-    resid = inputs_f + scatter_plane(contract(gated, out_b, 1, 0))
+    grad_output = cotangent[0].astype(f32) * row_weight[:, None]
+    gated, grad_output_b = together(gated, grad_output.astype(bf16))
+    grad_output_b = gather_near(grad_output_b, LINE)
+    mixed = scatter_tokens(contract(gated, out_b, 1, 0), PLANE)
+    mixed, grad_output_b = together(mixed, grad_output_b)
+    resid = inputs_f + mixed
 
     scale_two = lax.rsqrt(jnp.mean(resid * resid, axis=1, keepdims=True) + NORM_EPS)
     unit_two = resid * scale_two
-    second = gather_plane(feature_swap((unit_two * gain_f[2]).astype(bf16), plane, cores))
+    second_own = (unit_two * gain_f[2]).astype(bf16)
+    second_own, down_own, glu_rows = together(second_own, down_w.astype(bf16), glu_rows)
+    down_b = lax.all_gather(down_own, GLU_OWNERS, axis=0, tiled=True)
+    glu_b = (
+        glu_rows.reshape(plane * cores, line, rows, 2 * hidden_width)
+        .transpose(1, 0, 2, 3)
+        .reshape(width, 2 * hidden_width)
+    )
+    second, glu_b = together(gather_near(second_own, LINE), glu_b)
+    second = jnp.concatenate(gather_far(second, LINE), axis=0)
+    second, grad_output_b = together(second, grad_output_b)
     paired = contract(second, glu_b, 1, 0)
     up_gate = paired[:, :hidden_width]
     up_value = paired[:, hidden_width:]
     gate_silu = jax.nn.silu(up_gate)
     hidden = (gate_silu * up_value).astype(bf16)
-    output = resid + scatter_plane(contract(hidden, down_b, 1, 0))
-    block_out = output.astype(bf16)[None]
-
+
+    grad_output_b = jnp.concatenate(gather_far(grad_output_b, LINE), axis=0)
     grad_hidden = contract(grad_output_b, down_b, 1, 1)
     grad_paired = jnp.concatenate(
         [grad_hidden * up_value * silu_slope(up_gate), grad_hidden * gate_silu], axis=1
     ).astype(bf16)
-    grad_second = feature_swap(scatter_plane(contract(grad_paired, glu_b, 1, 1)), cores, plane)
-    glu_part = contract(second, grad_paired, 0, 0).astype(bf16)
+    second_part = contract(grad_paired, glu_b, 1, 1)
+    grad_second = scatter_tokens(second_part, LINE)
+    owned = (
+        second
+        .reshape(line * tok, line, plane * cores, rows)
+        .transpose(0, 2, 1, 3)
+        .reshape(line * tok, width)
+    )
+    glu_part = contract(owned, grad_paired, 0, 0).astype(bf16)
+    glu_held = lax.psum_scatter(glu_part, GLU_OWNERS, scatter_dimension=0, tiled=True)
     down_part = contract(hidden, grad_output_b, 0, 0).astype(bf16)
-    glu_held = lax.psum_scatter(glu_part, OWNERS, scatter_dimension=0, tiled=True)
-    down_grad = lax.psum_scatter(down_part, OWNERS, scatter_dimension=0, tiled=True)
+    down_sums = core_sums(down_part, PLANE)
     grad_gain_two = jnp.sum(grad_second * unit_two, axis=0)
     weighted_two = grad_second * gain_f[2]
     grad_resid = grad_output + scale_two * (
         weighted_two - unit_two * jnp.mean(weighted_two * unit_two, axis=1, keepdims=True)
     )
 
-    grad_resid_b = gather_plane(grad_resid.astype(bf16))
+    grad_resid, hidden = together(grad_resid, hidden)
+    output = resid + scatter_tokens(contract(hidden, down_b, 1, 0), LINE)
+    block_out = output.astype(bf16)[None]
+
+    grad_resid_b = gather_tokens(grad_resid.astype(bf16), PLANE)
+    grad_resid_b, block_out = together(grad_resid_b, block_out)
     grad_gated = contract(grad_resid_b, out_b, 1, 1)
     out_part = contract(gated, grad_resid_b, 0, 0).astype(bf16)
-    out_grad = lax.psum_scatter(out_part, OWNERS, scatter_dimension=0, tiled=True)
     grad_gain_mid = jnp.sum(grad_gated * unit_mid * gate_act, axis=0)
     grad_gate = grad_gated * unit_mid * gain_mid * silu_slope(gate_raw)
     weighted_mid = grad_gated * gain_mid * gate_act
-    mean_mid = total_plane(jnp.sum(weighted_mid * unit_mid, axis=1)) / width
+    mean_mid = total_tokens(jnp.sum(weighted_mid * unit_mid, axis=1), PLANE) / width
+    out_part, glu_held = together(out_part, glu_held)
+    out_grad = lax.psum_scatter(out_part, MIXER_OWNERS, scatter_dimension=0, tiled=True)
     grad_state = scale_mid * (weighted_mid - unit_mid * mean_mid[:, None])
     local_carried, local_rate, first = call_scan(
         back_kernel, order, proj, bound, rounded(grad_state)
@@ -408,39 +526,49 @@
     )
     grad_proj = jnp.concatenate([grad_in_raw, grad_forget_raw, grad_gate], axis=1).astype(bf16)
     in_part = contract(normed, grad_proj, 0, 0).astype(bf16)
-    in_held = lax.psum_scatter(in_part, OWNERS, scatter_dimension=0, tiled=True)
-    grad_normed = feature_swap(scatter_plane(contract(grad_proj, in_b, 1, 1)), cores, plane)
+    in_held = lax.psum_scatter(in_part, MIXER_OWNERS, scatter_dimension=0, tiled=True)
+    down_grad = rank_sums(down_sums, PLANE)
+    grad_normed = feature_swap(
+        scatter_tokens(contract(grad_proj, in_b, 1, 1), PLANE), cores, plane
+    )
     grad_gain_one = jnp.sum(grad_normed * unit_one, axis=0)
     weighted_one = grad_normed * gain_f[0]
     grad_block = grad_resid + scale_one * (
         weighted_one - unit_one * jnp.mean(weighted_one * unit_one, axis=1, keepdims=True)
     )
 
-    glu_grad = (
-        exchange_plane(glu_held.reshape(plane, rows, 2 * hidden_width))
-        .reshape(plane, rows, 2, line, hidden_rows)
-        .transpose(1, 2, 3, 0, 4)
-        .reshape(glu_w.shape)
-        .astype(f32)
-    )
+    mid_row = lax.dynamic_update_index_in_dim(
+        jnp.zeros((line, plane, chan), f32), grad_gain_mid.reshape(line, chan), rank, 1
+    ).reshape(width)
+    gain_part = jnp.stack([grad_gain_one, mid_row, grad_gain_two])
+    early_squares = squared(glu_held) + squared(down_grad) + squared(out_grad)
+    glu_sent = rank_blocks(glu_held.reshape(line, rows, 2 * hidden_width), LINE)
+    in_held, glu_sent, gain_part, early_squares, grad_block = together(
+        in_held, glu_sent, gain_part, early_squares, grad_block
+    )
+    glu_came = send_each(glu_sent, LINE)
+    squares = jnp.broadcast_to(early_squares + squared(in_held), (1, width))
+    totals = total_small(
+        jnp.concatenate([gain_part, squares], axis=0), (CORE, PLANE, LINE)
+    )
+    glu_blocks = in_order(glu_came, LINE)
+    glu_grad = jnp.concatenate(
+        [glu_blocks[q, :, :hidden_width] for q in range(line)]
+        + [glu_blocks[q, :, hidden_width:] for q in range(line)],
+        axis=1,
+    )
+    in_blocks = in_held.reshape(plane, rows, 3 * channels)
+    in_came = send_each(rank_blocks(in_blocks, PLANE), PLANE)
     in_grad = (
-        exchange_plane(in_held.reshape(plane, rows, 3 * channels))
+        in_order(in_came, PLANE)
         .reshape(plane, rows, 3, line, chan)
         .transpose(1, 2, 3, 0, 4)
         .reshape(in_w.shape)
-        .astype(f32)
-    )
-    out_grad = out_grad.astype(f32)
-    down_grad = down_grad.astype(f32)
-
-    mid_row = lax.dynamic_update_index_in_dim(
-        jnp.zeros((line, plane, chan), f32), grad_gain_mid.reshape(line, chan), rank, 1
-    ).reshape(width)
-    everyone = (CORE, "x", "y", LINE)
-    gain_total = total_small(jnp.stack([grad_gain_one, mid_row, grad_gain_two]), everyone)
-    squares = total_small(
-        squared(glu_held) + squared(down_grad) + squared(out_grad) + squared(in_held), everyone
-    ) + squared(gain_total)
+    )
+    gain_total = totals[:3]
+    squares = totals[3, 0] + squared(gain_total)
+    in_grad, glu_grad, squares = lax.optimization_barrier((in_grad, glu_grad, squares))
+    in_grad, glu_grad, out_grad = (v.astype(f32) for v in (in_grad, glu_grad, out_grad))
     columns = gains.shape[1]
     gain_grad = lax.dynamic_slice_in_dim(
         gain_total, (device * cores + lax.axis_index(CORE)) * columns, columns, 1

time: 821 us -> 618 us (0.75)
  the two profiles are of different devices: /device:TPU:8 before, /device:TPU:0 now
where the time goes in v2:
time: 618 us; the launch traced here: 610 us
  waiting for transfers between devices  306 us (50%)
  starting transfers between devices  79.3 us (13%)
  matrix products  74.7 us (12%)
  other arithmetic  61.3 us (10%)
  local copies, waits for them, and re-layouts  51.7 us (8%)
  between operations  28.8 us (5%)
  Pallas kernels  7.99 us (1%)
    ppermute x64, waiting for transfers between devices, swap(): return lax.ppermute(values, axis, [(i, i ^ bit) for i in range(size)])  271 us
    ppermute x64, starting transfers between devices, swap(): return lax.ppermute(values, axis, [(i, i ^ bit) for i in range(size)])  78.2 us
    dot_general x12, matrix products, contract(): lax.dot_general(left_side, right_side, (((left_dim,), (right_dim,)), ((),...  74.7 us
    unnamed x159, local copies, waits for them, and re-layouts  21.3 us
    all_gather x1, waiting for transfers between devices, on_device(): in_b = lax.all_gather(in_held, MIXER_OWNERS, axis=0, tiled=True)  20.5 us
    sub x5, other arithmetic, adam_step(): weight - rate * (first_hat / (jnp.sqrt(second_hat) + ADAM_EPS) + decay *...  17.1 us
    reduce_scatter x1, waiting for transfers between devices, on_device(): lax.psum_scatter(glu_part, GLU_OWNERS, scatter_dimension=0, tiled=True)  13.9 us
  transfers between devices with their start and end apart: 70, of which 49 were waited for; matrix products, arithmetic and copies ran while one was open for 20% of the time, Pallas kernels for 1%

profile of v2, /device:TPU:0, one launch (start us, length us, event | category | flops | bytes accessed | tf_op | source)
XLA Modules:
  0.0 609.8 jit_solution(6250274007932894434)
XLA Ops:
  10.4 3.9 collective-permute-start.2
  15.7 4.1 collective-permute-start.5
  26.2 3.0 collective-permute-done.5
  29.2 20.5 %collective-permute-done.4 = bf16[64,2816]{1,0:T(8,128)(2,1)S(1)} collective-permute-done((bf16[64,2816]{1,0:T(8,128)(2,1)S(1)}, bf16[64,2816]{1,0:T(8,128)(2,1)S(1)}, u32[]{:S(2)}, u32[]{:S(2)}) %collective-permute-start.4) | collective-permute-done | bytes 360480 | tf_op jit(solution)/shard_map/ppermute | solution.py:76
  51.7 3.6 collective-permute-done.6
  56.4 3.5 collective-permute-done.7
  66.9 2.2 collective-permute-done.10
  69.6 2.5 collective-permute-start.13
  73.2 12.3 %collective-permute-done.13 = bf16[128,2048]{0,1:T(8,128)(2,1)S(1)} collective-permute-done((bf16[128,2048]{0,1:T(8,128)(2,1)S(1)}, bf16[128,2048]{0,1:T(8,128)(2,1)S(1)}, u32[]{:S(2)}, u32[]{:S(2)}) %collective-permute-start.13) | collective-permute-done | bytes 524320 | tf_op jit(solution)/shard_map/ppermute | solution.py:76
  85.5 8.8 %collective-permute-done.12 = bf16[128,2048]{0,1:T(8,128)(2,1)S(1)} collective-permute-done((bf16[128,2048]{0,1:T(8,128)(2,1)S(1)}, bf16[128,2048]{0,1:T(8,128)(2,1)S(1)}, u32[]{:S(2)}, u32[]{:S(2)}) %collective-permute-start.12) | collective-permute-done | bytes 524320 | tf_op jit(solution)/shard_map/ppermute | solution.py:76
  95.9 20.5 %all-gather.5.cloned.1.call-done = bf16[2048,1536]{1,0:T(8,128)(2,1)} async-done(((bf16[256,1536]{1,0:T(8,128)(2,1)}), bf16[2048,1536]{1,0:T(8,128)(2,1)}) %all-gather.5.cloned.1.call-update) | async-done | bytes 6291472 | tf_op jit(solution)/shard_map/all_gather | solution.py:403
  116.4 6.2 %fusion.42.proj_ref = f32[512,1536]{1,0:T(8,128)S(1)} fusion(bf16[2048,1536]{1,0:T(8,128)(2,1)} %all-gather.5.cloned.1.call-done, bf16[128,2048]{0,1:T(8,128)(2,1)} %copy-done.61, bf16[128,2048]{0,1:T(8,128)(2,1)} %copy-done.63, bf16[128,2048]{0,1:T(8,128)(2,1)} %copy-done.65, bf16[128,2048]{0,1:T(8,128)(2,1)} %bitcast.293), kind=kOutput, calls=%fused_computation.135 | convolution fusion | flops 3229614080 | bytes 11534336 | tf_op jit(solution)/shard_map/dot_general | solution.py:30
  129.1 23.4 %collective-permute-done.15 = bf16[2,64,2048]{2,1,0:T(8,128)(2,1)S(1)} collective-permute-done((bf16[2,64,2048]{2,1,0:T(8,128)(2,1)S(1)}, bf16[2,64,2048]{2,1,0:T(8,128)(2,1)S(1)}, u32[]{:S(2)}, u32[]{:S(2)}) %collective-permute-start.15) | collective-permute-done | bytes 524320 | tf_op jit(solution)/shard_map/ppermute | solution.py:76
  154.1 3.3 shard_map.333
  166.7 5.3 collective-permute-done.18
  183.0 3.2 fusion.101
  192.0 2.2 collective-permute-start.25
  194.8 7.8 %collective-permute-done.24 = bf16[128,2048]{1,0:T(8,128)(2,1)} collective-permute-done((bf16[128,2048]{1,0:T(8,128)(2,1)}, bf16[128,2048]{1,0:T(8,128)(2,1)}, u32[]{:S(2)}, u32[]{:S(2)}) %collective-permute-start.24) | collective-permute-done | bytes 524320 | tf_op jit(solution)/shard_map/ppermute | solution.py:76
  202.6 8.4 %collective-permute-done.23 = bf16[128,2048]{1,0:T(8,128)(2,1)} collective-permute-done((bf16[128,2048]{1,0:T(8,128)(2,1)}, bf16[128,2048]{1,0:T(8,128)(2,1)}, u32[]{:S(2)}, u32[]{:S(2)}) %collective-permute-start.23) | collective-permute-done | bytes 524320 | tf_op jit(solution)/shard_map/ppermute | solution.py:76
  212.9 2.8 collective-permute-done.26
  220.5 6.7 %copy.80 = bf16[4,8,64,2816]{3,2,1,0:T(8,128)(2,1)S(1)} copy(bf16[4,8,64,2816]{3,2,0,1:T(8,128)(2,1)} %bitcast.268) | data formatting | bytes 23068672 | tf_op jit(solution)/shard_map/transpose | solution.py:446
  227.2 11.3 %collective-permute-done.27 = bf16[128,2048]{1,0:T(8,128)(2,1)S(1)} collective-permute-done((bf16[128,2048]{1,0:T(8,128)(2,1)}, bf16[128,2048]{1,0:T(8,128)(2,1)S(1)}, u32[]{:S(2)}, u32[]{:S(2)}) %collective-permute-start.27) | collective-permute-done | bytes 524320 | tf_op jit(solution)/shard_map/ppermute | solution.py:76
  242.6 9.5 %collective-permute-done.29 = bf16[128,2048]{1,0:T(8,128)(2,1)S(1)} collective-permute-done((bf16[128,2048]{1,0:T(8,128)(2,1)S(1)}, bf16[128,2048]{1,0:T(8,128)(2,1)S(1)}, u32[]{:S(2)}, u32[]{:S(2)}) %collective-permute-start.29) | collective-permute-done | bytes 524320 | tf_op jit(solution)/shard_map/ppermute | solution.py:76
  252.2 2.1 collective-permute-start.30
  254.4 7.9 %fusion.105 = f32[512,2816]{1,0:T(8,128)} fusion(bf16[512,2048]{1,0:T(8,128)(2,1)S(1)} %pad_maximum_fusion.4, bf16[2048,2816]{1,0:T(8,128)(2,1)S(1)} %bitcast.269), kind=kOutput, calls=%fused_computation.290 | convolution fusion | flops 5905580032 | bytes 19398656 | tf_op jit(solution)/shard_map/dot_general | solution.py:30
  263.1 3.9 copy.83
  267.0 3.2 copy.84
  274.8 10.5 %multiply_convert_fusion.2 = (bf16[512,1408]{1,0:T(8,128)(2,1)S(1)}, bf16[512,1408]{1,0:T(8,128)(2,1)S(1)}, bf16[512,1408]{1,0:T(8,128)(2,1)}) fusion(f32[512,2816]{1,0:T(8,128)} %fusion.105, bf16[512,2048]{1,0:T(8,128)(2,1)} %constant_dynamic-update-slice_fusion, bf16[1408,2048]{1,0:T(8,128)(2,1)} %all-gather.7.cloned.1.call-done), kind=kOutput, calls=%fused_computation.16 | convolution fusion | flops 2963603456 | bytes 17956864 | tf_op jit(solution)/shard_map/dot_general | solution.py:30
  286.9 8.9 %convolution_convert_fusion = bf16[2048,2816]{1,0:T(8,128)(2,1)} fusion(bf16[512,2048]{0,1:T(8,128)(2,1)S(1)} %bitcast.286, bf16[512,1408]{1,0:T(8,128)(2,1)S(1)} %get-tuple-element.154, bf16[512,1408]{1,0:T(8,128)(2,1)S(1)} %get-tuple-element.153), kind=kOutput, calls=%fused_computation | convolution fusion | flops 5917114368 | bytes 16515072 | tf_op jit(solution)/shard_map/dot_general | solution.py:30
  296.0 9.9 %fusion.102 = (bf16[512,2048]{1,0:T(8,128)(2,1)S(1)}, f32[512,2048]{1,0:T(8,128)S(1)}) fusion(bf16[2048,2816]{1,0:T(8,128)(2,1)} %bitcast.270, bf16[512,1408]{1,0:T(8,128)(2,1)} %copy-done.71, bf16[512,1408]{1,0:T(8,128)(2,1)} %copy-done.70), kind=kOutput, calls=%fused_computation.287 | convolution fusion | flops 5912395776 | bytes 20709376 | tf_op jit(solution)/shard_map/dot_general | solution.py:30
  308.1 14.9 %collective-permute-done.31 = bf16[128,2048]{1,0:T(8,128)(2,1)S(1)} collective-permute-done((bf16[128,2048]{1,0:T(8,128)(2,1)S(1)}, bf16[128,2048]{1,0:T(8,128)(2,1)S(1)}, u32[]{:S(2)}, u32[]{:S(2)}) %collective-permute-start.31) | collective-permute-done | bytes 524320 | tf_op jit(solution)/shard_map/ppermute | solution.py:76
  323.2 2.8 collective-permute-start.32
  326.0 3.6 collective-permute-done.33
  329.6 12.5 %collective-permute-done.32 = bf16[128,2048]{1,0:T(8,128)(2,1)S(1)} collective-permute-done((bf16[128,2048]{1,0:T(8,128)(2,1)S(1)}, bf16[128,2048]{1,0:T(8,128)(2,1)S(1)}, u32[]{:S(2)}, u32[]{:S(2)}) %collective-permute-start.32) | collective-permute-done | bytes 524320 | tf_op jit(solution)/shard_map/ppermute | solution.py:76
  344.0 5.5 fusion.103
  351.8 2.4 collective-permute-start.36
  356.9 9.7 %collective-permute-done.37 = bf16[128,2048]{1,0:T(8,128)(2,1)S(1)} collective-permute-done((bf16[128,2048]{1,0:T(8,128)(2,1)S(1)}, bf16[128,2048]{1,0:T(8,128)(2,1)S(1)}, u32[]{:S(2)}, u32[]{:S(2)}) %collective-permute-start.37) | collective-permute-done | bytes 524320 | tf_op jit(solution)/shard_map/ppermute | solution.py:76
  373.4 4.7 collective-permute-done.35
  379.9 2.6 collective-permute-done.38
  382.5 3.2 fusion.41
  385.7 2.6 convolution_convert_fusion.3
  388.3 13.9 %reduce-scatter.6.cloned.1.call-done = bf16[256,2816]{1,0:T(8,128)(2,1)} async-done(((bf16[2048,2816]{1,0:T(8,128)(2,1)}), bf16[256,2816]{1,0:T(8,128)(2,1)}) %reduce-scatter.6.cloned.1.call-update) | async-done | bytes 1441808 | tf_op jit(solution)/shard_map/reduce_scatter | solution.py:472
  402.5 4.3 multiply_reduce_fusion.4
  408.1 2.2 collective-permute-done.40
  411.8 2.2 collective-permute-done.41
  414.8 3.2 shard_map.334
  419.6 2.5 collective-permute-done.42
  422.2 2.5 collective-permute-start.43
  424.8 2.5 collective-permute-done.43
  429.5 5.3 convolution_convert_fusion.2
  434.8 5.4 convolution_convert_fusion.1
  443.6 5.1 fusion.104
  452.7 10.9 %collective-permute-done.46 = bf16[128,2048]{1,0:T(8,128)(2,1)S(1)} collective-permute-done((bf16[128,2048]{1,0:T(8,128)(2,1)S(1)}, bf16[128,2048]{1,0:T(8,128)(2,1)S(1)}, u32[]{:S(2)}, u32[]{:S(2)}) %collective-permute-start.46) | collective-permute-done | bytes 524320 | tf_op jit(solution)/shard_map/ppermute | solution.py:76
  463.6 12.0 %collective-permute-done.45 = bf16[128,2048]{1,0:T(8,128)(2,1)S(1)} collective-permute-done((bf16[128,2048]{1,0:T(8,128)(2,1)S(1)}, bf16[128,2048]{1,0:T(8,128)(2,1)S(1)}, u32[]{:S(2)}, u32[]{:S(2)}) %collective-permute-start.45) | collective-permute-done | bytes 524320 | tf_op jit(solution)/shard_map/ppermute | solution.py:76
  479.5 3.9 fusion
  488.5 15.1 %collective-permute-done.50 = bf16[176,2048]{1,0:T(8,128)(2,1)S(1)} collective-permute-done((bf16[176,2048]{1,0:T(8,128)(2,1)S(1)}, bf16[176,2048]{1,0:T(8,128)(2,1)S(1)}, u32[]{:S(2)}, u32[]{:S(2)}) %collective-permute-start.50) | collective-permute-done | bytes 720928 | tf_op jit(solution)/shard_map/ppermute | solution.py:76
  503.7 14.0 %collective-permute-done.49 = bf16[176,2048]{1,0:T(8,128)(2,1)S(1)} collective-permute-done((bf16[176,2048]{1,0:T(8,128)(2,1)S(1)}, bf16[176,2048]{1,0:T(8,128)(2,1)S(1)}, u32[]{:S(2)}, u32[]{:S(2)}) %collective-permute-start.49) | collective-permute-done | bytes 720928 | tf_op jit(solution)/shard_map/ppermute | solution.py:76
  524.7 2.1 multiply_reduce_fusion.1
  544.1 2.9 collective-permute-start.56
  554.0 3.6 collective-permute-done.56
  557.6 18.4 %collective-permute-done.55 = bf16[64,2816]{1,0:T(8,128)(2,1)} collective-permute-done((bf16[64,2816]{1,0:T(8,128)(2,1)}, bf16[64,2816]{1,0:T(8,128)(2,1)}, u32[]{:S(2)}, u32[]{:S(2)}) %collective-permute-start.55) | collective-permute-done | bytes 360480 | tf_op jit(solution)/shard_map/ppermute | solution.py:76
  583.0 5.3 multiply_subtract_fusion.1
  589.4 6.8 %multiply_subtract_fusion = (f32[64,11264]{1,0:T(8,128)}, f32[64,11264]{1,0:T(8,128)}, f32[64,11264]{1,0:T(8,128)}) fusion(f32[64,11264]{1,0:T(8,128)S(1)} %copy-done.1, f32[]{:T(128)S(6)} %min.3, bf16[64,11264]{1,0:T(8,128)(2,1)} %fusion.45, f32[64,11264]{1,0:T(8,128)S(1)} %copy-done.28, f32[64,11264]{1,0:T(8,128)S(1)} %copy-done.29), kind=kLoop, calls=%fused_computation.9 | loop fusion | flops 12255232 | bytes 18743300 | tf_op jit(solution)/shard_map/sub | solution.py:65
  596.3 2.8 multiply_subtract_fusion.2
  (409 shorter events, 147.9 us)
Async XLA Ops:
  7.2 109.2 %all-gather.5.cloned.1.call-start = ((), (), s32[]{:S(2)}) async-start(), calls=%async_computation.3 | async-start | bytes 7077888 | tf_op jit(solution)/shard_map/all_gather | solution.py:403
  10.4 9.9 %collective-permute-start.2 = (bf16[64,1536]{1,0:T(8,128)(2,1)}, bf16[64,1536]{1,0:T(8,128)(2,1)S(1)}, u32[]{:S(2)}, u32[]{:S(2)}) collective-permute-start(bf16[64,1536]{1,0:T(8,128)(2,1)} %get-tuple-element.202), channel_id=1, source_target_pairs={{0,6},{2,4},{4,2},{6,0},{1,7},{3,5},{5,3},{7,1},{8,14},{10,12},{12... | collective-permute-start | bytes 589832 | tf_op jit(solution)/shard_map/ppermute | solution.py:76
  14.3 9.4 %collective-permute-start.1 = (bf16[64,1536]{1,0:T(8,128)(2,1)}, bf16[64,1536]{1,0:T(8,128)(2,1)}, u32[]{:S(2)}, u32[]{:S(2)}) collective-permute-start(bf16[64,1536]{1,0:T(8,128)(2,1)} %get-tuple-element.203), channel_id=1, source_target_pairs={{0,4},{2,6},{4,0},{6,2},{1,5},{3,7},{5,1},{7,3},{8,12},{10,14},{12... | collective-permute-start | bytes 589832 | tf_op jit(solution)/shard_map/ppermute | solution.py:76
  14.8 9.2 %collective-permute-start = (bf16[64,1536]{1,0:T(8,128)(2,1)S(1)}, bf16[64,1536]{1,0:T(8,128)(2,1)}, u32[]{:S(2)}, u32[]{:S(2)}) collective-permute-start(bf16[64,1536]{1,0:T(8,128)(2,1)S(1)} %get-tuple-element.204), channel_id=1, source_target_pairs={{0,2},{2,0},{4,6},{6,4},{1,3},{3,1},{5,7},{7,5},{8,10},{10,8},{12,... | collective-permute-start | bytes 589832 | tf_op jit(solution)/shard_map/ppermute | solution.py:76
  15.7 13.6 %collective-permute-start.5 = (bf16[64,2816]{1,0:T(8,128)(2,1)S(1)}, bf16[64,2816]{1,0:T(8,128)(2,1)S(1)}, u32[]{:S(2)}, u32[]{:S(2)}) collective-permute-start(bf16[64,2816]{1,0:T(8,128)(2,1)S(1)} %get-tuple-element.186), channel_id=1, source_target_pairs={{0,24},{8,16},{16,8},{24,0},{1,25},{9,17},{17,9},{25,1},{2,26},{10... | collective-permute-start | bytes 1081352 | tf_op jit(solution)/shard_map/ppermute | solution.py:76
  19.8 29.9 %collective-permute-start.4 = (bf16[64,2816]{1,0:T(8,128)(2,1)S(1)}, bf16[64,2816]{1,0:T(8,128)(2,1)S(1)}, u32[]{:S(2)}, u32[]{:S(2)}) collective-permute-start(bf16[64,2816]{1,0:T(8,128)(2,1)S(1)} %get-tuple-element.187), channel_id=1, source_target_pairs={{0,16},{8,24},{16,0},{24,8},{1,17},{9,25},{17,1},{25,9},{2,18},{10... | collective-permute-start | bytes 1081352 | tf_op jit(solution)/shard_map/ppermute | solution.py:76
  20.3 29.4 %collective-permute-start.3 = (bf16[64,2816]{1,0:T(8,128)(2,1)S(1)}, bf16[64,2816]{1,0:T(8,128)(2,1)S(1)}, u32[]{:S(2)}, u32[]{:S(2)}) collective-permute-start(bf16[64,2816]{1,0:T(8,128)(2,1)S(1)} %get-tuple-element.188), channel_id=1, source_target_pairs={{0,8},{8,0},{16,24},{24,16},{1,9},{9,1},{17,25},{25,17},{2,10},{10... | collective-permute-start | bytes 1081352 | tf_op jit(solution)/shard_map/ppermute | solution.py:76
  51.3 166.6 %all-gather.9.cloned.1.call-start = ((), (), s32[]{:S(2)}) async-start(), calls=%async_computation.8 | async-start | bytes 12976128 | tf_op jit(solution)/shard_map/all_gather | solution.py:412
  51.6 3.7 collective-permute-start.6
  55.4 4.6 collective-permute-start.7
  61.2 3.8 collective-permute-start.9
  65.1 4.0 collective-permute-start.10
  69.6 15.9 %collective-permute-start.13 = (bf16[128,2048]{0,1:T(8,128)(2,1)S(1)}, bf16[128,2048]{0,1:T(8,128)(2,1)S(1)}, u32[]{:S(2)}, u32[]{:S(2)}) collective-permute-start(bf16[128,2048]{0,1:T(8,128)(2,1)S(1)} %bitcast.290), channel_id=1, source_target_pairs={{0,6},{2,4},{4,2},{6,0},{1,7},{3,5},{5,3},{7,1},{8,14},{10,12},{12... | collective-permute-start | bytes 1572872 | tf_op jit(solution)/shard_map/ppermute | solution.py:76
  72.1 22.2 %collective-permute-start.12 = (bf16[128,2048]{0,1:T(8,128)(2,1)S(1)}, bf16[128,2048]{0,1:T(8,128)(2,1)S(1)}, u32[]{:S(2)}, u32[]{:S(2)}) collective-permute-start(bf16[128,2048]{0,1:T(8,128)(2,1)S(1)} %bitcast.291), channel_id=1, source_target_pairs={{0,4},{2,6},{4,0},{6,2},{1,5},{3,7},{5,1},{7,3},{8,12},{10,14},{12... | collective-permute-start | bytes 1572872 | tf_op jit(solution)/shard_map/ppermute | solution.py:76
  72.6 21.8 %collective-permute-start.11 = (bf16[128,2048]{0,1:T(8,128)(2,1)S(1)}, bf16[128,2048]{0,1:T(8,128)(2,1)S(1)}, u32[]{:S(2)}, u32[]{:S(2)}) collective-permute-start(bf16[128,2048]{0,1:T(8,128)(2,1)S(1)} %bitcast.292), channel_id=1, source_target_pairs={{0,2},{2,0},{4,6},{6,4},{1,3},{3,1},{5,7},{7,5},{8,10},{10,8},{12,... | collective-permute-start | bytes 1572872 | tf_op jit(solution)/shard_map/ppermute | solution.py:76
  122.6 152.2 %all-gather.7.cloned.1.call-start = ((), (), s32[]{:S(2)}) async-start(), calls=%async_computation.4 | async-start | bytes 6488064 | tf_op jit(solution)/shard_map/all_gather | solution.py:443
  127.6 25.0 %collective-permute-start.15 = (bf16[2,64,2048]{2,1,0:T(8,128)(2,1)S(1)}, bf16[2,64,2048]{2,1,0:T(8,128)(2,1)S(1)}, u32[]{:S(2)}, u32[]{:S(2)}) collective-permute-start(bf16[2,64,2048]{2,1,0:T(8,128)(2,1)S(1)} %pad_maximum_fusion.19), channel_id=1, source_target_pairs={{0,8},{8,0},{16,24},{24,16},{1,9},{9,1},{17,25},{25,17},{2,10},{10... | collective-permute-start | bytes 1572872 | tf_op jit(solution)/shard_map/ppermute | solution.py:76
  127.7 26.4 %collective-permute-start.16 = (bf16[2,64,2048]{2,1,0:T(8,128)(2,1)S(1)}, bf16[2,64,2048]{2,1,0:T(8,128)(2,1)}, u32[]{:S(2)}, u32[]{:S(2)}) collective-permute-start(bf16[2,64,2048]{2,1,0:T(8,128)(2,1)S(1)} %pad_maximum_fusion.19), channel_id=1, source_target_pairs={{0,16},{8,24},{16,0},{24,8},{1,17},{9,25},{17,1},{25,9},{2,18},{10... | collective-permute-start | bytes 1572872 | tf_op jit(solution)/shard_map/ppermute | solution.py:76
  159.4 4.0 collective-permute-start.17
  159.6 13.7 %collective-permute-start.19 = (bf16[2,64,2048]{2,1,0:T(8,128)(2,1)}, bf16[2,64,2048]{2,1,0:T(8,128)(2,1)}, u32[]{:S(2)}, u32[]{:S(2)}) collective-permute-start(bf16[2,64,2048]{2,1,0:T(8,128)(2,1)} %collective-permute-done.16), channel_id=1, source_target_pairs={{0,8},{8,0},{16,24},{24,16},{1,9},{9,1},{17,25},{25,17},{2,10},{10... | collective-permute-start | bytes 1572872 | tf_op jit(solution)/shard_map/ppermute | solution.py:76
  163.4 8.6 %collective-permute-start.18 = (f32[4,2,512]{2,1,0:T(2,128)S(1)}, f32[4,2,512]{2,1,0:T(2,128)S(1)}, u32[]{:S(2)}, u32[]{:S(2)}) collective-permute-start(f32[4,2,512]{2,1,0:T(2,128)S(1)} %constant_dynamic-update-slice_fusion.10), channel_id=1, source_target_pairs={{0,16},{8,24},{16,0},{24,8},{1,17},{9,25},{17,1},{25,9},{2,18},{10... | collective-permute-start | bytes 49160 | tf_op jit(solution)/shard_map/ppermute | solution.py:76
  175.2 3.7 collective-permute-start.20
  187.4 15.2 %collective-permute-start.24 = (bf16[128,2048]{1,0:T(8,128)(2,1)}, bf16[128,2048]{1,0:T(8,128)(2,1)}, u32[]{:S(2)}, u32[]{:S(2)}) collective-permute-start(bf16[128,2048]{1,0:T(8,128)(2,1)} %get-tuple-element.171), channel_id=1, source_target_pairs={{0,2},{2,0},{4,6},{6,4},{1,3},{3,1},{5,7},{7,5},{8,10},{10,8},{12,... | collective-permute-start | bytes 1572872 | tf_op jit(solution)/shard_map/ppermute | solution.py:76
  188.9 22.1 %collective-permute-start.23 = (bf16[128,2048]{1,0:T(8,128)(2,1)}, bf16[128,2048]{1,0:T(8,128)(2,1)}, u32[]{:S(2)}, u32[]{:S(2)}) collective-permute-start(bf16[128,2048]{1,0:T(8,128)(2,1)} %get-tuple-element.172), channel_id=1, source_target_pairs={{0,4},{2,6},{4,0},{6,2},{1,5},{3,7},{5,1},{7,3},{8,12},{10,14},{12... | collective-permute-start | bytes 1572872 | tf_op jit(solution)/shard_map/ppermute | solution.py:76
  190.3 20.6 %collective-permute-start.22 = (bf16[128,2048]{1,0:T(8,128)(2,1)}, bf16[128,2048]{1,0:T(8,128)(2,1)}, u32[]{:S(2)}, u32[]{:S(2)}) collective-permute-start(bf16[128,2048]{1,0:T(8,128)(2,1)} %get-tuple-element.170), channel_id=1, source_target_pairs={{0,6},{2,4},{4,2},{6,0},{1,7},{3,5},{5,3},{7,1},{8,14},{10,12},{12... | collective-permute-start | bytes 1572872 | tf_op jit(solution)/shard_map/ppermute | solution.py:76
  192.0 21.0 %collective-permute-start.25 = (bf16[128,2048]{1,0:T(8,128)(2,1)}, bf16[128,2048]{1,0:T(8,128)(2,1)S(1)}, u32[]{:S(2)}, u32[]{:S(2)}) collective-permute-start(bf16[128,2048]{1,0:T(8,128)(2,1)} %fusion.19), channel_id=1, source_target_pairs={{0,8},{8,0},{16,24},{24,16},{1,9},{9,1},{17,25},{25,17},{2,10},{10... | collective-permute-start | bytes 1572872 | tf_op jit(solution)/shard_map/ppermute | solution.py:76
  194.1 21.6 %collective-permute-start.26 = (bf16[128,2048]{1,0:T(8,128)(2,1)}, bf16[128,2048]{1,0:T(8,128)(2,1)}, u32[]{:S(2)}, u32[]{:S(2)}) collective-permute-start(bf16[128,2048]{1,0:T(8,128)(2,1)} %fusion.19), channel_id=1, source_target_pairs={{0,16},{8,24},{16,0},{24,8},{1,17},{9,25},{17,1},{25,9},{2,18},{10... | collective-permute-start | bytes 1572872 | tf_op jit(solution)/shard_map/ppermute | solution.py:76
  218.0 184.2 %reduce-scatter.6.cloned.1.call-start = ((), (), s32[]{:S(2)}) async-start(), calls=%async_computation.6 | async-start | bytes 12976128 | tf_op jit(solution)/shard_map/reduce_scatter | solution.py:472
  218.5 20.0 %collective-permute-start.27 = (bf16[128,2048]{1,0:T(8,128)(2,1)}, bf16[128,2048]{1,0:T(8,128)(2,1)S(1)}, u32[]{:S(2)}, u32[]{:S(2)}) collective-permute-start(bf16[128,2048]{1,0:T(8,128)(2,1)} %multiply_convert_fusion.5), channel_id=1, source_target_pairs={{0,8},{8,0},{16,24},{24,16},{1,9},{9,1},{17,25},{25,17},{2,10},{10... | collective-permute-start | bytes 1572872 | tf_op jit(solution)/shard_map/ppermute | solution.py:76
  218.6 21.9 %collective-permute-start.28 = (bf16[128,2048]{1,0:T(8,128)(2,1)}, bf16[128,2048]{1,0:T(8,128)(2,1)S(1)}, u32[]{:S(2)}, u32[]{:S(2)}) collective-permute-start(bf16[128,2048]{1,0:T(8,128)(2,1)} %multiply_convert_fusion.5), channel_id=1, source_target_pairs={{0,16},{8,24},{16,0},{24,8},{1,17},{9,25},{17,1},{25,9},{2,18},{10... | collective-permute-start | bytes 1572872 | tf_op jit(solution)/shard_map/ppermute | solution.py:76
  240.5 11.6 %collective-permute-start.29 = (bf16[128,2048]{1,0:T(8,128)(2,1)S(1)}, bf16[128,2048]{1,0:T(8,128)(2,1)S(1)}, u32[]{:S(2)}, u32[]{:S(2)}) collective-permute-start(bf16[128,2048]{1,0:T(8,128)(2,1)S(1)} %collective-permute-done.28), channel_id=1, source_target_pairs={{0,8},{8,0},{16,24},{24,16},{1,9},{9,1},{17,25},{25,17},{2,10},{10... | collective-permute-start | bytes 1572872 | tf_op jit(solution)/shard_map/ppermute | solution.py:76
  252.2 20.7 %collective-permute-start.30 = (bf16[128,2048]{1,0:T(8,128)(2,1)}, bf16[128,2048]{1,0:T(8,128)(2,1)}, u32[]{:S(2)}, u32[]{:S(2)}) collective-permute-start(bf16[128,2048]{1,0:T(8,128)(2,1)} %collective-permute-done.26), channel_id=1, source_target_pairs={{0,8},{8,0},{16,24},{24,16},{1,9},{9,1},{17,25},{25,17},{2,10},{10... | collective-permute-start | bytes 1572872 | tf_op jit(solution)/shard_map/ppermute | solution.py:76
  295.8 226.6 %reduce-scatter.8.cloned.1.call-start = ((), (), s32[]{:S(2)}) async-start(), calls=%async_computation.7 | async-start | bytes 2359296 | tf_op jit(solution)/shard_map/reduce_scatter | solution.py:494
  306.0 17.0 %collective-permute-start.31 = (bf16[128,2048]{1,0:T(8,128)(2,1)S(1)}, bf16[128,2048]{1,0:T(8,128)(2,1)S(1)}, u32[]{:S(2)}, u32[]{:S(2)}) collective-permute-start(bf16[128,2048]{1,0:T(8,128)(2,1)S(1)} %get-tuple-element.168), channel_id=1, source_target_pairs={{0,8},{8,0},{16,24},{24,16},{1,9},{9,1},{17,25},{25,17},{2,10},{10... | collective-permute-start | bytes 1572872 | tf_op jit(solution)/shard_map/ppermute | solution.py:76
  306.1 23.5 %collective-permute-start.33 = (bf16[128,2048]{1,0:T(8,128)(2,1)S(1)}, bf16[128,2048]{1,0:T(8,128)(2,1)S(1)}, u32[]{:S(2)}, u32[]{:S(2)}) collective-permute-start(bf16[128,2048]{1,0:T(8,128)(2,1)S(1)} %get-tuple-element.169), channel_id=1, source_target_pairs={{0,8},{8,0},{16,24},{24,16},{1,9},{9,1},{17,25},{25,17},{2,10},{10... | collective-permute-start | bytes 1572872 | tf_op jit(solution)/shard_map/ppermute | solution.py:76
  323.2 18.9 %collective-permute-start.32 = (bf16[128,2048]{1,0:T(8,128)(2,1)S(1)}, bf16[128,2048]{1,0:T(8,128)(2,1)S(1)}, u32[]{:S(2)}, u32[]{:S(2)}) collective-permute-start(bf16[128,2048]{1,0:T(8,128)(2,1)S(1)} %fusion.14), channel_id=1, source_target_pairs={{0,16},{8,24},{16,0},{24,8},{1,17},{9,25},{17,1},{25,9},{2,18},{10... | collective-permute-start | bytes 1572872 | tf_op jit(solution)/shard_map/ppermute | solution.py:76
  350.5 16.1 %collective-permute-start.37 = (bf16[128,2048]{1,0:T(8,128)(2,1)S(1)}, bf16[128,2048]{1,0:T(8,128)(2,1)S(1)}, u32[]{:S(2)}, u32[]{:S(2)}) collective-permute-start(bf16[128,2048]{1,0:T(8,128)(2,1)S(1)} %get-tuple-element.166), channel_id=1, source_target_pairs={{0,8},{8,0},{16,24},{24,16},{1,9},{9,1},{17,25},{25,17},{2,10},{10... | collective-permute-start | bytes 1572872 | tf_op jit(solution)/shard_map/ppermute | solution.py:76
  351.8 21.5 %collective-permute-start.36 = (bf16[128,2048]{1,0:T(8,128)(2,1)}, bf16[128,2048]{1,0:T(8,128)(2,1)}, u32[]{:S(2)}, u32[]{:S(2)}) collective-permute-start(bf16[128,2048]{1,0:T(8,128)(2,1)} %convert_element_type.183), channel_id=1, source_target_pairs={{0,6},{2,4},{4,2},{6,0},{1,7},{3,5},{5,3},{7,1},{8,14},{10,12},{12... | collective-permute-start | bytes 1572872 | tf_op jit(solution)/shard_map/ppermute | solution.py:76
  354.2 23.9 %collective-permute-start.35 = (bf16[128,2048]{1,0:T(8,128)(2,1)}, bf16[128,2048]{1,0:T(8,128)(2,1)}, u32[]{:S(2)}, u32[]{:S(2)}) collective-permute-start(bf16[128,2048]{1,0:T(8,128)(2,1)} %convert_element_type.183), channel_id=1, source_target_pairs={{0,4},{2,6},{4,0},{6,2},{1,5},{3,7},{5,1},{7,3},{8,12},{10,14},{12... | collective-permute-start | bytes 1572872 | tf_op jit(solution)/shard_map/ppermute | solution.py:76
  354.7 23.4 %collective-permute-start.34 = (bf16[128,2048]{1,0:T(8,128)(2,1)}, bf16[128,2048]{1,0:T(8,128)(2,1)}, u32[]{:S(2)}, u32[]{:S(2)}) collective-permute-start(bf16[128,2048]{1,0:T(8,128)(2,1)} %convert_element_type.183), channel_id=1, source_target_pairs={{0,2},{2,0},{4,6},{6,4},{1,3},{3,1},{5,7},{7,5},{8,10},{10,8},{12,... | collective-permute-start | bytes 1572872 | tf_op jit(solution)/shard_map/ppermute | solution.py:76
  355.3 24.6 %collective-permute-start.39 = (bf16[128,2048]{1,0:T(8,128)(2,1)}, bf16[128,2048]{1,0:T(8,128)(2,1)}, u32[]{:S(2)}, u32[]{:S(2)}) collective-permute-start(bf16[128,2048]{1,0:T(8,128)(2,1)} %get-tuple-element.167), channel_id=1, source_target_pairs={{0,8},{8,0},{16,24},{24,16},{1,9},{9,1},{17,25},{25,17},{2,10},{10... | collective-permute-start | bytes 1572872 | tf_op jit(solution)/shard_map/ppermute | solution.py:76
  367.5 15.0 %collective-permute-start.38 = (bf16[128,2048]{1,0:T(8,128)(2,1)}, bf16[128,2048]{1,0:T(8,128)(2,1)}, u32[]{:S(2)}, u32[]{:S(2)}) collective-permute-start(bf16[128,2048]{1,0:T(8,128)(2,1)} %fusion.10), channel_id=1, source_target_pairs={{0,16},{8,24},{16,0},{24,8},{1,17},{9,25},{17,1},{25,9},{2,18},{10... | collective-permute-start | bytes 1572872 | tf_op jit(solution)/shard_map/ppermute | solution.py:76
  402.2 122.5 %reduce-scatter.4.cloned.1.call-start = ((), (), s32[]{:S(2)}) async-start(), calls=%async_computation.5 | async-start | bytes 7077888 | tf_op jit(solution)/shard_map/reduce_scatter | solution.py:529
  418.1 4.1 collective-permute-start.42
  422.2 5.1 collective-permute-start.43
  443.6 35.9 %collective-permute-start.47 = (bf16[4,176,2048]{2,1,0:T(8,128)(2,1)}, bf16[4,176,2048]{2,1,0:T(8,128)(2,1)}, u32[]{:S(2)}, u32[]{:S(2)}) collective-permute-start(bf16[4,176,2048]{2,1,0:T(8,128)(2,1)} %dynamic-slice_bitcast_fusion), channel_id=1, source_target_pairs={{0,1},{1,0},{2,3},{3,2},{4,5},{5,4},{6,7},{7,6},{8,9},{9,8},{10,11... | collective-permute-start | bytes 8650760 | tf_op jit(solution)/shard_map/ppermute | solution.py:76
  448.8 14.8 %collective-permute-start.46 = (bf16[128,2048]{1,0:T(8,128)(2,1)S(1)}, bf16[128,2048]{1,0:T(8,128)(2,1)S(1)}, u32[]{:S(2)}, u32[]{:S(2)}) collective-permute-start(bf16[128,2048]{1,0:T(8,128)(2,1)S(1)} %get-tuple-element.164), channel_id=1, source_target_pairs={{0,2},{2,0},{4,6},{6,4},{1,3},{3,1},{5,7},{7,5},{8,10},{10,8},{12,... | collective-permute-start | bytes 1572872 | tf_op jit(solution)/shard_map/ppermute | solution.py:76
  450.3 25.3 %collective-permute-start.45 = (bf16[128,2048]{1,0:T(8,128)(2,1)S(1)}, bf16[128,2048]{1,0:T(8,128)(2,1)S(1)}, u32[]{:S(2)}, u32[]{:S(2)}) collective-permute-start(bf16[128,2048]{1,0:T(8,128)(2,1)S(1)} %get-tuple-element.165), channel_id=1, source_target_pairs={{0,4},{2,6},{4,0},{6,2},{1,5},{3,7},{5,1},{7,3},{8,12},{10,14},{12... | collective-permute-start | bytes 1572872 | tf_op jit(solution)/shard_map/ppermute | solution.py:76
  450.7 24.9 %collective-permute-start.44 = (bf16[128,2048]{1,0:T(8,128)(2,1)S(1)}, bf16[128,2048]{1,0:T(8,128)(2,1)S(1)}, u32[]{:S(2)}, u32[]{:S(2)}) collective-permute-start(bf16[128,2048]{1,0:T(8,128)(2,1)S(1)} %get-tuple-element.163), channel_id=1, source_target_pairs={{0,6},{2,4},{4,2},{6,0},{1,7},{3,5},{5,3},{7,1},{8,14},{10,12},{12... | collective-permute-start | bytes 1572872 | tf_op jit(solution)/shard_map/ppermute | solution.py:76
  483.6 20.1 %collective-permute-start.50 = (bf16[176,2048]{1,0:T(8,128)(2,1)S(1)}, bf16[176,2048]{1,0:T(8,128)(2,1)S(1)}, u32[]{:S(2)}, u32[]{:S(2)}) collective-permute-start(bf16[176,2048]{1,0:T(8,128)(2,1)S(1)} %get-tuple-element.161), channel_id=1, source_target_pairs={{0,6},{2,4},{4,2},{6,0},{1,7},{3,5},{5,3},{7,1},{8,14},{10,12},{12... | collective-permute-start | bytes 2162696 | tf_op jit(solution)/shard_map/ppermute | solution.py:76
  485.1 32.5 %collective-permute-start.49 = (bf16[176,2048]{1,0:T(8,128)(2,1)S(1)}, bf16[176,2048]{1,0:T(8,128)(2,1)S(1)}, u32[]{:S(2)}, u32[]{:S(2)}) collective-permute-start(bf16[176,2048]{1,0:T(8,128)(2,1)S(1)} %get-tuple-element.162), channel_id=1, source_target_pairs={{0,4},{2,6},{4,0},{6,2},{1,5},{3,7},{5,1},{7,3},{8,12},{10,14},{12... | collective-permute-start | bytes 2162696 | tf_op jit(solution)/shard_map/ppermute | solution.py:76
  485.7 31.9 %collective-permute-start.48 = (bf16[176,2048]{1,0:T(8,128)(2,1)S(1)}, bf16[176,2048]{1,0:T(8,128)(2,1)S(1)}, u32[]{:S(2)}, u32[]{:S(2)}) collective-permute-start(bf16[176,2048]{1,0:T(8,128)(2,1)S(1)} %get-tuple-element.160), channel_id=1, source_target_pairs={{0,2},{2,0},{4,6},{6,4},{1,3},{3,1},{5,7},{7,5},{8,10},{10,8},{12,... | collective-permute-start | bytes 2162696 | tf_op jit(solution)/shard_map/ppermute | solution.py:76
  528.8 4.0 collective-permute-start.59
  529.5 5.1 collective-permute-start.60
  531.0 3.9 collective-permute-start.58
  534.9 8.1 %collective-permute-start.62 = (f32[4,2048]{1,0:T(4,128)S(1)}, f32[4,2048]{1,0:T(4,128)S(1)}, u32[]{:S(2)}, u32[]{:S(2)}) collective-permute-start(f32[4,2048]{1,0:T(4,128)S(1)} %add_add_fusion.1), channel_id=1, source_target_pairs={{0,16},{8,24},{16,0},{24,8},{1,17},{9,25},{17,1},{25,9},{2,18},{10... | collective-permute-start | bytes 98312 | tf_op jit(solution)/shard_map/ppermute | solution.py:76
  536.8 7.2 %collective-permute-start.63 = (f32[4,2048]{1,0:T(4,128)S(1)}, f32[4,2048]{1,0:T(4,128)S(1)}, u32[]{:S(2)}, u32[]{:S(2)}) collective-permute-start(f32[4,2048]{1,0:T(4,128)S(1)} %add_add_fusion.1), channel_id=1, source_target_pairs={{0,24},{8,16},{16,8},{24,0},{1,25},{9,17},{17,9},{25,1},{2,26},{10... | collective-permute-start | bytes 98312 | tf_op jit(solution)/shard_map/ppermute | solution.py:76
  538.8 8.2 %collective-permute-start.61 = (f32[4,2048]{1,0:T(4,128)S(1)}, f32[4,2048]{1,0:T(4,128)S(1)}, u32[]{:S(2)}, u32[]{:S(2)}) collective-permute-start(f32[4,2048]{1,0:T(4,128)S(1)} %add_add_fusion.1), channel_id=1, source_target_pairs={{0,8},{8,0},{16,24},{24,16},{1,9},{9,1},{17,25},{25,17},{2,10},{10... | collective-permute-start | bytes 98312 | tf_op jit(solution)/shard_map/ppermute | solution.py:76
  540.5 9.0 %collective-permute-start.53 = (bf16[64,1536]{1,0:T(8,128)(2,1)S(1)}, bf16[64,1536]{1,0:T(8,128)(2,1)S(1)}, u32[]{:S(2)}, u32[]{:S(2)}) collective-permute-start(bf16[64,1536]{1,0:T(8,128)(2,1)S(1)} %get-tuple-element.194), channel_id=1, source_target_pairs={{0,6},{2,4},{4,2},{6,0},{1,7},{3,5},{5,3},{7,1},{8,14},{10,12},{12... | collective-permute-start | bytes 589832 | tf_op jit(solution)/shard_map/ppermute | solution.py:76
  541.8 9.2 %collective-permute-start.52 = (bf16[64,1536]{1,0:T(8,128)(2,1)S(1)}, bf16[64,1536]{1,0:T(8,128)(2,1)S(1)}, u32[]{:S(2)}, u32[]{:S(2)}) collective-permute-start(bf16[64,1536]{1,0:T(8,128)(2,1)S(1)} %get-tuple-element.195), channel_id=1, source_target_pairs={{0,4},{2,6},{4,0},{6,2},{1,5},{3,7},{5,1},{7,3},{8,12},{10,14},{12... | collective-permute-start | bytes 589832 | tf_op jit(solution)/shard_map/ppermute | solution.py:76
  543.0 8.0 %collective-permute-start.51 = (bf16[64,1536]{1,0:T(8,128)(2,1)S(1)}, bf16[64,1536]{1,0:T(8,128)(2,1)S(1)}, u32[]{:S(2)}, u32[]{:S(2)}) collective-permute-start(bf16[64,1536]{1,0:T(8,128)(2,1)S(1)} %get-tuple-element.196), channel_id=1, source_target_pairs={{0,2},{2,0},{4,6},{6,4},{1,3},{3,1},{5,7},{7,5},{8,10},{10,8},{12,... | collective-permute-start | bytes 589832 | tf_op jit(solution)/shard_map/ppermute | solution.py:76
  544.1 13.5 %collective-permute-start.56 = (bf16[64,2816]{1,0:T(8,128)(2,1)}, bf16[64,2816]{1,0:T(8,128)(2,1)}, u32[]{:S(2)}, u32[]{:S(2)}) collective-permute-start(bf16[64,2816]{1,0:T(8,128)(2,1)} %get-tuple-element.118), channel_id=1, source_target_pairs={{0,24},{8,16},{16,8},{24,0},{1,25},{9,17},{17,9},{25,1},{2,26},{10... | collective-permute-start | bytes 1081352 | tf_op jit(solution)/shard_map/ppermute | solution.py:76
  547.0 29.0 %collective-permute-start.55 = (bf16[64,2816]{1,0:T(8,128)(2,1)}, bf16[64,2816]{1,0:T(8,128)(2,1)}, u32[]{:S(2)}, u32[]{:S(2)}) collective-permute-start(bf16[64,2816]{1,0:T(8,128)(2,1)} %get-tuple-element.117), channel_id=1, source_target_pairs={{0,16},{8,24},{16,0},{24,8},{1,17},{9,25},{17,1},{25,9},{2,18},{10... | collective-permute-start | bytes 1081352 | tf_op jit(solution)/shard_map/ppermute | solution.py:76
  549.5 26.4 %collective-permute-start.54 = (bf16[64,2816]{1,0:T(8,128)(2,1)}, bf16[64,2816]{1,0:T(8,128)(2,1)}, u32[]{:S(2)}, u32[]{:S(2)}) collective-permute-start(bf16[64,2816]{1,0:T(8,128)(2,1)} %get-tuple-element.116), channel_id=1, source_target_pairs={{0,8},{8,0},{16,24},{24,16},{1,9},{9,1},{17,25},{25,17},{2,10},{10... | collective-permute-start | bytes 1081352 | tf_op jit(solution)/shard_map/ppermute | solution.py:76
  (80 other events, 594.2 us)
Sparse Core Ops, SparseCore 0:
  51.5 64.8 all-gather.4
  122.8 66.3 all-gather.8
  218.1 42.2 all-gather.6
  295.9 106.2 reduce-scatter.5
  404.3 35.9 reduce-scatter.7
  442.5 68.4 reduce-scatter.3

commit v3 on v2

--- a/solution.py
+++ b/solution.py
@@ -226,6 +226,61 @@
         out_specs=vmem,
         compiler_params=pltpu.CompilerParams(vmem_limit_bytes=32 * 1024 * 1024),
     )(order, values)
+
+
+def join_kernel(groups, order_ref, *refs):
+    *came_refs, out_ref = refs
+    count = len(came_refs)
+    unit = out_ref.shape[1] // (groups * count)
+    for k, came_ref in enumerate(came_refs):
+        for g in range(groups):
+            start = pl.multiple_of((g * count + order_ref[k]) * unit, unit)
+            out_ref[:, pl.ds(start, unit)] = came_ref[:, g * unit : (g + 1) * unit]
+
+
+def join_columns(came, groups, order, axes):
+    rows, held = came[0].shape
+    unit = held // groups
+    if unit % 128:
+        blocks = in_order(came, axes)
+        return jnp.concatenate(
+            [block[:, g * unit : (g + 1) * unit] for g in range(groups) for block in blocks], axis=1
+        )
+    vmem = pl.BlockSpec(memory_space=pltpu.VMEM)
+    return pl.pallas_call(
+        functools.partial(join_kernel, groups),
+        out_shape=jax.ShapeDtypeStruct((rows, held * len(came)), came[0].dtype),
+        in_specs=[pl.BlockSpec(memory_space=pltpu.SMEM)] + [vmem] * len(came),
+        out_specs=vmem,
+        compiler_params=pltpu.CompilerParams(vmem_limit_bytes=32 * 1024 * 1024),
+    )(order, *came)
+
+
+def turn_kernel(groups, outer, inner, values_ref, out_ref):
+    unit = out_ref.shape[1] // (groups * outer * inner)
+    for g in range(groups):
+        for i in range(outer):
+            for j in range(inner):
+                old, new = (g * outer + i) * inner + j, (g * inner + j) * outer + i
+                out_ref[:, new * unit : (new + 1) * unit] = values_ref[
+                    :, old * unit : (old + 1) * unit
+                ].astype(out_ref.dtype)
+
+
+def turn_columns(values, groups, outer, inner, dtype):
+    rows, width = values.shape
+    unit = width // (groups * outer * inner)
+    if unit % 64:
+        values = values.astype(dtype).reshape(rows, groups, outer, inner, unit)
+        return values.transpose(0, 1, 3, 2, 4).reshape(rows, width)
+    vmem = pl.BlockSpec(memory_space=pltpu.VMEM)
+    return pl.pallas_call(
+        functools.partial(turn_kernel, groups, outer, inner),
+        out_shape=jax.ShapeDtypeStruct((rows, width), dtype),
+        in_specs=[vmem],
+        out_specs=vmem,
+        compiler_params=pltpu.CompilerParams(vmem_limit_bytes=32 * 1024 * 1024),
+    )(values)
 
 
 TILE = 8
@@ -368,13 +423,6 @@
     )
     row_weight = jnp.sum(pick * seq_scale[None, :], axis=1)
 
-    def feature_swap(values, outer, inner):
-        count = values.shape[0]
-        return (
-            values.reshape(count, line, outer, inner, rows)
-            .transpose(0, 1, 3, 2, 4)
-            .reshape(count, width)
-        )
 
     line_order = jnp.arange(line, dtype=jnp.int32) ^ level
     glu_came = send_each(split_columns(glu_w, 2, line_order), LINE)
@@ -404,12 +452,12 @@
 
     scale_one = lax.rsqrt(jnp.mean(inputs_f * inputs_f, axis=1, keepdims=True) + NORM_EPS)
     unit_one = inputs_f * scale_one
-    normed = feature_swap((unit_one * gain_f[0]).astype(bf16), plane, cores)
+    normed = turn_columns(unit_one * gain_f[0], line, plane, cores, bf16)
     normed = gather_tokens(normed, PLANE)
     proj = contract(normed, in_b, 1, 0)
 
     glu_held, proj = together(glu_held, proj)
-    glu_rows = lax.all_gather(glu_held, GLU_OWNERS, axis=0, tiled=False)
+    glu_b = lax.all_gather(glu_held, GLU_OWNERS, axis=0, tiled=True)
     out_pair = core_pair(out_w.astype(bf16))
     out_blocks = gather_near(out_pair, LINE)
     proj, out_blocks = together(proj, out_blocks)
@@ -438,14 +486,9 @@
 
     scale_two = lax.rsqrt(jnp.mean(resid * resid, axis=1, keepdims=True) + NORM_EPS)
     unit_two = resid * scale_two
-    second_own = (unit_two * gain_f[2]).astype(bf16)
-    second_own, down_own, glu_rows = together(second_own, down_w.astype(bf16), glu_rows)
+    second_own = turn_columns(unit_two * gain_f[2], 1, line, plane * cores, bf16)
+    second_own, down_own, glu_b = together(second_own, down_w.astype(bf16), glu_b)
     down_b = lax.all_gather(down_own, GLU_OWNERS, axis=0, tiled=True)
-    glu_b = (
-        glu_rows.reshape(plane * cores, line, rows, 2 * hidden_width)
-        .transpose(1, 0, 2, 3)
-        .reshape(width, 2 * hidden_width)
-    )
     second, glu_b = together(gather_near(second_own, LINE), glu_b)
     second = jnp.concatenate(gather_far(second, LINE), axis=0)
     second, grad_output_b = together(second, grad_output_b)
@@ -462,16 +505,12 @@
     ).astype(bf16)
     second_part = contract(grad_paired, glu_b, 1, 1)
     grad_second = scatter_tokens(second_part, LINE)
-    owned = (
-        second
-        .reshape(line * tok, line, plane * cores, rows)
-        .transpose(0, 2, 1, 3)
-        .reshape(line * tok, width)
-    )
-    glu_part = contract(owned, grad_paired, 0, 0).astype(bf16)
+    grad_second = turn_columns(grad_second, 1, plane * cores, line, f32)
+    glu_part = contract(second, grad_paired, 0, 0).astype(bf16)
     glu_held = lax.psum_scatter(glu_part, GLU_OWNERS, scatter_dimension=0, tiled=True)
     down_part = contract(hidden, grad_output_b, 0, 0).astype(bf16)
     down_sums = core_sums(down_part, PLANE)
+    grad_second, down_sums = together(grad_second, down_sums)
     grad_gain_two = jnp.sum(grad_second * unit_two, axis=0)
     weighted_two = grad_second * gain_f[2]
     grad_resid = grad_output + scale_two * (
@@ -528,9 +567,8 @@
     in_part = contract(normed, grad_proj, 0, 0).astype(bf16)
     in_held = lax.psum_scatter(in_part, MIXER_OWNERS, scatter_dimension=0, tiled=True)
     down_grad = rank_sums(down_sums, PLANE)
-    grad_normed = feature_swap(
-        scatter_tokens(contract(grad_proj, in_b, 1, 1), PLANE), cores, plane
-    )
+    grad_normed = scatter_tokens(contract(grad_proj, in_b, 1, 1), PLANE)
+    grad_normed = turn_columns(grad_normed, line, cores, plane, f32)
     grad_gain_one = jnp.sum(grad_normed * unit_one, axis=0)
     weighted_one = grad_normed * gain_f[0]
     grad_block = grad_resid + scale_one * (
@@ -549,26 +587,16 @@
     glu_came = send_each(glu_sent, LINE)
     squares = jnp.broadcast_to(early_squares + squared(in_held), (1, width))
     totals = total_small(
-        jnp.concatenate([gain_part, squares], axis=0), (CORE, PLANE, LINE)
-    )
-    glu_blocks = in_order(glu_came, LINE)
-    glu_grad = jnp.concatenate(
-        [glu_blocks[q, :, :hidden_width] for q in range(line)]
-        + [glu_blocks[q, :, hidden_width:] for q in range(line)],
-        axis=1,
+        jnp.concatenate([gain_part, squares], axis=0), (LINE, PLANE, CORE)
     )
     in_blocks = in_held.reshape(plane, rows, 3 * channels)
-    in_came = send_each(rank_blocks(in_blocks, PLANE), PLANE)
-    in_grad = (
-        in_order(in_came, PLANE)
-        .reshape(plane, rows, 3, line, chan)
-        .transpose(1, 2, 3, 0, 4)
-        .reshape(in_w.shape)
+    in_grad = join_columns(
+        send_each(rank_blocks(in_blocks, PLANE), PLANE), 3 * line, order, PLANE
     )
     gain_total = totals[:3]
     squares = totals[3, 0] + squared(gain_total)
-    in_grad, glu_grad, squares = lax.optimization_barrier((in_grad, glu_grad, squares))
-    in_grad, glu_grad, out_grad = (v.astype(f32) for v in (in_grad, glu_grad, out_grad))
+    in_grad, squares = together(in_grad, squares)
+    in_grad, out_grad = in_grad.astype(f32), out_grad.astype(f32)
     columns = gains.shape[1]
     gain_grad = lax.dynamic_slice_in_dim(
         gain_total, (device * cores + lax.axis_index(CORE)) * columns, columns, 1
@@ -577,8 +605,10 @@
     factor = jnp.minimum(1.0, CLIP_LIMIT / (grad_norm + 1e-06))
     in_res = adam_step(in_w, in_m, in_v, in_grad, factor, MATRIX_RATE, MATRIX_DECAY)
     out_res = adam_step(out_w, out_m, out_v, out_grad, factor, MATRIX_RATE, MATRIX_DECAY)
+    down_res = adam_step(down_w, down_m, down_v, down_grad, factor, MATRIX_RATE, MATRIX_DECAY)
+    glu_came, in_res, out_res, down_res = together(glu_came, in_res, out_res, down_res)
+    glu_grad = join_columns(glu_came, 2, line_order, LINE).astype(f32)
     glu_res = adam_step(glu_w, glu_m, glu_v, glu_grad, factor, MATRIX_RATE, MATRIX_DECAY)
-    down_res = adam_step(down_w, down_m, down_v, down_grad, factor, MATRIX_RATE, MATRIX_DECAY)
     gain_res = adam_step(gains, gain_m, gain_v, gain_grad, factor, GAIN_RATE, 0.0)
     return (
         block_out,

time: 618 us -> 581 us (0.940)
  the two profiles are of different devices: /device:TPU:0 before, /device:TPU:8 now
where the time goes in v3:
time: 581 us; the launch traced here: 572 us
  waiting for transfers between devices  278 us (48%)
  matrix products  83.6 us (14%)
  starting transfers between devices  81.7 us (14%)
  other arithmetic  57.8 us (10%)
  local copies, waits for them, and re-layouts  30.6 us (5%)
  between operations  28.7 us (5%)
  Pallas kernels  11.5 us (2%)
    ppermute x64, waiting for transfers between devices, swap(): return lax.ppermute(values, axis, [(i, i ^ bit) for i in range(size)])  254 us
    dot_general x12, matrix products, contract(): lax.dot_general(left_side, right_side, (((left_dim,), (right_dim,)), ((),...  83.6 us
    ppermute x64, starting transfers between devices, swap(): return lax.ppermute(values, axis, [(i, i ^ bit) for i in range(size)])  81 us
    all_gather x1, waiting for transfers between devices, on_device(): in_b = lax.all_gather(in_held, MIXER_OWNERS, axis=0, tiled=True)  20.6 us
    unnamed x160, local copies, waits for them, and re-layouts  17.8 us
    sub x5, other arithmetic, adam_step(): weight - rate * (first_hat / (jnp.sqrt(second_hat) + ADAM_EPS) + decay *...  15 us
  transfers between devices with their start and end apart: 70, of which 51 were waited for; matrix products, arithmetic and copies ran while one was open for 21% of the time, Pallas kernels for 2%

profile of v3, /device:TPU:8, one launch (start us, length us, event | category | flops | bytes accessed | tf_op | source)
XLA Modules:
  0.0 571.7 jit_solution(2926614344835505559)
XLA Ops:
  10.4 2.4 collective-permute-start.2
  19.4 3.0 collective-permute-done.1
  24.8 15.8 %collective-permute-done.5 = bf16[64,2816]{1,0:T(8,128)(2,1)S(1)} collective-permute-done((bf16[64,2816]{1,0:T(8,128)(2,1)S(1)}, bf16[64,2816]{1,0:T(8,128)(2,1)S(1)}, u32[]{:S(2)}, u32[]{:S(2)}) %collective-permute-start.5) | collective-permute-done | bytes 360480 | tf_op jit(solution)/shard_map/ppermute | solution.py:76
  40.7 5.7 collective-permute-done.4
  48.3 2.4 collective-permute-start.6
  52.4 3.1 collective-permute-start.7
  63.8 2.4 collective-permute-done.10
  67.0 2.5 collective-permute-start.13
  70.5 12.3 %collective-permute-done.13 = bf16[128,2048]{1,0:T(8,128)(2,1)S(1)} collective-permute-done((bf16[128,2048]{1,0:T(8,128)(2,1)S(1)}, bf16[128,2048]{1,0:T(8,128)(2,1)S(1)}, u32[]{:S(2)}, u32[]{:S(2)}) %collective-permute-start.13) | collective-permute-done | bytes 524320 | tf_op jit(solution)/shard_map/ppermute | solution.py:76
  82.8 8.4 %collective-permute-done.12 = bf16[128,2048]{1,0:T(8,128)(2,1)S(1)} collective-permute-done((bf16[128,2048]{1,0:T(8,128)(2,1)S(1)}, bf16[128,2048]{1,0:T(8,128)(2,1)S(1)}, u32[]{:S(2)}, u32[]{:S(2)}) %collective-permute-start.12) | collective-permute-done | bytes 524320 | tf_op jit(solution)/shard_map/ppermute | solution.py:76
  92.0 20.6 %all-gather.4.cloned.1.call-done = bf16[2048,1536]{1,0:T(8,128)(2,1)} async-done(((bf16[256,1536]{1,0:T(8,128)(2,1)}), bf16[2048,1536]{1,0:T(8,128)(2,1)}) %all-gather.4.cloned.1.call-update) | async-done | bytes 6291472 | tf_op jit(solution)/shard_map/all_gather | solution.py:451
  112.7 6.1 %fusion.43.proj_ref = f32[512,1536]{1,0:T(8,128)S(1)} fusion(bf16[2048,1536]{1,0:T(8,128)(2,1)} %all-gather.4.cloned.1.call-done, bf16[128,2048]{1,0:T(8,128)(2,1)} %copy-done.67, bf16[128,2048]{1,0:T(8,128)(2,1)} %copy-done.69, bf16[128,2048]{1,0:T(8,128)(2,1)} %collective-permute-done.11, bf16[128,2048]{1,0:T(8,128)(2,1)} %copy-done.7), kind=kOutput, calls=%fused_computation.129 | convolution fusion | flops 3229614080 | bytes 11534336 | tf_op jit(solution)/shard_map/dot_general | solution.py:30
  123.7 2.8 collective-permute-start.15
  127.8 21.2 %collective-permute-done.15 = bf16[2,64,2048]{2,1,0:T(8,128)(2,1)S(1)} collective-permute-done((bf16[2,64,2048]{2,1,0:T(8,128)(2,1)S(1)}, bf16[2,64,2048]{2,1,0:T(8,128)(2,1)S(1)}, u32[]{:S(2)}, u32[]{:S(2)}) %collective-permute-start.15) | collective-permute-done | bytes 524320 | tf_op jit(solution)/shard_map/ppermute | solution.py:76
  151.1 3.3 shard_map.334
  160.3 2.7 collective-permute-start.18
  165.8 6.6 %collective-permute-done.18 = f32[4,2,512]{2,1,0:T(2,128)S(1)} collective-permute-done((f32[4,2,512]{2,1,0:T(2,128)S(1)}, f32[4,2,512]{2,1,0:T(2,128)S(1)}, u32[]{:S(2)}, u32[]{:S(2)}) %collective-permute-start.18) | collective-permute-done | bytes 16416 | tf_op jit(solution)/shard_map/ppermute | solution.py:76
  182.1 3.2 fusion.93
  193.0 8.7 %collective-permute-done.24 = bf16[128,2048]{1,0:T(8,128)(2,1)} collective-permute-done((bf16[128,2048]{1,0:T(8,128)(2,1)}, bf16[128,2048]{1,0:T(8,128)(2,1)}, u32[]{:S(2)}, u32[]{:S(2)}) %collective-permute-start.24) | collective-permute-done | bytes 524320 | tf_op jit(solution)/shard_map/ppermute | solution.py:76
  201.7 7.7 %collective-permute-done.23 = bf16[128,2048]{1,0:T(8,128)(2,1)} collective-permute-done((bf16[128,2048]{1,0:T(8,128)(2,1)}, bf16[128,2048]{1,0:T(8,128)(2,1)}, u32[]{:S(2)}, u32[]{:S(2)}) %collective-permute-start.23) | collective-permute-done | bytes 524320 | tf_op jit(solution)/shard_map/ppermute | solution.py:76
  214.9 2.8 collective-permute-start.27
  218.1 16.9 %collective-permute-done.27 = bf16[128,2048]{1,0:T(8,128)(2,1)S(1)} collective-permute-done((bf16[128,2048]{1,0:T(8,128)(2,1)}, bf16[128,2048]{1,0:T(8,128)(2,1)S(1)}, u32[]{:S(2)}, u32[]{:S(2)}) %collective-permute-start.27) | collective-permute-done | bytes 524320 | tf_op jit(solution)/shard_map/ppermute | solution.py:76
  234.9 4.1 collective-permute-done.28
  239.4 10.6 %collective-permute-done.29 = bf16[128,2048]{1,0:T(8,128)(2,1)S(1)} collective-permute-done((bf16[128,2048]{1,0:T(8,128)(2,1)S(1)}, bf16[128,2048]{1,0:T(8,128)(2,1)S(1)}, u32[]{:S(2)}, u32[]{:S(2)}) %collective-permute-start.29) | collective-permute-done | bytes 524320 | tf_op jit(solution)/shard_map/ppermute | solution.py:76
  251.4 11.9 %fusion.97 = f32[512,2816]{1,0:T(8,128)} fusion(bf16[512,2048]{1,0:T(8,128)(2,1)S(1)} %pad_maximum_fusion.4, bf16[2048,2816]{1,0:T(8,128)(2,1)} %all-gather.6.cloned.1.call-done), kind=kOutput, calls=%fused_computation.262 | convolution fusion | flops 5905580032 | bytes 19398656 | tf_op jit(solution)/shard_map/dot_general | solution.py:30
  266.7 10.5 %multiply_convert_fusion.2 = (bf16[512,1408]{1,0:T(8,128)(2,1)S(1)}, bf16[512,1408]{1,0:T(8,128)(2,1)S(1)}, bf16[512,1408]{1,0:T(8,128)(2,1)}) fusion(f32[512,2816]{1,0:T(8,128)} %fusion.97, bf16[512,2048]{1,0:T(8,128)(2,1)} %constant_dynamic-update-slice_fusion.13, bf16[1408,2048]{1,0:T(8,128)(2,1)} %all-gather.8.cloned.1.call-done), kind=kOutput, calls=%fused_computation.16 | convolution fusion | flops 2963603456 | bytes 17956864 | tf_op jit(solution)/shard_map/dot_general | solution.py:30
  278.7 8.9 %convolution_convert_fusion = bf16[2048,2816]{1,0:T(8,128)(2,1)} fusion(bf16[512,2048]{1,0:T(8,128)(2,1)S(1)} %copy-done.38, bf16[512,1408]{1,0:T(8,128)(2,1)S(1)} %get-tuple-element.182, bf16[512,1408]{1,0:T(8,128)(2,1)S(1)} %get-tuple-element.181), kind=kOutput, calls=%fused_computation | convolution fusion | flops 5917114368 | bytes 16515072 | tf_op jit(solution)/shard_map/dot_general | solution.py:30
  287.8 5.2 convolution_convert_fusion.2
  293.4 12.2 %fusion.94 = (bf16[512,2048]{1,0:T(8,128)(2,1)}, f32[512,2048]{1,0:T(8,128)S(1)}) fusion(bf16[2048,2816]{1,0:T(8,128)(2,1)} %all-gather.6.cloned.1.call-done, bf16[512,1408]{1,0:T(8,128)(2,1)} %copy-done.75, bf16[512,1408]{1,0:T(8,128)(2,1)} %copy-done.74), kind=kOutput, calls=%fused_computation.259 | convolution fusion | flops 5912395776 | bytes 20709376 | tf_op jit(solution)/shard_map/dot_general | solution.py:30
  309.4 12.8 %collective-permute-done.31 = bf16[128,2048]{1,0:T(8,128)(2,1)S(1)} collective-permute-done((bf16[128,2048]{1,0:T(8,128)(2,1)S(1)}, bf16[128,2048]{1,0:T(8,128)(2,1)S(1)}, u32[]{:S(2)}, u32[]{:S(2)}) %collective-permute-start.31) | collective-permute-done | bytes 524320 | tf_op jit(solution)/shard_map/ppermute | solution.py:76
  324.4 16.0 %collective-permute-done.33 = bf16[128,2048]{1,0:T(8,128)(2,1)S(1)} collective-permute-done((bf16[128,2048]{1,0:T(8,128)(2,1)S(1)}, bf16[128,2048]{1,0:T(8,128)(2,1)S(1)}, u32[]{:S(2)}, u32[]{:S(2)}) %collective-permute-start.33) | collective-permute-done | bytes 524320 | tf_op jit(solution)/shard_map/ppermute | solution.py:76
  340.4 4.6 collective-permute-done.32
  345.7 2.9 fusion
  350.3 3.4 fusion.95
  354.8 4.0 collective-permute-start.38
  363.6 8.0 %collective-permute-done.38 = bf16[128,2048]{1,0:T(8,128)(2,1)S(1)} collective-permute-done((bf16[128,2048]{1,0:T(8,128)(2,1)S(1)}, bf16[128,2048]{1,0:T(8,128)(2,1)S(1)}, u32[]{:S(2)}, u32[]{:S(2)}) %collective-permute-start.38) | collective-permute-done | bytes 524320 | tf_op jit(solution)/shard_map/ppermute | solution.py:76
  372.5 6.7 %collective-permute-start.39 = (bf16[128,2048]{1,0:T(8,128)(2,1)}, bf16[128,2048]{1,0:T(8,128)(2,1)}, u32[]{:S(2)}, u32[]{:S(2)}) collective-permute-start(bf16[128,2048]{1,0:T(8,128)(2,1)} %fusion.20), channel_id=1, source_target_pairs={{0,16},{8,24},{16,0},{24,8},{1,17},{9,25},{17,1},{25,9},{2,18},{10... | collective-permute-start | bytes 1572872 | tf_op jit(solution)/shard_map/ppermute | solution.py:76
  386.9 9.5 %collective-permute-done.36 = bf16[128,2048]{1,0:T(8,128)(2,1)} collective-permute-done((bf16[128,2048]{1,0:T(8,128)(2,1)}, bf16[128,2048]{1,0:T(8,128)(2,1)}, u32[]{:S(2)}, u32[]{:S(2)}) %collective-permute-start.36) | collective-permute-done | bytes 524320 | tf_op jit(solution)/shard_map/ppermute | solution.py:76
  396.4 2.5 collective-permute-done.35
  400.8 3.4 fusion.42
  404.1 2.6 convolution_convert_fusion.3
  406.8 4.2 multiply_reduce_fusion.4
  411.2 3.5 collective-permute-done.41
  416.1 2.2 collective-permute-done.42
  419.1 3.4 shard_map.337
  423.2 3.4 collective-permute-done.43
  426.7 4.5 collective-permute-done.44
  433.4 7.1 %convolution_convert_fusion.1 = bf16[2048,1536]{1,0:T(8,128)(2,1)} fusion(bf16[512,512]{1,0:T(8,128)(2,1)S(1)} %get-tuple-element.187, bf16[512,512]{1,0:T(8,128)(2,1)S(1)} %get-tuple-element.185, bf16[512,512]{1,0:T(8,128)(2,1)S(1)} %get-tuple-element.184, bf16[128,2048]{1,0:T(8,128)(2,1)S(1)} %copy-done.68, bf16[128,2048]{1,0:T(8,128)(2,1)S(1)} %copy-done.70, ...), kind=kOutput, calls=%fused_computation.1 | convolution fusion | flops 3237478400 | bytes 9961472 | tf_op jit(solution)/shard_map/dot_general | solution.py:30
  446.0 8.1 %fusion.96 = (bf16[512,2048]{1,0:T(8,128)(2,1)S(1)}, f32[512,2048]{1,0:T(8,128)}) fusion(bf16[2048,1536]{1,0:T(8,128)(2,1)} %all-gather.4.cloned.1.call-done, bf16[512,512]{1,0:T(8,128)(2,1)S(1)} %copy-done.49, bf16[512,512]{1,0:T(8,128)(2,1)S(1)} %copy-done.53, bf16[512,512]{1,0:T(8,128)(2,1)S(1)} %copy-done.51), kind=kOutput, calls=%fused_computation.261 | convolution fusion | flops 3226992640 | bytes 14155776 | tf_op jit(solution)/shard_map/dot_general | solution.py:30
  457.0 5.5 collective-permute-done.50
  464.0 8.8 %collective-permute-done.49 = bf16[176,2048]{1,0:T(8,128)(2,1)S(1)} collective-permute-done((bf16[176,2048]{1,0:T(8,128)(2,1)S(1)}, bf16[176,2048]{1,0:T(8,128)(2,1)S(1)}, u32[]{:S(2)}, u32[]{:S(2)}) %collective-permute-start.49) | collective-permute-done | bytes 720928 | tf_op jit(solution)/shard_map/ppermute | solution.py:76
  472.8 5.0 collective-permute-done.48
  477.8 2.2 multiply_reduce_fusion.2
  480.2 8.8 %collective-permute-done.47 = bf16[128,2048]{1,0:T(8,128)(2,1)S(1)} collective-permute-done((bf16[128,2048]{1,0:T(8,128)(2,1)}, bf16[128,2048]{1,0:T(8,128)(2,1)S(1)}, u32[]{:S(2)}, u32[]{:S(2)}) %collective-permute-start.47) | collective-permute-done | bytes 524320 | tf_op jit(solution)/shard_map/ppermute | solution.py:76
  489.0 6.3 %collective-permute-done.45 = bf16[128,2048]{1,0:T(8,128)(2,1)} collective-permute-done((bf16[128,2048]{1,0:T(8,128)(2,1)}, bf16[128,2048]{1,0:T(8,128)(2,1)}, u32[]{:S(2)}, u32[]{:S(2)}) %collective-permute-start.45) | collective-permute-done | bytes 524320 | tf_op jit(solution)/shard_map/ppermute | solution.py:76
  505.7 3.4 reduce-scatter.4.cloned.1.call-done
  509.1 2.3 multiply_reduce_fusion.1
  512.1 2.8 collective-permute-start.58
  514.9 2.1 collective-permute-start.59
  517.1 2.8 collective-permute-done.59
  538.6 3.9 collective-permute-done.56.refs_3_
  545.9 5.0 multiply_subtract_fusion.1
  551.0 2.9 multiply_subtract_fusion.2
  558.2 5.1 multiply_subtract_fusion
  (399 shorter events, 139.0 us)
Async XLA Ops:
  7.2 105.5 %all-gather.4.cloned.1.call-start = ((), (), s32[]{:S(2)}) async-start(), calls=%async_computation.3 | async-start | bytes 7077888 | tf_op jit(solution)/shard_map/all_gather | solution.py:451
  10.4 9.0 %collective-permute-start.2 = (bf16[64,1536]{1,0:T(8,128)(2,1)}, bf16[64,1536]{1,0:T(8,128)(2,1)}, u32[]{:S(2)}, u32[]{:S(2)}) collective-permute-start(bf16[64,1536]{1,0:T(8,128)(2,1)} %get-tuple-element.226), channel_id=1, source_target_pairs={{0,6},{2,4},{4,2},{6,0},{1,7},{3,5},{5,3},{7,1},{8,14},{10,12},{12... | collective-permute-start | bytes 589832 | tf_op jit(solution)/shard_map/ppermute | solution.py:76
  12.9 9.6 %collective-permute-start.1 = (bf16[64,1536]{1,0:T(8,128)(2,1)}, bf16[64,1536]{1,0:T(8,128)(2,1)}, u32[]{:S(2)}, u32[]{:S(2)}) collective-permute-start(bf16[64,1536]{1,0:T(8,128)(2,1)} %get-tuple-element.227), channel_id=1, source_target_pairs={{0,4},{2,6},{4,0},{6,2},{1,5},{3,7},{5,1},{7,3},{8,12},{10,14},{12... | collective-permute-start | bytes 589832 | tf_op jit(solution)/shard_map/ppermute | solution.py:76
  13.4 9.2 %collective-permute-start = (bf16[64,1536]{1,0:T(8,128)(2,1)}, bf16[64,1536]{1,0:T(8,128)(2,1)}, u32[]{:S(2)}, u32[]{:S(2)}) collective-permute-start(bf16[64,1536]{1,0:T(8,128)(2,1)} %get-tuple-element.228), channel_id=1, source_target_pairs={{0,2},{2,0},{4,6},{6,4},{1,3},{3,1},{5,7},{7,5},{8,10},{10,8},{12,... | collective-permute-start | bytes 589832 | tf_op jit(solution)/shard_map/ppermute | solution.py:76
  14.7 26.0 %collective-permute-start.5 = (bf16[64,2816]{1,0:T(8,128)(2,1)S(1)}, bf16[64,2816]{1,0:T(8,128)(2,1)S(1)}, u32[]{:S(2)}, u32[]{:S(2)}) collective-permute-start(bf16[64,2816]{1,0:T(8,128)(2,1)S(1)} %get-tuple-element.214), channel_id=1, source_target_pairs={{0,24},{8,16},{16,8},{24,0},{1,25},{9,17},{17,9},{25,1},{2,26},{10... | collective-permute-start | bytes 1081352 | tf_op jit(solution)/shard_map/ppermute | solution.py:76
  16.4 30.0 %collective-permute-start.4 = (bf16[64,2816]{1,0:T(8,128)(2,1)S(1)}, bf16[64,2816]{1,0:T(8,128)(2,1)S(1)}, u32[]{:S(2)}, u32[]{:S(2)}) collective-permute-start(bf16[64,2816]{1,0:T(8,128)(2,1)S(1)} %get-tuple-element.215), channel_id=1, source_target_pairs={{0,16},{8,24},{16,0},{24,8},{1,17},{9,25},{17,1},{25,9},{2,18},{10... | collective-permute-start | bytes 1081352 | tf_op jit(solution)/shard_map/ppermute | solution.py:76
  19.4 26.9 %collective-permute-start.3 = (bf16[64,2816]{1,0:T(8,128)(2,1)S(1)}, bf16[64,2816]{1,0:T(8,128)(2,1)S(1)}, u32[]{:S(2)}, u32[]{:S(2)}) collective-permute-start(bf16[64,2816]{1,0:T(8,128)(2,1)S(1)} %get-tuple-element.216), channel_id=1, source_target_pairs={{0,8},{8,0},{16,24},{24,16},{1,9},{9,1},{17,25},{25,17},{2,10},{10... | collective-permute-start | bytes 1081352 | tf_op jit(solution)/shard_map/ppermute | solution.py:76
  48.0 166.4 %all-gather.6.cloned.1.call-start = ((), (), s32[]{:S(2)}) async-start(), calls=%async_computation.4 | async-start | bytes 12976128 | tf_op jit(solution)/shard_map/all_gather | solution.py:460
  48.3 4.0 collective-permute-start.6
  52.4 4.7 collective-permute-start.7
  58.3 3.8 collective-permute-start.9
  62.2 4.0 collective-permute-start.10
  67.0 15.9 %collective-permute-start.13 = (bf16[128,2048]{1,0:T(8,128)(2,1)S(1)}, bf16[128,2048]{1,0:T(8,128)(2,1)S(1)}, u32[]{:S(2)}, u32[]{:S(2)}) collective-permute-start(bf16[128,2048]{1,0:T(8,128)(2,1)S(1)} %shard_map.333), channel_id=1, source_target_pairs={{0,6},{2,4},{4,2},{6,0},{1,7},{3,5},{5,3},{7,1},{8,14},{10,12},{12... | collective-permute-start | bytes 1572872 | tf_op jit(solution)/shard_map/ppermute | solution.py:76
  69.5 21.7 %collective-permute-start.12 = (bf16[128,2048]{1,0:T(8,128)(2,1)S(1)}, bf16[128,2048]{1,0:T(8,128)(2,1)S(1)}, u32[]{:S(2)}, u32[]{:S(2)}) collective-permute-start(bf16[128,2048]{1,0:T(8,128)(2,1)S(1)} %shard_map.333), channel_id=1, source_target_pairs={{0,4},{2,6},{4,0},{6,2},{1,5},{3,7},{5,1},{7,3},{8,12},{10,14},{12... | collective-permute-start | bytes 1572872 | tf_op jit(solution)/shard_map/ppermute | solution.py:76
  70.0 22.0 %collective-permute-start.11 = (bf16[128,2048]{1,0:T(8,128)(2,1)S(1)}, bf16[128,2048]{1,0:T(8,128)(2,1)}, u32[]{:S(2)}, u32[]{:S(2)}) collective-permute-start(bf16[128,2048]{1,0:T(8,128)(2,1)S(1)} %shard_map.333), channel_id=1, source_target_pairs={{0,2},{2,0},{4,6},{6,4},{1,3},{3,1},{5,7},{7,5},{8,10},{10,8},{12,... | collective-permute-start | bytes 1572872 | tf_op jit(solution)/shard_map/ppermute | solution.py:76
  118.8 147.9 %all-gather.8.cloned.1.call-start = ((), (), s32[]{:S(2)}) async-start(), calls=%async_computation.5 | async-start | bytes 6488064 | tf_op jit(solution)/shard_map/all_gather | solution.py:491
  123.7 25.2 %collective-permute-start.15 = (bf16[2,64,2048]{2,1,0:T(8,128)(2,1)S(1)}, bf16[2,64,2048]{2,1,0:T(8,128)(2,1)S(1)}, u32[]{:S(2)}, u32[]{:S(2)}) collective-permute-start(bf16[2,64,2048]{2,1,0:T(8,128)(2,1)S(1)} %pad_maximum_fusion.16), channel_id=1, source_target_pairs={{0,8},{8,0},{16,24},{24,16},{1,9},{9,1},{17,25},{25,17},{2,10},{10... | collective-permute-start | bytes 1572872 | tf_op jit(solution)/shard_map/ppermute | solution.py:76
  126.6 24.6 %collective-permute-start.16 = (bf16[2,64,2048]{2,1,0:T(8,128)(2,1)S(1)}, bf16[2,64,2048]{2,1,0:T(8,128)(2,1)}, u32[]{:S(2)}, u32[]{:S(2)}) collective-permute-start(bf16[2,64,2048]{2,1,0:T(8,128)(2,1)S(1)} %pad_maximum_fusion.16), channel_id=1, source_target_pairs={{0,16},{8,24},{16,0},{24,8},{1,17},{9,25},{17,1},{25,9},{2,18},{10... | collective-permute-start | bytes 1572872 | tf_op jit(solution)/shard_map/ppermute | solution.py:76
  156.4 3.9 collective-permute-start.17
  158.4 14.0 %collective-permute-start.19 = (bf16[2,64,2048]{2,1,0:T(8,128)(2,1)}, bf16[2,64,2048]{2,1,0:T(8,128)(2,1)}, u32[]{:S(2)}, u32[]{:S(2)}) collective-permute-start(bf16[2,64,2048]{2,1,0:T(8,128)(2,1)} %collective-permute-done.16), channel_id=1, source_target_pairs={{0,8},{8,0},{16,24},{24,16},{1,9},{9,1},{17,25},{25,17},{2,10},{10... | collective-permute-start | bytes 1572872 | tf_op jit(solution)/shard_map/ppermute | solution.py:76
  160.3 12.0 %collective-permute-start.18 = (f32[4,2,512]{2,1,0:T(2,128)S(1)}, f32[4,2,512]{2,1,0:T(2,128)S(1)}, u32[]{:S(2)}, u32[]{:S(2)}) collective-permute-start(f32[4,2,512]{2,1,0:T(2,128)S(1)} %constant_dynamic-update-slice_fusion.6), channel_id=1, source_target_pairs={{0,16},{8,24},{16,0},{24,8},{1,17},{9,25},{17,1},{25,9},{2,18},{10... | collective-permute-start | bytes 49160 | tf_op jit(solution)/shard_map/ppermute | solution.py:76
  186.5 15.2 %collective-permute-start.24 = (bf16[128,2048]{1,0:T(8,128)(2,1)}, bf16[128,2048]{1,0:T(8,128)(2,1)}, u32[]{:S(2)}, u32[]{:S(2)}) collective-permute-start(bf16[128,2048]{1,0:T(8,128)(2,1)} %get-tuple-element.199), channel_id=1, source_target_pairs={{0,2},{2,0},{4,6},{6,4},{1,3},{3,1},{5,7},{7,5},{8,10},{10,8},{12,... | collective-permute-start | bytes 1572872 | tf_op jit(solution)/shard_map/ppermute | solution.py:76
  188.0 21.4 %collective-permute-start.23 = (bf16[128,2048]{1,0:T(8,128)(2,1)}, bf16[128,2048]{1,0:T(8,128)(2,1)}, u32[]{:S(2)}, u32[]{:S(2)}) collective-permute-start(bf16[128,2048]{1,0:T(8,128)(2,1)} %get-tuple-element.200), channel_id=1, source_target_pairs={{0,4},{2,6},{4,0},{6,2},{1,5},{3,7},{5,1},{7,3},{8,12},{10,14},{12... | collective-permute-start | bytes 1572872 | tf_op jit(solution)/shard_map/ppermute | solution.py:76
  189.4 20.0 %collective-permute-start.22 = (bf16[128,2048]{1,0:T(8,128)(2,1)}, bf16[128,2048]{1,0:T(8,128)(2,1)}, u32[]{:S(2)}, u32[]{:S(2)}) collective-permute-start(bf16[128,2048]{1,0:T(8,128)(2,1)} %get-tuple-element.198), channel_id=1, source_target_pairs={{0,6},{2,4},{4,2},{6,0},{1,7},{3,5},{5,3},{7,1},{8,14},{10,12},{12... | collective-permute-start | bytes 1572872 | tf_op jit(solution)/shard_map/ppermute | solution.py:76
  191.0 20.3 %collective-permute-start.25 = (bf16[128,2048]{1,0:T(8,128)(2,1)}, bf16[128,2048]{1,0:T(8,128)(2,1)S(1)}, u32[]{:S(2)}, u32[]{:S(2)}) collective-permute-start(bf16[128,2048]{1,0:T(8,128)(2,1)} %fusion.29), channel_id=1, source_target_pairs={{0,8},{8,0},{16,24},{24,16},{1,9},{9,1},{17,25},{25,17},{2,10},{10... | collective-permute-start | bytes 1572872 | tf_op jit(solution)/shard_map/ppermute | solution.py:76
  191.1 20.8 %collective-permute-start.26 = (bf16[128,2048]{1,0:T(8,128)(2,1)}, bf16[128,2048]{1,0:T(8,128)(2,1)S(1)}, u32[]{:S(2)}, u32[]{:S(2)}) collective-permute-start(bf16[128,2048]{1,0:T(8,128)(2,1)} %fusion.29), channel_id=1, source_target_pairs={{0,16},{8,24},{16,0},{24,8},{1,17},{9,25},{17,1},{25,9},{2,18},{10... | collective-permute-start | bytes 1572872 | tf_op jit(solution)/shard_map/ppermute | solution.py:76
  214.4 192.3 %reduce-scatter.6.cloned.1.call-start = ((), (), s32[]{:S(2)}) async-start(), calls=%async_computation.7 | async-start | bytes 12976128 | tf_op jit(solution)/shard_map/reduce_scatter | solution.py:510
  214.9 20.0 %collective-permute-start.27 = (bf16[128,2048]{1,0:T(8,128)(2,1)}, bf16[128,2048]{1,0:T(8,128)(2,1)S(1)}, u32[]{:S(2)}, u32[]{:S(2)}) collective-permute-start(bf16[128,2048]{1,0:T(8,128)(2,1)} %copy-done.4), channel_id=1, source_target_pairs={{0,8},{8,0},{16,24},{24,16},{1,9},{9,1},{17,25},{25,17},{2,10},{10... | collective-permute-start | bytes 1572872 | tf_op jit(solution)/shard_map/ppermute | solution.py:76
  217.7 21.4 %collective-permute-start.28 = (bf16[128,2048]{1,0:T(8,128)(2,1)}, bf16[128,2048]{1,0:T(8,128)(2,1)S(1)}, u32[]{:S(2)}, u32[]{:S(2)}) collective-permute-start(bf16[128,2048]{1,0:T(8,128)(2,1)} %copy-done.4), channel_id=1, source_target_pairs={{0,16},{8,24},{16,0},{24,8},{1,17},{9,25},{17,1},{25,9},{2,18},{10... | collective-permute-start | bytes 1572872 | tf_op jit(solution)/shard_map/ppermute | solution.py:76
  239.1 10.9 %collective-permute-start.29 = (bf16[128,2048]{1,0:T(8,128)(2,1)S(1)}, bf16[128,2048]{1,0:T(8,128)(2,1)S(1)}, u32[]{:S(2)}, u32[]{:S(2)}) collective-permute-start(bf16[128,2048]{1,0:T(8,128)(2,1)S(1)} %collective-permute-done.28), channel_id=1, source_target_pairs={{0,8},{8,0},{16,24},{24,16},{1,9},{9,1},{17,25},{25,17},{2,10},{10... | collective-permute-start | bytes 1572872 | tf_op jit(solution)/shard_map/ppermute | solution.py:76
  251.3 14.5 %collective-permute-start.30 = (bf16[128,2048]{1,0:T(8,128)(2,1)S(1)}, bf16[128,2048]{1,0:T(8,128)(2,1)S(1)}, u32[]{:S(2)}, u32[]{:S(2)}) collective-permute-start(bf16[128,2048]{1,0:T(8,128)(2,1)S(1)} %copy-done.57), channel_id=1, source_target_pairs={{0,8},{8,0},{16,24},{24,16},{1,9},{9,1},{17,25},{25,17},{2,10},{10... | collective-permute-start | bytes 1572872 | tf_op jit(solution)/shard_map/ppermute | solution.py:76
  287.7 215.7 %reduce-scatter.8.cloned.1.call-start = ((), (), s32[]{:S(2)}) async-start(), calls=%async_computation.8 | async-start | bytes 2359296 | tf_op jit(solution)/shard_map/reduce_scatter | solution.py:533
  293.4 52.3 %collective-permute-start.34 = (bf16[4,176,2048]{2,1,0:T(8,128)(2,1)S(1)}, bf16[4,176,2048]{2,1,0:T(8,128)(2,1)S(1)}, u32[]{:S(2)}, u32[]{:S(2)}) collective-permute-start(bf16[4,176,2048]{2,1,0:T(8,128)(2,1)S(1)} %dynamic-slice_bitcast_fusion), channel_id=1, source_target_pairs={{0,1},{1,0},{2,3},{3,2},{4,5},{5,4},{6,7},{7,6},{8,9},{9,8},{10,11... | collective-permute-start | bytes 8650760 | tf_op jit(solution)/shard_map/ppermute | solution.py:76
  307.3 14.8 %collective-permute-start.31 = (bf16[128,2048]{1,0:T(8,128)(2,1)S(1)}, bf16[128,2048]{1,0:T(8,128)(2,1)S(1)}, u32[]{:S(2)}, u32[]{:S(2)}) collective-permute-start(bf16[128,2048]{1,0:T(8,128)(2,1)S(1)} %get-tuple-element.196), channel_id=1, source_target_pairs={{0,8},{8,0},{16,24},{24,16},{1,9},{9,1},{17,25},{25,17},{2,10},{10... | collective-permute-start | bytes 1572872 | tf_op jit(solution)/shard_map/ppermute | solution.py:76
  308.6 31.8 %collective-permute-start.33 = (bf16[128,2048]{1,0:T(8,128)(2,1)S(1)}, bf16[128,2048]{1,0:T(8,128)(2,1)S(1)}, u32[]{:S(2)}, u32[]{:S(2)}) collective-permute-start(bf16[128,2048]{1,0:T(8,128)(2,1)S(1)} %get-tuple-element.197), channel_id=1, source_target_pairs={{0,8},{8,0},{16,24},{24,16},{1,9},{9,1},{17,25},{25,17},{2,10},{10... | collective-permute-start | bytes 1572872 | tf_op jit(solution)/shard_map/ppermute | solution.py:76
  322.3 22.8 %collective-permute-start.32 = (bf16[128,2048]{1,0:T(8,128)(2,1)S(1)}, bf16[128,2048]{1,0:T(8,128)(2,1)S(1)}, u32[]{:S(2)}, u32[]{:S(2)}) collective-permute-start(bf16[128,2048]{1,0:T(8,128)(2,1)S(1)} %fusion.24), channel_id=1, source_target_pairs={{0,16},{8,24},{16,0},{24,8},{1,17},{9,25},{17,1},{25,9},{2,18},{10... | collective-permute-start | bytes 1572872 | tf_op jit(solution)/shard_map/ppermute | solution.py:76
  354.8 16.9 %collective-permute-start.38 = (bf16[128,2048]{1,0:T(8,128)(2,1)S(1)}, bf16[128,2048]{1,0:T(8,128)(2,1)S(1)}, u32[]{:S(2)}, u32[]{:S(2)}) collective-permute-start(bf16[128,2048]{1,0:T(8,128)(2,1)S(1)} %get-tuple-element.194), channel_id=1, source_target_pairs={{0,8},{8,0},{16,24},{24,16},{1,9},{9,1},{17,25},{25,17},{2,10},{10... | collective-permute-start | bytes 1572872 | tf_op jit(solution)/shard_map/ppermute | solution.py:76
  359.6 27.2 %collective-permute-start.37 = (bf16[128,2048]{1,0:T(8,128)(2,1)}, bf16[128,2048]{1,0:T(8,128)(2,1)}, u32[]{:S(2)}, u32[]{:S(2)}) collective-permute-start(bf16[128,2048]{1,0:T(8,128)(2,1)} %convert_element_type.169), channel_id=1, source_target_pairs={{0,6},{2,4},{4,2},{6,0},{1,7},{3,5},{5,3},{7,1},{8,14},{10,12},{12... | collective-permute-start | bytes 1572872 | tf_op jit(solution)/shard_map/ppermute | solution.py:76
  361.0 35.4 %collective-permute-start.36 = (bf16[128,2048]{1,0:T(8,128)(2,1)}, bf16[128,2048]{1,0:T(8,128)(2,1)}, u32[]{:S(2)}, u32[]{:S(2)}) collective-permute-start(bf16[128,2048]{1,0:T(8,128)(2,1)} %convert_element_type.169), channel_id=1, source_target_pairs={{0,4},{2,6},{4,0},{6,2},{1,5},{3,7},{5,1},{7,3},{8,12},{10,14},{12... | collective-permute-start | bytes 1572872 | tf_op jit(solution)/shard_map/ppermute | solution.py:76
  362.1 36.9 %collective-permute-start.35 = (bf16[128,2048]{1,0:T(8,128)(2,1)}, bf16[128,2048]{1,0:T(8,128)(2,1)}, u32[]{:S(2)}, u32[]{:S(2)}) collective-permute-start(bf16[128,2048]{1,0:T(8,128)(2,1)} %convert_element_type.169), channel_id=1, source_target_pairs={{0,2},{2,0},{4,6},{6,4},{1,3},{3,1},{5,7},{7,5},{8,10},{10,8},{12,... | collective-permute-start | bytes 1572872 | tf_op jit(solution)/shard_map/ppermute | solution.py:76
  363.1 37.6 %collective-permute-start.40 = (bf16[128,2048]{1,0:T(8,128)(2,1)}, bf16[128,2048]{1,0:T(8,128)(2,1)}, u32[]{:S(2)}, u32[]{:S(2)}) collective-permute-start(bf16[128,2048]{1,0:T(8,128)(2,1)} %get-tuple-element.195), channel_id=1, source_target_pairs={{0,8},{8,0},{16,24},{24,16},{1,9},{9,1},{17,25},{25,17},{2,10},{10... | collective-permute-start | bytes 1572872 | tf_op jit(solution)/shard_map/ppermute | solution.py:76
  372.5 28.2 %collective-permute-start.39 = (bf16[128,2048]{1,0:T(8,128)(2,1)}, bf16[128,2048]{1,0:T(8,128)(2,1)}, u32[]{:S(2)}, u32[]{:S(2)}) collective-permute-start(bf16[128,2048]{1,0:T(8,128)(2,1)} %fusion.20), channel_id=1, source_target_pairs={{0,16},{8,24},{16,0},{24,8},{1,17},{9,25},{17,1},{25,9},{2,18},{10... | collective-permute-start | bytes 1572872 | tf_op jit(solution)/shard_map/ppermute | solution.py:76
  406.7 102.4 %reduce-scatter.4.cloned.1.call-start = ((), (), s32[]{:S(2)}) async-start(), calls=%async_computation.6 | async-start | bytes 7077888 | tf_op jit(solution)/shard_map/reduce_scatter | solution.py:568
  422.6 4.0 collective-permute-start.43
  426.6 4.7 collective-permute-start.44
  442.5 20.0 %collective-permute-start.50 = (bf16[176,2048]{1,0:T(8,128)(2,1)S(1)}, bf16[176,2048]{1,0:T(8,128)(2,1)S(1)}, u32[]{:S(2)}, u32[]{:S(2)}) collective-permute-start(bf16[176,2048]{1,0:T(8,128)(2,1)S(1)} %get-tuple-element.189), channel_id=1, source_target_pairs={{0,6},{2,4},{4,2},{6,0},{1,7},{3,5},{5,3},{7,1},{8,14},{10,12},{12... | collective-permute-start | bytes 2162696 | tf_op jit(solution)/shard_map/ppermute | solution.py:76
  444.0 28.8 %collective-permute-start.49 = (bf16[176,2048]{1,0:T(8,128)(2,1)S(1)}, bf16[176,2048]{1,0:T(8,128)(2,1)S(1)}, u32[]{:S(2)}, u32[]{:S(2)}) collective-permute-start(bf16[176,2048]{1,0:T(8,128)(2,1)S(1)} %get-tuple-element.190), channel_id=1, source_target_pairs={{0,4},{2,6},{4,0},{6,2},{1,5},{3,7},{5,1},{7,3},{8,12},{10,14},{12... | collective-permute-start | bytes 2162696 | tf_op jit(solution)/shard_map/ppermute | solution.py:76
  444.1 33.7 %collective-permute-start.48 = (bf16[176,2048]{1,0:T(8,128)(2,1)S(1)}, bf16[176,2048]{1,0:T(8,128)(2,1)S(1)}, u32[]{:S(2)}, u32[]{:S(2)}) collective-permute-start(bf16[176,2048]{1,0:T(8,128)(2,1)S(1)} %get-tuple-element.188), channel_id=1, source_target_pairs={{0,2},{2,0},{4,6},{6,4},{1,3},{3,1},{5,7},{7,5},{8,10},{10,8},{12,... | collective-permute-start | bytes 2162696 | tf_op jit(solution)/shard_map/ppermute | solution.py:76
  455.3 33.7 %collective-permute-start.47 = (bf16[128,2048]{1,0:T(8,128)(2,1)}, bf16[128,2048]{1,0:T(8,128)(2,1)S(1)}, u32[]{:S(2)}, u32[]{:S(2)}) collective-permute-start(bf16[128,2048]{1,0:T(8,128)(2,1)} %get-tuple-element.192), channel_id=1, source_target_pairs={{0,2},{2,0},{4,6},{6,4},{1,3},{3,1},{5,7},{7,5},{8,10},{10,8},{12,... | collective-permute-start | bytes 1572872 | tf_op jit(solution)/shard_map/ppermute | solution.py:76
  455.3 33.7 %collective-permute-start.46 = (bf16[128,2048]{1,0:T(8,128)(2,1)}, bf16[128,2048]{1,0:T(8,128)(2,1)}, u32[]{:S(2)}, u32[]{:S(2)}) collective-permute-start(bf16[128,2048]{1,0:T(8,128)(2,1)} %get-tuple-element.193), channel_id=1, source_target_pairs={{0,4},{2,6},{4,0},{6,2},{1,5},{3,7},{5,1},{7,3},{8,12},{10,14},{12... | collective-permute-start | bytes 1572872 | tf_op jit(solution)/shard_map/ppermute | solution.py:76
  462.5 32.8 %collective-permute-start.45 = (bf16[128,2048]{1,0:T(8,128)(2,1)}, bf16[128,2048]{1,0:T(8,128)(2,1)}, u32[]{:S(2)}, u32[]{:S(2)}) collective-permute-start(bf16[128,2048]{1,0:T(8,128)(2,1)} %get-tuple-element.191), channel_id=1, source_target_pairs={{0,6},{2,4},{4,2},{6,0},{1,7},{3,5},{5,3},{7,1},{8,14},{10,12},{12... | collective-permute-start | bytes 1572872 | tf_op jit(solution)/shard_map/ppermute | solution.py:76
  512.1 5.1 collective-permute-start.58
  514.9 5.1 collective-permute-start.59
  517.0 3.9 collective-permute-start.57
  520.9 5.0 collective-permute-start.61
  522.5 4.8 collective-permute-start.62
  523.9 3.9 collective-permute-start.60
  524.5 31.6 %collective-permute-start.51 = (bf16[64,2816]{1,0:T(8,128)(2,1)}, bf16[64,2816]{1,0:T(8,128)(2,1)S(1)}, u32[]{:S(2)}, u32[]{:S(2)}) collective-permute-start(bf16[64,2816]{1,0:T(8,128)(2,1)} %get-tuple-element.131), channel_id=1, source_target_pairs={{0,8},{8,0},{16,24},{24,16},{1,9},{9,1},{17,25},{25,17},{2,10},{10... | collective-permute-start | bytes 1081352 | tf_op jit(solution)/shard_map/ppermute | solution.py:76
  525.1 31.0 %collective-permute-start.52 = (bf16[64,2816]{1,0:T(8,128)(2,1)}, bf16[64,2816]{1,0:T(8,128)(2,1)}, u32[]{:S(2)}, u32[]{:S(2)}) collective-permute-start(bf16[64,2816]{1,0:T(8,128)(2,1)} %get-tuple-element.132), channel_id=1, source_target_pairs={{0,16},{8,24},{16,0},{24,8},{1,17},{9,25},{17,1},{25,9},{2,18},{10... | collective-permute-start | bytes 1081352 | tf_op jit(solution)/shard_map/ppermute | solution.py:76
  527.9 4.1 collective-permute-start.63
  529.9 7.9 %collective-permute-start.54 = (bf16[64,1536]{1,0:T(8,128)(2,1)}, bf16[64,1536]{1,0:T(8,128)(2,1)S(1)}, u32[]{:S(2)}, u32[]{:S(2)}) collective-permute-start(bf16[64,1536]{1,0:T(8,128)(2,1)} %get-tuple-element.219), channel_id=1, source_target_pairs={{0,2},{2,0},{4,6},{6,4},{1,3},{3,1},{5,7},{7,5},{8,10},{10,8},{12,... | collective-permute-start | bytes 589832 | tf_op jit(solution)/shard_map/ppermute | solution.py:76
  530.8 7.2 %collective-permute-start.55 = (bf16[64,1536]{1,0:T(8,128)(2,1)S(1)}, bf16[64,1536]{1,0:T(8,128)(2,1)S(1)}, u32[]{:S(2)}, u32[]{:S(2)}) collective-permute-start(bf16[64,1536]{1,0:T(8,128)(2,1)S(1)} %get-tuple-element.218), channel_id=1, source_target_pairs={{0,4},{2,6},{4,0},{6,2},{1,5},{3,7},{5,1},{7,3},{8,12},{10,14},{12... | collective-permute-start | bytes 589832 | tf_op jit(solution)/shard_map/ppermute | solution.py:76
  531.9 10.6 %collective-permute-start.56 = (bf16[64,1536]{1,0:T(8,128)(2,1)S(1)}, bf16[64,1536]{1,0:T(8,128)(2,1)S(1)}, u32[]{:S(2)}, u32[]{:S(2)}) collective-permute-start(bf16[64,1536]{1,0:T(8,128)(2,1)S(1)} %get-tuple-element.217), channel_id=1, source_target_pairs={{0,6},{2,4},{4,2},{6,0},{1,7},{3,5},{5,3},{7,1},{8,14},{10,12},{12... | collective-permute-start | bytes 589832 | tf_op jit(solution)/shard_map/ppermute | solution.py:76
  537.8 19.1 %collective-permute-start.53 = (bf16[64,2816]{1,0:T(8,128)(2,1)}, bf16[64,2816]{1,0:T(8,128)(2,1)}, u32[]{:S(2)}, u32[]{:S(2)}) collective-permute-start(bf16[64,2816]{1,0:T(8,128)(2,1)} %get-tuple-element.133), channel_id=1, source_target_pairs={{0,24},{8,16},{16,8},{24,0},{1,25},{9,17},{17,9},{25,1},{2,26},{10... | collective-permute-start | bytes 1081352 | tf_op jit(solution)/shard_map/ppermute | solution.py:76
  (84 other events, 482.6 us)
Sparse Core Ops, SparseCore 0:
  48.1 64.4 all-gather.3
  118.9 68.5 all-gather.5
  214.5 44.4 all-gather.7
  287.8 112.6 reduce-scatter.5
  406.9 30.4 reduce-scatter.7
  440.6 68.4 reduce-scatter.3

commit v4 on v3

--- a/solution.py
+++ b/solution.py
@@ -454,16 +454,16 @@
     unit_one = inputs_f * scale_one
     normed = turn_columns(unit_one * gain_f[0], line, plane, cores, bf16)
     normed = gather_tokens(normed, PLANE)
+    normed, in_b, glu_held = together(normed, in_b, glu_held)
     proj = contract(normed, in_b, 1, 0)
 
-    glu_held, proj = together(glu_held, proj)
     glu_b = lax.all_gather(glu_held, GLU_OWNERS, axis=0, tiled=True)
     out_pair = core_pair(out_w.astype(bf16))
     out_blocks = gather_near(out_pair, LINE)
     proj, out_blocks = together(proj, out_blocks)
     out_blocks = gather_far(out_blocks, LINE)
     local_state, local_prod, last = call_scan(scan_kernel, order, proj, bound)
-    lasts = gather_small(last, LINE)
+    lasts = in_order([last] + [swap(last, LINE, k) for k in range(1, line)], LINE)
     lasts, out_blocks = together(lasts, out_blocks)
     state_in = jnp.zeros((channels,), f32)
     for k in range(line):
@@ -510,7 +510,6 @@
     glu_held = lax.psum_scatter(glu_part, GLU_OWNERS, scatter_dimension=0, tiled=True)
     down_part = contract(hidden, grad_output_b, 0, 0).astype(bf16)
     down_sums = core_sums(down_part, PLANE)
-    grad_second, down_sums = together(grad_second, down_sums)
     grad_gain_two = jnp.sum(grad_second * unit_two, axis=0)
     weighted_two = grad_second * gain_f[2]
     grad_resid = grad_output + scale_two * (
@@ -522,7 +521,7 @@
     block_out = output.astype(bf16)[None]
 
     grad_resid_b = gather_tokens(grad_resid.astype(bf16), PLANE)
-    grad_resid_b, block_out = together(grad_resid_b, block_out)
+    grad_resid_b, block_out, down_sums = together(grad_resid_b, block_out, down_sums)
     grad_gated = contract(grad_resid_b, out_b, 1, 1)
     out_part = contract(gated, grad_resid_b, 0, 0).astype(bf16)
     grad_gain_mid = jnp.sum(grad_gated * unit_mid * gate_act, axis=0)
@@ -535,7 +534,7 @@
     local_carried, local_rate, first = call_scan(
         back_kernel, order, proj, bound, rounded(grad_state)
     )
-    firsts = gather_small(first, LINE)
+    firsts = in_order([first] + [swap(first, LINE, k) for k in range(1, line)], LINE)
     carried_in = jnp.zeros((channels,), f32)
     for k in range(line - 1, -1, -1):
         carried_in = jnp.where(k > level, firsts[k, 1] * carried_in + firsts[k, 0], carried_in)
@@ -590,23 +589,22 @@
         jnp.concatenate([gain_part, squares], axis=0), (LINE, PLANE, CORE)
     )
     in_blocks = in_held.reshape(plane, rows, 3 * channels)
-    in_grad = join_columns(
-        send_each(rank_blocks(in_blocks, PLANE), PLANE), 3 * line, order, PLANE
-    )
+    in_came = send_each(rank_blocks(in_blocks, PLANE), PLANE)
     gain_total = totals[:3]
     squares = totals[3, 0] + squared(gain_total)
-    in_grad, squares = together(in_grad, squares)
-    in_grad, out_grad = in_grad.astype(f32), out_grad.astype(f32)
+    out_grad = out_grad.astype(f32)
     columns = gains.shape[1]
     gain_grad = lax.dynamic_slice_in_dim(
         gain_total, (device * cores + lax.axis_index(CORE)) * columns, columns, 1
     )
     grad_norm = jnp.sqrt(squares)
     factor = jnp.minimum(1.0, CLIP_LIMIT / (grad_norm + 1e-06))
-    in_res = adam_step(in_w, in_m, in_v, in_grad, factor, MATRIX_RATE, MATRIX_DECAY)
     out_res = adam_step(out_w, out_m, out_v, out_grad, factor, MATRIX_RATE, MATRIX_DECAY)
     down_res = adam_step(down_w, down_m, down_v, down_grad, factor, MATRIX_RATE, MATRIX_DECAY)
-    glu_came, in_res, out_res, down_res = together(glu_came, in_res, out_res, down_res)
+    in_came, out_res, down_res = together(in_came, out_res, down_res)
+    in_grad = join_columns(in_came, 3 * line, order, PLANE).astype(f32)
+    in_res = adam_step(in_w, in_m, in_v, in_grad, factor, MATRIX_RATE, MATRIX_DECAY)
+    glu_came, in_res = together(glu_came, in_res)
     glu_grad = join_columns(glu_came, 2, line_order, LINE).astype(f32)
     glu_res = adam_step(glu_w, glu_m, glu_v, glu_grad, factor, MATRIX_RATE, MATRIX_DECAY)
     gain_res = adam_step(gains, gain_m, gain_v, gain_grad, factor, GAIN_RATE, 0.0)

time: 581 us -> 570 us (0.981)
  waiting for transfers between devices: 278 us -> 264 us
    ppermute x64 -> x66, waiting for transfers between devices: 254 us -> 244 us  [swap(): return lax.ppermute(values, axis, [(i, i ^ bit) for i in range(size)])]
    ppermute x64 -> x66, starting transfers between devices: 81 us -> 84.5 us  [swap(): return lax.ppermute(values, axis, [(i, i ^ bit) for i in range(size)])]
    unnamed x160 -> x148, local copies, waits for them, and re-layouts: 17.8 us -> 15.8 us
  transfers between devices with their start and end apart: 70 -> 72, of which waited for: 51 -> 42; matrix products, arithmetic and copies ran while one was open for 21% -> 23% of each run, Pallas kernels for 2% -> 2%
where the time goes in v4:
time: 570 us; the launch traced here: 561 us
  waiting for transfers between devices  264 us (46%)
  starting transfers between devices  85.4 us (15%)
  matrix products  79.6 us (14%)
  other arithmetic  60.3 us (11%)
  local copies, waits for them, and re-layouts  32.1 us (6%)
  between operations  28.7 us (5%)
  Pallas kernels  10.8 us (2%)
    ppermute x66, waiting for transfers between devices, swap(): return lax.ppermute(values, axis, [(i, i ^ bit) for i in range(size)])  244 us
    ppermute x66, starting transfers between devices, swap(): return lax.ppermute(values, axis, [(i, i ^ bit) for i in range(size)])  84.5 us
    dot_general x12, matrix products, contract(): lax.dot_general(left_side, right_side, (((left_dim,), (right_dim,)), ((),...  79.6 us
    all_gather x1, waiting for transfers between devices, on_device(): in_b = lax.all_gather(in_held, MIXER_OWNERS, axis=0, tiled=True)  19.7 us
    unnamed x148, local copies, waits for them, and re-layouts  15.8 us
    sub x5, other arithmetic, adam_step(): weight - rate * (first_hat / (jnp.sqrt(second_hat) + ADAM_EPS) + decay *...  15.5 us
  transfers between devices with their start and end apart: 72, of which 42 were waited for; matrix products, arithmetic and copies ran while one was open for 23% of the time, Pallas kernels for 2%

profile of v4, /device:TPU:8, one launch (start us, length us, event | category | flops | bytes accessed | tf_op | source)
XLA Modules:
  0.0 561.1 jit_solution(17080096114270483842)
XLA Ops:
  10.4 2.4 collective-permute-start.10
  19.3 3.1 collective-permute-done.9
  24.7 15.9 %collective-permute-done.13 = bf16[64,2816]{1,0:T(8,128)(2,1)S(1)} collective-permute-done((bf16[64,2816]{1,0:T(8,128)(2,1)S(1)}, bf16[64,2816]{1,0:T(8,128)(2,1)S(1)}, u32[]{:S(2)}, u32[]{:S(2)}) %collective-permute-start.13) | collective-permute-done | bytes 360480 | tf_op jit(solution)/shard_map/ppermute | solution.py:76
  40.6 5.7 %collective-permute-done.12 = bf16[64,2816]{1,0:T(8,128)(2,1)S(1)} collective-permute-done((bf16[64,2816]{1,0:T(8,128)(2,1)S(1)}, bf16[64,2816]{1,0:T(8,128)(2,1)S(1)}, u32[]{:S(2)}, u32[]{:S(2)}) %collective-permute-start.12) | collective-permute-done | bytes 360480 | tf_op jit(solution)/shard_map/ppermute | solution.py:76
  48.3 2.4 collective-permute-start
  52.3 3.1 collective-permute-start.1
  63.8 2.4 collective-permute-done.4
  66.9 2.5 collective-permute-start.7
  70.5 12.3 %collective-permute-done.7 = bf16[128,2048]{1,0:T(8,128)(2,1)S(1)} collective-permute-done((bf16[128,2048]{1,0:T(8,128)(2,1)S(1)}, bf16[128,2048]{1,0:T(8,128)(2,1)S(1)}, u32[]{:S(2)}, u32[]{:S(2)}) %collective-permute-start.7) | collective-permute-done | bytes 524320 | tf_op jit(solution)/shard_map/ppermute | solution.py:76
  82.8 8.4 %collective-permute-done.6 = bf16[128,2048]{1,0:T(8,128)(2,1)S(1)} collective-permute-done((bf16[128,2048]{1,0:T(8,128)(2,1)S(1)}, bf16[128,2048]{1,0:T(8,128)(2,1)S(1)}, u32[]{:S(2)}, u32[]{:S(2)}) %collective-permute-start.6) | collective-permute-done | bytes 524320 | tf_op jit(solution)/shard_map/ppermute | solution.py:76
  92.9 19.7 %all-gather.4.cloned.1.call-done = bf16[2048,1536]{1,0:T(8,128)(2,1)} async-done(((bf16[256,1536]{1,0:T(8,128)(2,1)}), bf16[2048,1536]{1,0:T(8,128)(2,1)}) %all-gather.4.cloned.1.call-update) | async-done | bytes 6291472 | tf_op jit(solution)/shard_map/all_gather | solution.py:451
  114.9 2.8 collective-permute-start.15
  118.7 6.2 %fusion.94.proj_ref = f32[512,1536]{1,0:T(8,128)S(1)} fusion(bf16[512,2048]{1,0:T(8,128)(2,1)} %pad_maximum_fusion.1, bf16[2048,1536]{1,0:T(8,128)(2,1)} %all-gather.4.cloned.1.call-done), kind=kOutput, calls=%fused_computation.266 | convolution fusion | flops 3221225472 | bytes 11534336 | tf_op jit(solution)/shard_map/dot_general | solution.py:30
  124.9 15.2 %collective-permute-done.15 = bf16[2,64,2048]{2,1,0:T(8,128)(2,1)S(1)} collective-permute-done((bf16[2,64,2048]{2,1,0:T(8,128)(2,1)S(1)}, bf16[2,64,2048]{2,1,0:T(8,128)(2,1)S(1)}, u32[]{:S(2)}, u32[]{:S(2)}) %collective-permute-start.15) | collective-permute-done | bytes 524320 | tf_op jit(solution)/shard_map/ppermute | solution.py:76
  140.1 2.1 collective-permute-done.16
  144.2 3.3 shard_map.334
  166.2 3.3 fusion.90
  177.6 16.6 %collective-permute-done.25 = bf16[128,2048]{1,0:T(8,128)(2,1)} collective-permute-done((bf16[128,2048]{1,0:T(8,128)(2,1)}, bf16[128,2048]{1,0:T(8,128)(2,1)}, u32[]{:S(2)}, u32[]{:S(2)}) %collective-permute-start.25) | collective-permute-done | bytes 524320 | tf_op jit(solution)/shard_map/ppermute | solution.py:76
  194.3 10.8 %collective-permute-done.23 = bf16[128,2048]{1,0:T(8,128)(2,1)} collective-permute-done((bf16[128,2048]{1,0:T(8,128)(2,1)}, bf16[128,2048]{1,0:T(8,128)(2,1)}, u32[]{:S(2)}, u32[]{:S(2)}) %collective-permute-start.23) | collective-permute-done | bytes 524320 | tf_op jit(solution)/shard_map/ppermute | solution.py:76
  210.8 2.4 collective-permute-start.29
  213.2 19.1 %collective-permute-done.28 = bf16[128,2048]{1,0:T(8,128)(2,1)S(1)} collective-permute-done((bf16[128,2048]{1,0:T(8,128)(2,1)}, bf16[128,2048]{1,0:T(8,128)(2,1)S(1)}, u32[]{:S(2)}, u32[]{:S(2)}) %collective-permute-start.28) | collective-permute-done | bytes 524320 | tf_op jit(solution)/shard_map/ppermute | solution.py:76
  232.2 3.1 collective-permute-done.29
  237.0 10.0 %collective-permute-done.30 = bf16[128,2048]{1,0:T(8,128)(2,1)S(1)} collective-permute-done((bf16[128,2048]{1,0:T(8,128)(2,1)S(1)}, bf16[128,2048]{1,0:T(8,128)(2,1)S(1)}, u32[]{:S(2)}, u32[]{:S(2)}) %collective-permute-start.30) | collective-permute-done | bytes 524320 | tf_op jit(solution)/shard_map/ppermute | solution.py:76
  248.8 11.8 %fusion.95 = f32[512,2816]{1,0:T(8,128)} fusion(bf16[512,2048]{1,0:T(8,128)(2,1)S(1)} %pad_maximum_fusion.4, bf16[2048,2816]{1,0:T(8,128)(2,1)} %all-gather.6.cloned.1.call-done), kind=kOutput, calls=%fused_computation.267 | convolution fusion | flops 5905580032 | bytes 19398656 | tf_op jit(solution)/shard_map/dot_general | solution.py:30
  264.0 10.5 %multiply_convert_fusion.2 = (bf16[512,1408]{1,0:T(8,128)(2,1)S(1)}, bf16[512,1408]{1,0:T(8,128)(2,1)S(1)}, bf16[512,1408]{1,0:T(8,128)(2,1)}) fusion(f32[512,2816]{1,0:T(8,128)} %fusion.95, bf16[512,2048]{1,0:T(8,128)(2,1)} %constant_dynamic-update-slice_fusion.9, bf16[1408,2048]{1,0:T(8,128)(2,1)} %all-gather.8.cloned.1.call-done), kind=kOutput, calls=%fused_computation.16 | convolution fusion | flops 2963603456 | bytes 17956864 | tf_op jit(solution)/shard_map/dot_general | solution.py:30
  276.0 8.9 %convolution_convert_fusion = bf16[2048,2816]{1,0:T(8,128)(2,1)} fusion(bf16[512,2048]{1,0:T(8,128)(2,1)S(1)} %copy-done.34, bf16[512,1408]{1,0:T(8,128)(2,1)S(1)} %get-tuple-element.186, bf16[512,1408]{1,0:T(8,128)(2,1)S(1)} %get-tuple-element.185), kind=kOutput, calls=%fused_computation | convolution fusion | flops 5917114368 | bytes 16515072 | tf_op jit(solution)/shard_map/dot_general | solution.py:30
  285.0 10.0 %fusion.91 = (bf16[512,2048]{1,0:T(8,128)(2,1)S(1)}, f32[512,2048]{1,0:T(8,128)S(1)}) fusion(bf16[2048,2816]{1,0:T(8,128)(2,1)} %all-gather.6.cloned.1.call-done, bf16[512,1408]{1,0:T(8,128)(2,1)} %copy-done.69, bf16[512,1408]{1,0:T(8,128)(2,1)} %copy-done.68), kind=kOutput, calls=%fused_computation.263 | convolution fusion | flops 5912395776 | bytes 20709376 | tf_op jit(solution)/shard_map/dot_general | solution.py:30
  297.2 17.0 %collective-permute-done.32 = bf16[128,2048]{1,0:T(8,128)(2,1)S(1)} collective-permute-done((bf16[128,2048]{1,0:T(8,128)(2,1)S(1)}, bf16[128,2048]{1,0:T(8,128)(2,1)S(1)}, u32[]{:S(2)}, u32[]{:S(2)}) %collective-permute-start.32) | collective-permute-done | bytes 524320 | tf_op jit(solution)/shard_map/ppermute | solution.py:76
  314.4 3.4 collective-permute-start.33
  317.8 5.2 convolution_convert_fusion.2
  323.0 2.4 copy-done.23
  327.3 4.9 collective-permute-done.33
  333.9 3.4 fusion.92
  338.3 2.4 collective-permute-start.38
  345.1 6.8 %collective-permute-done.38 = bf16[128,2048]{1,0:T(8,128)(2,1)S(1)} collective-permute-done((bf16[128,2048]{1,0:T(8,128)(2,1)S(1)}, bf16[128,2048]{1,0:T(8,128)(2,1)S(1)}, u32[]{:S(2)}, u32[]{:S(2)}) %collective-permute-start.38) | collective-permute-done | bytes 524320 | tf_op jit(solution)/shard_map/ppermute | solution.py:76
  351.9 2.5 collective-permute-start.40
  355.3 3.3 collective-permute-done.37
  359.5 2.5 collective-permute-start.39
  367.9 2.4 pad_maximum_fusion.5
  370.3 9.5 %collective-permute-done.39 = bf16[128,2048]{1,0:T(8,128)(2,1)} collective-permute-done((bf16[128,2048]{1,0:T(8,128)(2,1)}, bf16[128,2048]{1,0:T(8,128)(2,1)}, u32[]{:S(2)}, u32[]{:S(2)}) %collective-permute-start.39) | collective-permute-done | bytes 524320 | tf_op jit(solution)/shard_map/ppermute | solution.py:76
  379.8 2.7 fusion.42
  382.4 5.9 %fusion = bf16[4,176,2048]{2,1,0:T(8,128)(2,1)} fusion(bf16[4,176,2048]{2,1,0:T(8,128)(2,1)} %collective-permute-done.41, bf16[4,2,176,2048]{3,2,1,0:T(8,128)(2,1)} %bitcast.206, s32[]{:T(128)S(6)} %select_n.214), kind=kLoop, calls=%fused_computation.4 | loop fusion | flops 5767168 | bytes 8650756 | tf_op jit(solution)/shard_map/convert_element_type | solution.py:160
  388.3 2.6 convolution_convert_fusion.3
  392.0 4.3 multiply_reduce_fusion.4
  397.0 2.9 collective-permute-done.42
  400.7 2.9 collective-permute-done.43
  404.4 3.2 shard_map.337
  407.8 4.2 collective-permute-start.45
  417.7 5.7 %convolution_convert_fusion.1 = bf16[2048,1536]{1,0:T(8,128)(2,1)} fusion(bf16[512,2048]{1,0:T(8,128)(2,1)S(1)} %copy-done.31, bf16[512,512]{1,0:T(8,128)(2,1)S(1)} %get-tuple-element.191, bf16[512,512]{1,0:T(8,128)(2,1)S(1)} %get-tuple-element.189, bf16[512,512]{1,0:T(8,128)(2,1)S(1)} %get-tuple-element.188), kind=kOutput, calls=%fused_computation.1 | convolution fusion | flops 3229089792 | bytes 9961472 | tf_op jit(solution)/shard_map/dot_general | solution.py:30
  424.7 7.8 %fusion.93 = (bf16[512,2048]{1,0:T(8,128)(2,1)S(1)}, f32[512,2048]{1,0:T(8,128)}) fusion(bf16[2048,1536]{1,0:T(8,128)(2,1)} %all-gather.4.cloned.1.call-done, bf16[512,512]{1,0:T(8,128)(2,1)S(1)} %copy-done.45, bf16[512,512]{1,0:T(8,128)(2,1)S(1)} %copy-done.49, bf16[512,512]{1,0:T(8,128)(2,1)S(1)} %copy-done.47), kind=kOutput, calls=%fused_computation.265 | convolution fusion | flops 3226992640 | bytes 14155776 | tf_op jit(solution)/shard_map/dot_general | solution.py:30
  434.7 2.5 collective-permute-start.47
  440.8 7.9 %collective-permute-done.49 = bf16[128,2048]{1,0:T(8,128)(2,1)S(1)} collective-permute-done((bf16[128,2048]{1,0:T(8,128)(2,1)}, bf16[128,2048]{1,0:T(8,128)(2,1)S(1)}, u32[]{:S(2)}, u32[]{:S(2)}) %collective-permute-start.49) | collective-permute-done | bytes 524320 | tf_op jit(solution)/shard_map/ppermute | solution.py:76
  449.3 23.3 %collective-permute-done.48 = bf16[128,2048]{1,0:T(8,128)(2,1)} collective-permute-done((bf16[128,2048]{1,0:T(8,128)(2,1)}, bf16[128,2048]{1,0:T(8,128)(2,1)}, u32[]{:S(2)}, u32[]{:S(2)}) %collective-permute-start.48) | collective-permute-done | bytes 524320 | tf_op jit(solution)/shard_map/ppermute | solution.py:76
  477.0 6.9 %collective-permute-done.51 = bf16[176,2048]{1,0:T(8,128)(2,1)} collective-permute-done((bf16[176,2048]{1,0:T(8,128)(2,1)}, bf16[176,2048]{1,0:T(8,128)(2,1)}, u32[]{:S(2)}, u32[]{:S(2)}) %collective-permute-start.51) | collective-permute-done | bytes 720928 | tf_op jit(solution)/shard_map/ppermute | solution.py:76
  483.9 3.5 multiply_reduce_fusion.2
  490.0 2.4 dynamic-slice_bitcast_fusion.4
  494.9 2.1 multiply_reduce_fusion.1
  497.7 2.8 collective-permute-start.60
  500.5 2.2 collective-permute-start.61
  502.8 2.9 collective-permute-done.61
  521.8 5.3 multiply_subtract_fusion.2
  530.2 3.1 multiply_subtract_fusion.1
  533.2 13.7 %collective-permute-done.55.refs_3_ = bf16[64,2816]{1,0:T(8,128)(2,1)S(1)} collective-permute-done((bf16[64,2816]{1,0:T(8,128)(2,1)S(1)}, bf16[64,2816]{1,0:T(8,128)(2,1)S(1)}, u32[]{:S(2)}, u32[]{:S(2)}) %collective-permute-start.55) | collective-permute-done | bytes 360480 | tf_op jit(solution)/shard_map/ppermute | solution.py:76
  547.6 5.1 multiply_subtract_fusion
  (388 shorter events, 127.0 us)
Async XLA Ops:
  7.2 105.4 %all-gather.4.cloned.1.call-start = ((), (), s32[]{:S(2)}) async-start(), calls=%async_computation.3 | async-start | bytes 7077888 | tf_op jit(solution)/shard_map/all_gather | solution.py:451
  10.4 8.9 %collective-permute-start.10 = (bf16[64,1536]{1,0:T(8,128)(2,1)}, bf16[64,1536]{1,0:T(8,128)(2,1)S(1)}, u32[]{:S(2)}, u32[]{:S(2)}) collective-permute-start(bf16[64,1536]{1,0:T(8,128)(2,1)} %get-tuple-element.230), channel_id=1, source_target_pairs={{0,6},{2,4},{4,2},{6,0},{1,7},{3,5},{5,3},{7,1},{8,14},{10,12},{12... | collective-permute-start | bytes 589832 | tf_op jit(solution)/shard_map/ppermute | solution.py:76
  12.8 9.6 %collective-permute-start.9 = (bf16[64,1536]{1,0:T(8,128)(2,1)}, bf16[64,1536]{1,0:T(8,128)(2,1)}, u32[]{:S(2)}, u32[]{:S(2)}) collective-permute-start(bf16[64,1536]{1,0:T(8,128)(2,1)} %get-tuple-element.231), channel_id=1, source_target_pairs={{0,4},{2,6},{4,0},{6,2},{1,5},{3,7},{5,1},{7,3},{8,12},{10,14},{12... | collective-permute-start | bytes 589832 | tf_op jit(solution)/shard_map/ppermute | solution.py:76
  13.3 9.2 %collective-permute-start.8 = (bf16[64,1536]{1,0:T(8,128)(2,1)S(1)}, bf16[64,1536]{1,0:T(8,128)(2,1)}, u32[]{:S(2)}, u32[]{:S(2)}) collective-permute-start(bf16[64,1536]{1,0:T(8,128)(2,1)S(1)} %get-tuple-element.232), channel_id=1, source_target_pairs={{0,2},{2,0},{4,6},{6,4},{1,3},{3,1},{5,7},{7,5},{8,10},{10,8},{12,... | collective-permute-start | bytes 589832 | tf_op jit(solution)/shard_map/ppermute | solution.py:76
  14.7 26.0 %collective-permute-start.13 = (bf16[64,2816]{1,0:T(8,128)(2,1)S(1)}, bf16[64,2816]{1,0:T(8,128)(2,1)S(1)}, u32[]{:S(2)}, u32[]{:S(2)}) collective-permute-start(bf16[64,2816]{1,0:T(8,128)(2,1)S(1)} %get-tuple-element.218), channel_id=1, source_target_pairs={{0,24},{8,16},{16,8},{24,0},{1,25},{9,17},{17,9},{25,1},{2,26},{10... | collective-permute-start | bytes 1081352 | tf_op jit(solution)/shard_map/ppermute | solution.py:76
  16.3 30.0 %collective-permute-start.12 = (bf16[64,2816]{1,0:T(8,128)(2,1)S(1)}, bf16[64,2816]{1,0:T(8,128)(2,1)S(1)}, u32[]{:S(2)}, u32[]{:S(2)}) collective-permute-start(bf16[64,2816]{1,0:T(8,128)(2,1)S(1)} %get-tuple-element.219), channel_id=1, source_target_pairs={{0,16},{8,24},{16,0},{24,8},{1,17},{9,25},{17,1},{25,9},{2,18},{10... | collective-permute-start | bytes 1081352 | tf_op jit(solution)/shard_map/ppermute | solution.py:76
  19.3 27.0 %collective-permute-start.11 = (bf16[64,2816]{1,0:T(8,128)(2,1)S(1)}, bf16[64,2816]{1,0:T(8,128)(2,1)S(1)}, u32[]{:S(2)}, u32[]{:S(2)}) collective-permute-start(bf16[64,2816]{1,0:T(8,128)(2,1)S(1)} %get-tuple-element.220), channel_id=1, source_target_pairs={{0,8},{8,0},{16,24},{24,16},{1,9},{9,1},{17,25},{25,17},{2,10},{10... | collective-permute-start | bytes 1081352 | tf_op jit(solution)/shard_map/ppermute | solution.py:76
  48.0 161.6 %all-gather.6.cloned.1.call-start = ((), (), s32[]{:S(2)}) async-start(), calls=%async_computation.4 | async-start | bytes 12976128 | tf_op jit(solution)/shard_map/all_gather | solution.py:460
  48.3 4.0 collective-permute-start
  52.3 4.7 collective-permute-start.1
  62.2 4.0 collective-permute-start.4
  66.9 15.9 %collective-permute-start.7 = (bf16[128,2048]{1,0:T(8,128)(2,1)S(1)}, bf16[128,2048]{1,0:T(8,128)(2,1)S(1)}, u32[]{:S(2)}, u32[]{:S(2)}) collective-permute-start(bf16[128,2048]{1,0:T(8,128)(2,1)S(1)} %shard_map.331), channel_id=1, source_target_pairs={{0,6},{2,4},{4,2},{6,0},{1,7},{3,5},{5,3},{7,1},{8,14},{10,12},{12... | collective-permute-start | bytes 1572872 | tf_op jit(solution)/shard_map/ppermute | solution.py:76
  69.5 21.7 %collective-permute-start.6 = (bf16[128,2048]{1,0:T(8,128)(2,1)S(1)}, bf16[128,2048]{1,0:T(8,128)(2,1)S(1)}, u32[]{:S(2)}, u32[]{:S(2)}) collective-permute-start(bf16[128,2048]{1,0:T(8,128)(2,1)S(1)} %shard_map.331), channel_id=1, source_target_pairs={{0,4},{2,6},{4,0},{6,2},{1,5},{3,7},{5,1},{7,3},{8,12},{10,14},{12... | collective-permute-start | bytes 1572872 | tf_op jit(solution)/shard_map/ppermute | solution.py:76
  70.0 21.4 %collective-permute-start.5 = (bf16[128,2048]{1,0:T(8,128)(2,1)S(1)}, bf16[128,2048]{1,0:T(8,128)(2,1)S(1)}, u32[]{:S(2)}, u32[]{:S(2)}) collective-permute-start(bf16[128,2048]{1,0:T(8,128)(2,1)S(1)} %shard_map.331), channel_id=1, source_target_pairs={{0,2},{2,0},{4,6},{6,4},{1,3},{3,1},{5,7},{7,5},{8,10},{10,8},{12,... | collective-permute-start | bytes 1572872 | tf_op jit(solution)/shard_map/ppermute | solution.py:76
  112.7 151.3 %all-gather.8.cloned.1.call-start = ((), (), s32[]{:S(2)}) async-start(), calls=%async_computation.5 | async-start | bytes 6488064 | tf_op jit(solution)/shard_map/all_gather | solution.py:491
  114.9 25.2 %collective-permute-start.15 = (bf16[2,64,2048]{2,1,0:T(8,128)(2,1)S(1)}, bf16[2,64,2048]{2,1,0:T(8,128)(2,1)S(1)}, u32[]{:S(2)}, u32[]{:S(2)}) collective-permute-start(bf16[2,64,2048]{2,1,0:T(8,128)(2,1)S(1)} %pad_maximum_fusion.16), channel_id=1, source_target_pairs={{0,8},{8,0},{16,24},{24,16},{1,9},{9,1},{17,25},{25,17},{2,10},{10... | collective-permute-start | bytes 1572872 | tf_op jit(solution)/shard_map/ppermute | solution.py:76
  117.7 24.6 %collective-permute-start.16 = (bf16[2,64,2048]{2,1,0:T(8,128)(2,1)S(1)}, bf16[2,64,2048]{2,1,0:T(8,128)(2,1)}, u32[]{:S(2)}, u32[]{:S(2)}) collective-permute-start(bf16[2,64,2048]{2,1,0:T(8,128)(2,1)S(1)} %pad_maximum_fusion.16), channel_id=1, source_target_pairs={{0,16},{8,24},{16,0},{24,8},{1,17},{9,25},{17,1},{25,9},{2,18},{10... | collective-permute-start | bytes 1572872 | tf_op jit(solution)/shard_map/ppermute | solution.py:76
  142.2 14.3 %collective-permute-start.20 = (bf16[2,64,2048]{2,1,0:T(8,128)(2,1)}, bf16[2,64,2048]{2,1,0:T(8,128)(2,1)}, u32[]{:S(2)}, u32[]{:S(2)}) collective-permute-start(bf16[2,64,2048]{2,1,0:T(8,128)(2,1)} %collective-permute-done.16), channel_id=1, source_target_pairs={{0,8},{8,0},{16,24},{24,16},{1,9},{9,1},{17,25},{25,17},{2,10},{10... | collective-permute-start | bytes 1572872 | tf_op jit(solution)/shard_map/ppermute | solution.py:76
  149.5 6.2 %collective-permute-start.19 = (f32[2,512]{1,0:T(2,128)S(1)}, f32[2,512]{1,0:T(2,128)S(1)}, u32[]{:S(2)}, u32[]{:S(2)}) collective-permute-start(f32[2,512]{1,0:T(2,128)S(1)} %get-tuple-element.94), channel_id=1, source_target_pairs={{0,24},{8,16},{16,8},{24,0},{1,25},{9,17},{17,9},{25,1},{2,26},{10... | collective-permute-start | bytes 12296 | tf_op jit(solution)/shard_map/ppermute | solution.py:76
  150.8 5.7 %collective-permute-start.18 = (f32[2,512]{1,0:T(2,128)S(1)}, f32[2,512]{1,0:T(2,128)S(1)}, u32[]{:S(2)}, u32[]{:S(2)}) collective-permute-start(f32[2,512]{1,0:T(2,128)S(1)} %get-tuple-element.94), channel_id=1, source_target_pairs={{0,16},{8,24},{16,0},{24,8},{1,17},{9,25},{17,1},{25,9},{2,18},{10... | collective-permute-start | bytes 12296 | tf_op jit(solution)/shard_map/ppermute | solution.py:76
  152.0 4.5 collective-permute-start.17
  170.8 23.5 %collective-permute-start.25 = (bf16[128,2048]{1,0:T(8,128)(2,1)}, bf16[128,2048]{1,0:T(8,128)(2,1)}, u32[]{:S(2)}, u32[]{:S(2)}) collective-permute-start(bf16[128,2048]{1,0:T(8,128)(2,1)} %get-tuple-element.203), channel_id=1, source_target_pairs={{0,2},{2,0},{4,6},{6,4},{1,3},{3,1},{5,7},{7,5},{8,10},{10,8},{12,... | collective-permute-start | bytes 1572872 | tf_op jit(solution)/shard_map/ppermute | solution.py:76
  172.2 22.0 %collective-permute-start.24 = (bf16[128,2048]{1,0:T(8,128)(2,1)}, bf16[128,2048]{1,0:T(8,128)(2,1)}, u32[]{:S(2)}, u32[]{:S(2)}) collective-permute-start(bf16[128,2048]{1,0:T(8,128)(2,1)} %get-tuple-element.204), channel_id=1, source_target_pairs={{0,4},{2,6},{4,0},{6,2},{1,5},{3,7},{5,1},{7,3},{8,12},{10,14},{12... | collective-permute-start | bytes 1572872 | tf_op jit(solution)/shard_map/ppermute | solution.py:76
  173.7 31.3 %collective-permute-start.23 = (bf16[128,2048]{1,0:T(8,128)(2,1)}, bf16[128,2048]{1,0:T(8,128)(2,1)}, u32[]{:S(2)}, u32[]{:S(2)}) collective-permute-start(bf16[128,2048]{1,0:T(8,128)(2,1)} %get-tuple-element.202), channel_id=1, source_target_pairs={{0,6},{2,4},{4,2},{6,0},{1,7},{3,5},{5,3},{7,1},{8,14},{10,12},{12... | collective-permute-start | bytes 1572872 | tf_op jit(solution)/shard_map/ppermute | solution.py:76
  175.3 31.7 %collective-permute-start.26 = (bf16[128,2048]{1,0:T(8,128)(2,1)}, bf16[128,2048]{1,0:T(8,128)(2,1)S(1)}, u32[]{:S(2)}, u32[]{:S(2)}) collective-permute-start(bf16[128,2048]{1,0:T(8,128)(2,1)} %fusion.29), channel_id=1, source_target_pairs={{0,8},{8,0},{16,24},{24,16},{1,9},{9,1},{17,25},{25,17},{2,10},{10... | collective-permute-start | bytes 1572872 | tf_op jit(solution)/shard_map/ppermute | solution.py:76
  176.7 30.3 %collective-permute-start.27 = (bf16[128,2048]{1,0:T(8,128)(2,1)}, bf16[128,2048]{1,0:T(8,128)(2,1)S(1)}, u32[]{:S(2)}, u32[]{:S(2)}) collective-permute-start(bf16[128,2048]{1,0:T(8,128)(2,1)} %fusion.29), channel_id=1, source_target_pairs={{0,16},{8,24},{16,0},{24,8},{1,17},{9,25},{17,1},{25,9},{2,18},{10... | collective-permute-start | bytes 1572872 | tf_op jit(solution)/shard_map/ppermute | solution.py:76
  209.6 181.3 %reduce-scatter.6.cloned.1.call-start = ((), (), s32[]{:S(2)}) async-start(), calls=%async_computation.7 | async-start | bytes 12976128 | tf_op jit(solution)/shard_map/reduce_scatter | solution.py:510
  210.2 22.1 %collective-permute-start.28 = (bf16[128,2048]{1,0:T(8,128)(2,1)}, bf16[128,2048]{1,0:T(8,128)(2,1)S(1)}, u32[]{:S(2)}, u32[]{:S(2)}) collective-permute-start(bf16[128,2048]{1,0:T(8,128)(2,1)} %copy-done.4), channel_id=1, source_target_pairs={{0,8},{8,0},{16,24},{24,16},{1,9},{9,1},{17,25},{25,17},{2,10},{10... | collective-permute-start | bytes 1572872 | tf_op jit(solution)/shard_map/ppermute | solution.py:76
  210.8 24.6 %collective-permute-start.29 = (bf16[128,2048]{1,0:T(8,128)(2,1)}, bf16[128,2048]{1,0:T(8,128)(2,1)S(1)}, u32[]{:S(2)}, u32[]{:S(2)}) collective-permute-start(bf16[128,2048]{1,0:T(8,128)(2,1)} %copy-done.4), channel_id=1, source_target_pairs={{0,16},{8,24},{16,0},{24,8},{1,17},{9,25},{17,1},{25,9},{2,18},{10... | collective-permute-start | bytes 1572872 | tf_op jit(solution)/shard_map/ppermute | solution.py:76
  235.3 11.7 %collective-permute-start.30 = (bf16[128,2048]{1,0:T(8,128)(2,1)S(1)}, bf16[128,2048]{1,0:T(8,128)(2,1)S(1)}, u32[]{:S(2)}, u32[]{:S(2)}) collective-permute-start(bf16[128,2048]{1,0:T(8,128)(2,1)S(1)} %collective-permute-done.29), channel_id=1, source_target_pairs={{0,8},{8,0},{16,24},{24,16},{1,9},{9,1},{17,25},{25,17},{2,10},{10... | collective-permute-start | bytes 1572872 | tf_op jit(solution)/shard_map/ppermute | solution.py:76
  248.4 14.8 %collective-permute-start.31 = (bf16[128,2048]{1,0:T(8,128)(2,1)S(1)}, bf16[128,2048]{1,0:T(8,128)(2,1)S(1)}, u32[]{:S(2)}, u32[]{:S(2)}) collective-permute-start(bf16[128,2048]{1,0:T(8,128)(2,1)S(1)} %copy-done.53), channel_id=1, source_target_pairs={{0,8},{8,0},{16,24},{24,16},{1,9},{9,1},{17,25},{25,17},{2,10},{10... | collective-permute-start | bytes 1572872 | tf_op jit(solution)/shard_map/ppermute | solution.py:76
  284.9 207.5 %reduce-scatter.8.cloned.1.call-start = ((), (), s32[]{:S(2)}) async-start(), calls=%async_computation.8 | async-start | bytes 2359296 | tf_op jit(solution)/shard_map/reduce_scatter | solution.py:532
  295.1 19.1 %collective-permute-start.32 = (bf16[128,2048]{1,0:T(8,128)(2,1)S(1)}, bf16[128,2048]{1,0:T(8,128)(2,1)S(1)}, u32[]{:S(2)}, u32[]{:S(2)}) collective-permute-start(bf16[128,2048]{1,0:T(8,128)(2,1)S(1)} %get-tuple-element.200), channel_id=1, source_target_pairs={{0,8},{8,0},{16,24},{24,16},{1,9},{9,1},{17,25},{25,17},{2,10},{10... | collective-permute-start | bytes 1572872 | tf_op jit(solution)/shard_map/ppermute | solution.py:76
  296.3 31.1 %collective-permute-start.34 = (bf16[128,2048]{1,0:T(8,128)(2,1)S(1)}, bf16[128,2048]{1,0:T(8,128)(2,1)S(1)}, u32[]{:S(2)}, u32[]{:S(2)}) collective-permute-start(bf16[128,2048]{1,0:T(8,128)(2,1)S(1)} %get-tuple-element.201), channel_id=1, source_target_pairs={{0,8},{8,0},{16,24},{24,16},{1,9},{9,1},{17,25},{25,17},{2,10},{10... | collective-permute-start | bytes 1572872 | tf_op jit(solution)/shard_map/ppermute | solution.py:76
  314.4 17.9 %collective-permute-start.33 = (bf16[128,2048]{1,0:T(8,128)(2,1)S(1)}, bf16[128,2048]{1,0:T(8,128)(2,1)S(1)}, u32[]{:S(2)}, u32[]{:S(2)}) collective-permute-start(bf16[128,2048]{1,0:T(8,128)(2,1)S(1)} %fusion.24), channel_id=1, source_target_pairs={{0,16},{8,24},{16,0},{24,8},{1,17},{9,25},{17,1},{25,9},{2,18},{10... | collective-permute-start | bytes 1572872 | tf_op jit(solution)/shard_map/ppermute | solution.py:76
  327.3 55.1 %collective-permute-start.41 = (bf16[4,176,2048]{2,1,0:T(8,128)(2,1)}, bf16[4,176,2048]{2,1,0:T(8,128)(2,1)}, u32[]{:S(2)}, u32[]{:S(2)}) collective-permute-start(bf16[4,176,2048]{2,1,0:T(8,128)(2,1)} %dynamic-slice_bitcast_fusion), channel_id=1, source_target_pairs={{0,1},{1,0},{2,3},{3,2},{4,5},{5,4},{6,7},{7,6},{8,9},{9,8},{10,11... | collective-permute-start | bytes 8650760 | tf_op jit(solution)/shard_map/ppermute | solution.py:76
  338.3 13.6 %collective-permute-start.38 = (bf16[128,2048]{1,0:T(8,128)(2,1)S(1)}, bf16[128,2048]{1,0:T(8,128)(2,1)S(1)}, u32[]{:S(2)}, u32[]{:S(2)}) collective-permute-start(bf16[128,2048]{1,0:T(8,128)(2,1)S(1)} %get-tuple-element.198), channel_id=1, source_target_pairs={{0,8},{8,0},{16,24},{24,16},{1,9},{9,1},{17,25},{25,17},{2,10},{10... | collective-permute-start | bytes 1572872 | tf_op jit(solution)/shard_map/ppermute | solution.py:76
  341.6 17.0 %collective-permute-start.37 = (bf16[128,2048]{1,0:T(8,128)(2,1)}, bf16[128,2048]{1,0:T(8,128)(2,1)S(1)}, u32[]{:S(2)}, u32[]{:S(2)}) collective-permute-start(bf16[128,2048]{1,0:T(8,128)(2,1)} %convert_element_type.164), channel_id=1, source_target_pairs={{0,6},{2,4},{4,2},{6,0},{1,7},{3,5},{5,3},{7,1},{8,14},{10,12},{12... | collective-permute-start | bytes 1572872 | tf_op jit(solution)/shard_map/ppermute | solution.py:76
  342.0 25.8 %collective-permute-start.36 = (bf16[128,2048]{1,0:T(8,128)(2,1)}, bf16[128,2048]{1,0:T(8,128)(2,1)}, u32[]{:S(2)}, u32[]{:S(2)}) collective-permute-start(bf16[128,2048]{1,0:T(8,128)(2,1)} %convert_element_type.164), channel_id=1, source_target_pairs={{0,4},{2,6},{4,0},{6,2},{1,5},{3,7},{5,1},{7,3},{8,12},{10,14},{12... | collective-permute-start | bytes 1572872 | tf_op jit(solution)/shard_map/ppermute | solution.py:76
  343.5 24.4 %collective-permute-start.35 = (bf16[128,2048]{1,0:T(8,128)(2,1)}, bf16[128,2048]{1,0:T(8,128)(2,1)}, u32[]{:S(2)}, u32[]{:S(2)}) collective-permute-start(bf16[128,2048]{1,0:T(8,128)(2,1)} %convert_element_type.164), channel_id=1, source_target_pairs={{0,2},{2,0},{4,6},{6,4},{1,3},{3,1},{5,7},{7,5},{8,10},{10,8},{12,... | collective-permute-start | bytes 1572872 | tf_op jit(solution)/shard_map/ppermute | solution.py:76
  351.9 18.3 %collective-permute-start.40 = (bf16[128,2048]{1,0:T(8,128)(2,1)}, bf16[128,2048]{1,0:T(8,128)(2,1)}, u32[]{:S(2)}, u32[]{:S(2)}) collective-permute-start(bf16[128,2048]{1,0:T(8,128)(2,1)} %get-tuple-element.199), channel_id=1, source_target_pairs={{0,8},{8,0},{16,24},{24,16},{1,9},{9,1},{17,25},{25,17},{2,10},{10... | collective-permute-start | bytes 1572872 | tf_op jit(solution)/shard_map/ppermute | solution.py:76
  359.5 20.3 %collective-permute-start.39 = (bf16[128,2048]{1,0:T(8,128)(2,1)}, bf16[128,2048]{1,0:T(8,128)(2,1)}, u32[]{:S(2)}, u32[]{:S(2)}) collective-permute-start(bf16[128,2048]{1,0:T(8,128)(2,1)} %fusion.20), channel_id=1, source_target_pairs={{0,16},{8,24},{16,0},{24,8},{1,17},{9,25},{17,1},{25,9},{2,18},{10... | collective-permute-start | bytes 1572872 | tf_op jit(solution)/shard_map/ppermute | solution.py:76
  391.0 103.9 %reduce-scatter.4.cloned.1.call-start = ((), (), s32[]{:S(2)}) async-start(), calls=%async_computation.6 | async-start | bytes 7077888 | tf_op jit(solution)/shard_map/reduce_scatter | solution.py:567
  407.6 5.0 collective-permute-start.46
  407.8 5.8 %collective-permute-start.45 = (f32[2,512]{1,0:T(2,128)S(1)}, f32[2,512]{1,0:T(2,128)S(1)}, u32[]{:S(2)}, u32[]{:S(2)}) collective-permute-start(f32[2,512]{1,0:T(2,128)S(1)} %get-tuple-element.127), channel_id=1, source_target_pairs={{0,16},{8,24},{16,0},{24,8},{1,17},{9,25},{17,1},{25,9},{2,18},{10... | collective-permute-start | bytes 12296 | tf_op jit(solution)/shard_map/ppermute | solution.py:76
  433.6 15.1 %collective-permute-start.49 = (bf16[128,2048]{1,0:T(8,128)(2,1)}, bf16[128,2048]{1,0:T(8,128)(2,1)S(1)}, u32[]{:S(2)}, u32[]{:S(2)}) collective-permute-start(bf16[128,2048]{1,0:T(8,128)(2,1)} %get-tuple-element.196), channel_id=1, source_target_pairs={{0,2},{2,0},{4,6},{6,4},{1,3},{3,1},{5,7},{7,5},{8,10},{10,8},{12,... | collective-permute-start | bytes 1572872 | tf_op jit(solution)/shard_map/ppermute | solution.py:76
  434.2 38.3 %collective-permute-start.48 = (bf16[128,2048]{1,0:T(8,128)(2,1)}, bf16[128,2048]{1,0:T(8,128)(2,1)}, u32[]{:S(2)}, u32[]{:S(2)}) collective-permute-start(bf16[128,2048]{1,0:T(8,128)(2,1)} %get-tuple-element.197), channel_id=1, source_target_pairs={{0,4},{2,6},{4,0},{6,2},{1,5},{3,7},{5,1},{7,3},{8,12},{10,14},{12... | collective-permute-start | bytes 1572872 | tf_op jit(solution)/shard_map/ppermute | solution.py:76
  434.7 37.9 %collective-permute-start.47 = (bf16[128,2048]{1,0:T(8,128)(2,1)}, bf16[128,2048]{1,0:T(8,128)(2,1)}, u32[]{:S(2)}, u32[]{:S(2)}) collective-permute-start(bf16[128,2048]{1,0:T(8,128)(2,1)} %get-tuple-element.195), channel_id=1, source_target_pairs={{0,6},{2,4},{4,2},{6,0},{1,7},{3,5},{5,3},{7,1},{8,14},{10,12},{12... | collective-permute-start | bytes 1572872 | tf_op jit(solution)/shard_map/ppermute | solution.py:76
  438.5 38.5 %collective-permute-start.52 = (bf16[176,2048]{1,0:T(8,128)(2,1)}, bf16[176,2048]{1,0:T(8,128)(2,1)}, u32[]{:S(2)}, u32[]{:S(2)}) collective-permute-start(bf16[176,2048]{1,0:T(8,128)(2,1)} %get-tuple-element.193), channel_id=1, source_target_pairs={{0,6},{2,4},{4,2},{6,0},{1,7},{3,5},{5,3},{7,1},{8,14},{10,12},{12... | collective-permute-start | bytes 2162696 | tf_op jit(solution)/shard_map/ppermute | solution.py:76
  439.0 44.9 %collective-permute-start.51 = (bf16[176,2048]{1,0:T(8,128)(2,1)}, bf16[176,2048]{1,0:T(8,128)(2,1)}, u32[]{:S(2)}, u32[]{:S(2)}) collective-permute-start(bf16[176,2048]{1,0:T(8,128)(2,1)} %get-tuple-element.194), channel_id=1, source_target_pairs={{0,4},{2,6},{4,0},{6,2},{1,5},{3,7},{5,1},{7,3},{8,12},{10,14},{12... | collective-permute-start | bytes 2162696 | tf_op jit(solution)/shard_map/ppermute | solution.py:76
  448.7 35.2 %collective-permute-start.50 = (bf16[176,2048]{1,0:T(8,128)(2,1)}, bf16[176,2048]{1,0:T(8,128)(2,1)S(1)}, u32[]{:S(2)}, u32[]{:S(2)}) collective-permute-start(bf16[176,2048]{1,0:T(8,128)(2,1)} %get-tuple-element.192), channel_id=1, source_target_pairs={{0,2},{2,0},{4,6},{6,4},{1,3},{3,1},{5,7},{7,5},{8,10},{10,8},{12,... | collective-permute-start | bytes 2162696 | tf_op jit(solution)/shard_map/ppermute | solution.py:76
  497.7 5.0 collective-permute-start.60
  500.5 5.1 collective-permute-start.61
  502.7 3.9 collective-permute-start.59
  506.6 5.0 collective-permute-start.63
  508.1 4.8 collective-permute-start.64
  509.6 3.9 collective-permute-start.62
  510.2 23.1 %collective-permute-start.53 = (bf16[64,2816]{1,0:T(8,128)(2,1)}, bf16[64,2816]{1,0:T(8,128)(2,1)S(1)}, u32[]{:S(2)}, u32[]{:S(2)}) collective-permute-start(bf16[64,2816]{1,0:T(8,128)(2,1)} %get-tuple-element.133), channel_id=1, source_target_pairs={{0,8},{8,0},{16,24},{24,16},{1,9},{9,1},{17,25},{25,17},{2,10},{10... | collective-permute-start | bytes 1081352 | tf_op jit(solution)/shard_map/ppermute | solution.py:76
  510.7 22.5 %collective-permute-start.54 = (bf16[64,2816]{1,0:T(8,128)(2,1)}, bf16[64,2816]{1,0:T(8,128)(2,1)S(1)}, u32[]{:S(2)}, u32[]{:S(2)}) collective-permute-start(bf16[64,2816]{1,0:T(8,128)(2,1)} %get-tuple-element.134), channel_id=1, source_target_pairs={{0,16},{8,24},{16,0},{24,8},{1,17},{9,25},{17,1},{25,9},{2,18},{10... | collective-permute-start | bytes 1081352 | tf_op jit(solution)/shard_map/ppermute | solution.py:76
  513.6 4.1 collective-permute-start.65
  515.7 13.6 %collective-permute-start.56 = (bf16[64,1536]{1,0:T(8,128)(2,1)}, bf16[64,1536]{1,0:T(8,128)(2,1)S(1)}, u32[]{:S(2)}, u32[]{:S(2)}) collective-permute-start(bf16[64,1536]{1,0:T(8,128)(2,1)} %get-tuple-element.223), channel_id=1, source_target_pairs={{0,2},{2,0},{4,6},{6,4},{1,3},{3,1},{5,7},{7,5},{8,10},{10,8},{12,... | collective-permute-start | bytes 589832 | tf_op jit(solution)/shard_map/ppermute | solution.py:76
  516.5 12.8 %collective-permute-start.57 = (bf16[64,1536]{1,0:T(8,128)(2,1)}, bf16[64,1536]{1,0:T(8,128)(2,1)S(1)}, u32[]{:S(2)}, u32[]{:S(2)}) collective-permute-start(bf16[64,1536]{1,0:T(8,128)(2,1)} %get-tuple-element.222), channel_id=1, source_target_pairs={{0,4},{2,6},{4,0},{6,2},{1,5},{3,7},{5,1},{7,3},{8,12},{10,14},{12... | collective-permute-start | bytes 589832 | tf_op jit(solution)/shard_map/ppermute | solution.py:76
  517.7 11.7 %collective-permute-start.58 = (bf16[64,1536]{1,0:T(8,128)(2,1)S(1)}, bf16[64,1536]{1,0:T(8,128)(2,1)S(1)}, u32[]{:S(2)}, u32[]{:S(2)}) collective-permute-start(bf16[64,1536]{1,0:T(8,128)(2,1)S(1)} %get-tuple-element.221), channel_id=1, source_target_pairs={{0,6},{2,4},{4,2},{6,0},{1,7},{3,5},{5,3},{7,1},{8,14},{10,12},{12... | collective-permute-start | bytes 589832 | tf_op jit(solution)/shard_map/ppermute | solution.py:76
  529.2 17.7 %collective-permute-start.55 = (bf16[64,2816]{1,0:T(8,128)(2,1)S(1)}, bf16[64,2816]{1,0:T(8,128)(2,1)S(1)}, u32[]{:S(2)}, u32[]{:S(2)}) collective-permute-start(bf16[64,2816]{1,0:T(8,128)(2,1)S(1)} %copy-done.59), channel_id=1, source_target_pairs={{0,24},{8,16},{16,8},{24,0},{1,25},{9,17},{17,9},{25,1},{2,26},{10... | collective-permute-start | bytes 1081352 | tf_op jit(solution)/shard_map/ppermute | solution.py:76
  (80 other events, 654.6 us)
Sparse Core Ops, SparseCore 0:
  48.1 64.4 all-gather.3
  115.1 78.1 all-gather.5
  209.8 42.4 all-gather.7
  285.0 102.2 reduce-scatter.5
  391.1 32.3 reduce-scatter.7
  425.6 69.2 reduce-scatter.3

commit v5 on v4

--- a/solution.py
+++ b/solution.py
@@ -177,8 +177,11 @@
     )
 
 
-def core_pair(values):
-    return in_order([values] + [swap(values, CORE, k) for k in range(1, lax.axis_size(CORE))], CORE)
+def gather_pairs(blocks, axes):
+    blocks = jnp.stack(blocks)
+    cores = [blocks] + [swap(blocks, CORE, k) for k in range(1, lax.axis_size(CORE))]
+    cores = in_order(cores, CORE).swapaxes(0, 1)
+    return in_order(list(cores), axes).reshape(-1, blocks.shape[2])
 
 
 def send_each(blocks, axes):
@@ -454,24 +457,23 @@
     unit_one = inputs_f * scale_one
     normed = turn_columns(unit_one * gain_f[0], line, plane, cores, bf16)
     normed = gather_tokens(normed, PLANE)
+    normed, out_own = together(normed, out_w.astype(bf16))
+    out_blocks = gather_near(out_own, LINE)
     normed, in_b, glu_held = together(normed, in_b, glu_held)
     proj = contract(normed, in_b, 1, 0)
 
     glu_b = lax.all_gather(glu_held, GLU_OWNERS, axis=0, tiled=True)
-    out_pair = core_pair(out_w.astype(bf16))
-    out_blocks = gather_near(out_pair, LINE)
     proj, out_blocks = together(proj, out_blocks)
-    out_blocks = gather_far(out_blocks, LINE)
+    out_b = gather_pairs(gather_far(out_blocks, LINE), LINE)
     local_state, local_prod, last = call_scan(scan_kernel, order, proj, bound)
     lasts = in_order([last] + [swap(last, LINE, k) for k in range(1, line)], LINE)
-    lasts, out_blocks = together(lasts, out_blocks)
+    lasts, out_b = together(lasts, out_b)
     state_in = jnp.zeros((channels,), f32)
     for k in range(line):
         state_in = jnp.where(k < level, lasts[k, 1] * state_in + lasts[k, 0], state_in)
     state = local_state + local_prod * state_in[None, :]
     state_f = rounded(state)
     square_mid = total_tokens(jnp.sum(state_f * state_f, axis=1), PLANE)
-    out_b = in_order(out_blocks, LINE).reshape(channels, width)
     scale_mid = lax.rsqrt(square_mid / width + NORM_EPS)[:, None]
     unit_mid = state_f * scale_mid
     gate_raw = proj[:, 2 * channels :]

time: 570 us -> 570 us (level)
    unnamed x148 -> x142, local copies, waits for them, and re-layouts: 15.8 us -> 16.5 us
  transfers between devices with their start and end apart: 72 -> 72, of which waited for: 42 -> 43; matrix products, arithmetic and copies ran while one was open for 23% -> 24% of each run, Pallas kernels for 2% -> 2%
where the time goes in v5:
time: 570 us; the launch traced here: 561 us
  waiting for transfers between devices  259 us (45%)
  starting transfers between devices  87.1 us (15%)
  matrix products  79.4 us (14%)
  other arithmetic  64.3 us (11%)
  local copies, waits for them, and re-layouts  32.5 us (6%)
  between operations  28.6 us (5%)
  Pallas kernels  10.8 us (2%)
    ppermute x66, waiting for transfers between devices, swap(): return lax.ppermute(values, axis, [(i, i ^ bit) for i in range(size)])  239 us
    ppermute x66, starting transfers between devices, swap(): return lax.ppermute(values, axis, [(i, i ^ bit) for i in range(size)])  86.2 us
    dot_general x12, matrix products, contract(): lax.dot_general(left_side, right_side, (((left_dim,), (right_dim,)), ((),...  79.4 us
    all_gather x1, waiting for transfers between devices, on_device(): in_b = lax.all_gather(in_held, MIXER_OWNERS, axis=0, tiled=True)  19.8 us
    unnamed x142, local copies, waits for them, and re-layouts  16.5 us
    sub x5, other arithmetic, adam_step(): weight - rate * (first_hat / (jnp.sqrt(second_hat) + ADAM_EPS) + decay *...  15.5 us
  transfers between devices with their start and end apart: 72, of which 43 were waited for; matrix products, arithmetic and copies ran while one was open for 24% of the time, Pallas kernels for 2%

profile of v5, /device:TPU:8, one launch (start us, length us, event | category | flops | bytes accessed | tf_op | source)
XLA Modules:
  0.0 561.5 jit_solution(5102684988820789856)
XLA Ops:
  10.4 2.4 collective-permute-start.10
  19.3 3.1 collective-permute-done.9
  24.7 15.9 %collective-permute-done.13 = bf16[64,2816]{1,0:T(8,128)(2,1)S(1)} collective-permute-done((bf16[64,2816]{1,0:T(8,128)(2,1)S(1)}, bf16[64,2816]{1,0:T(8,128)(2,1)S(1)}, u32[]{:S(2)}, u32[]{:S(2)}) %collective-permute-start.13) | collective-permute-done | bytes 360480 | tf_op jit(solution)/shard_map/ppermute | solution.py:76
  40.6 5.7 %collective-permute-done.12 = bf16[64,2816]{1,0:T(8,128)(2,1)S(1)} collective-permute-done((bf16[64,2816]{1,0:T(8,128)(2,1)S(1)}, bf16[64,2816]{1,0:T(8,128)(2,1)S(1)}, u32[]{:S(2)}, u32[]{:S(2)}) %collective-permute-start.12) | collective-permute-done | bytes 360480 | tf_op jit(solution)/shard_map/ppermute | solution.py:76
  48.3 2.4 collective-permute-start
  52.4 3.1 collective-permute-start.1
  63.8 2.4 collective-permute-done.4
  66.9 2.5 collective-permute-start.7
  70.5 12.3 %collective-permute-done.7 = bf16[128,2048]{1,0:T(8,128)(2,1)S(1)} collective-permute-done((bf16[128,2048]{1,0:T(8,128)(2,1)S(1)}, bf16[128,2048]{1,0:T(8,128)(2,1)S(1)}, u32[]{:S(2)}, u32[]{:S(2)}) %collective-permute-start.7) | collective-permute-done | bytes 524320 | tf_op jit(solution)/shard_map/ppermute | solution.py:76
  82.8 8.4 %collective-permute-done.6 = bf16[128,2048]{1,0:T(8,128)(2,1)S(1)} collective-permute-done((bf16[128,2048]{1,0:T(8,128)(2,1)S(1)}, bf16[128,2048]{1,0:T(8,128)(2,1)S(1)}, u32[]{:S(2)}, u32[]{:S(2)}) %collective-permute-start.6) | collective-permute-done | bytes 524320 | tf_op jit(solution)/shard_map/ppermute | solution.py:76
  92.8 19.8 %all-gather.4.cloned.1.call-done = bf16[2048,1536]{1,0:T(8,128)(2,1)} async-done(((bf16[256,1536]{1,0:T(8,128)(2,1)}), bf16[2048,1536]{1,0:T(8,128)(2,1)}) %all-gather.4.cloned.1.call-update) | async-done | bytes 6291472 | tf_op jit(solution)/shard_map/all_gather | solution.py:454
  112.7 2.8 collective-permute-start.14
  116.6 6.2 %fusion.103.proj_ref = f32[512,1536]{1,0:T(8,128)S(1)} fusion(bf16[512,2048]{1,0:T(8,128)(2,1)} %pad_maximum_fusion.1, bf16[2048,1536]{1,0:T(8,128)(2,1)} %all-gather.4.cloned.1.call-done), kind=kOutput, calls=%fused_computation.278 | convolution fusion | flops 3221225472 | bytes 11534336 | tf_op jit(solution)/shard_map/dot_general | solution.py:30
  122.8 3.9 collective-permute-done.14
  130.8 5.5 collective-permute-done.19
  138.7 3.4 shard_map.334
  150.7 2.3 fusion.18
  165.6 3.2 fusion.99
  178.3 15.5 %collective-permute-done.25 = bf16[128,2048]{1,0:T(8,128)(2,1)} collective-permute-done((bf16[128,2048]{1,0:T(8,128)(2,1)}, bf16[128,2048]{1,0:T(8,128)(2,1)}, u32[]{:S(2)}, u32[]{:S(2)}) %collective-permute-start.25) | collective-permute-done | bytes 524320 | tf_op jit(solution)/shard_map/ppermute | solution.py:76
  193.8 11.2 %collective-permute-done.23 = bf16[128,2048]{1,0:T(8,128)(2,1)} collective-permute-done((bf16[128,2048]{1,0:T(8,128)(2,1)}, bf16[128,2048]{1,0:T(8,128)(2,1)}, u32[]{:S(2)}, u32[]{:S(2)}) %collective-permute-start.23) | collective-permute-done | bytes 524320 | tf_op jit(solution)/shard_map/ppermute | solution.py:76
  210.8 2.4 collective-permute-start.29
  213.2 19.2 %collective-permute-done.28 = bf16[128,2048]{1,0:T(8,128)(2,1)S(1)} collective-permute-done((bf16[128,2048]{1,0:T(8,128)(2,1)}, bf16[128,2048]{1,0:T(8,128)(2,1)S(1)}, u32[]{:S(2)}, u32[]{:S(2)}) %collective-permute-start.28) | collective-permute-done | bytes 524320 | tf_op jit(solution)/shard_map/ppermute | solution.py:76
  232.3 3.2 collective-permute-done.29
  237.4 10.0 %collective-permute-done.30 = bf16[128,2048]{1,0:T(8,128)(2,1)S(1)} collective-permute-done((bf16[128,2048]{1,0:T(8,128)(2,1)S(1)}, bf16[128,2048]{1,0:T(8,128)(2,1)S(1)}, u32[]{:S(2)}, u32[]{:S(2)}) %collective-permute-start.30) | collective-permute-done | bytes 524320 | tf_op jit(solution)/shard_map/ppermute | solution.py:76
  249.4 11.6 %fusion.104 = f32[512,2816]{1,0:T(8,128)} fusion(bf16[512,2048]{1,0:T(8,128)(2,1)S(1)} %pad_maximum_fusion.3, bf16[2048,2816]{1,0:T(8,128)(2,1)} %all-gather.6.cloned.1.call-done), kind=kOutput, calls=%fused_computation.279 | convolution fusion | flops 5905580032 | bytes 19398656 | tf_op jit(solution)/shard_map/dot_general | solution.py:30
  264.3 10.5 %multiply_convert_fusion.2 = (bf16[512,1408]{1,0:T(8,128)(2,1)S(1)}, bf16[512,1408]{1,0:T(8,128)(2,1)S(1)}, bf16[512,1408]{1,0:T(8,128)(2,1)}) fusion(f32[512,2816]{1,0:T(8,128)} %fusion.104, bf16[512,2048]{1,0:T(8,128)(2,1)} %constant_dynamic-update-slice_fusion.9, bf16[1408,2048]{1,0:T(8,128)(2,1)} %all-gather.8.cloned.1.call-done), kind=kOutput, calls=%fused_computation.24 | convolution fusion | flops 2963603456 | bytes 17956864 | tf_op jit(solution)/shard_map/dot_general | solution.py:30
  276.4 8.9 %convolution_convert_fusion = bf16[2048,2816]{1,0:T(8,128)(2,1)} fusion(bf16[512,2048]{1,0:T(8,128)(2,1)S(1)} %copy-done.33, bf16[512,1408]{1,0:T(8,128)(2,1)S(1)} %get-tuple-element.184, bf16[512,1408]{1,0:T(8,128)(2,1)S(1)} %get-tuple-element.183), kind=kOutput, calls=%fused_computation | convolution fusion | flops 5917114368 | bytes 16515072 | tf_op jit(solution)/shard_map/dot_general | solution.py:30
  285.3 10.0 %fusion.100 = (bf16[512,2048]{1,0:T(8,128)(2,1)S(1)}, f32[512,2048]{1,0:T(8,128)S(1)}) fusion(bf16[2048,2816]{1,0:T(8,128)(2,1)} %all-gather.6.cloned.1.call-done, bf16[512,1408]{1,0:T(8,128)(2,1)} %copy-done.66, bf16[512,1408]{1,0:T(8,128)(2,1)} %copy-done.65), kind=kOutput, calls=%fused_computation.275 | convolution fusion | flops 5912395776 | bytes 20709376 | tf_op jit(solution)/shard_map/dot_general | solution.py:30
  297.6 17.0 %collective-permute-done.32 = bf16[128,2048]{1,0:T(8,128)(2,1)S(1)} collective-permute-done((bf16[128,2048]{1,0:T(8,128)(2,1)S(1)}, bf16[128,2048]{1,0:T(8,128)(2,1)S(1)}, u32[]{:S(2)}, u32[]{:S(2)}) %collective-permute-start.32) | collective-permute-done | bytes 524320 | tf_op jit(solution)/shard_map/ppermute | solution.py:76
  314.7 3.5 collective-permute-start.33
  318.2 5.2 convolution_convert_fusion.2
  323.4 2.5 copy-done.24
  327.8 4.9 collective-permute-done.33
  334.4 3.4 fusion.101
  338.8 2.2 collective-permute-start.38
  345.4 6.6 %collective-permute-done.38 = bf16[128,2048]{1,0:T(8,128)(2,1)S(1)} collective-permute-done((bf16[128,2048]{1,0:T(8,128)(2,1)S(1)}, bf16[128,2048]{1,0:T(8,128)(2,1)S(1)}, u32[]{:S(2)}, u32[]{:S(2)}) %collective-permute-start.38) | collective-permute-done | bytes 524320 | tf_op jit(solution)/shard_map/ppermute | solution.py:76
  352.0 2.5 collective-permute-start.40
  355.4 3.6 collective-permute-done.37
  359.8 2.6 collective-permute-start.39
  368.3 2.3 pad_maximum_fusion.4
  370.7 9.5 %collective-permute-done.39 = bf16[128,2048]{1,0:T(8,128)(2,1)} collective-permute-done((bf16[128,2048]{1,0:T(8,128)(2,1)}, bf16[128,2048]{1,0:T(8,128)(2,1)}, u32[]{:S(2)}, u32[]{:S(2)}) %collective-permute-start.39) | collective-permute-done | bytes 524320 | tf_op jit(solution)/shard_map/ppermute | solution.py:76
  380.2 2.7 fusion.44
  382.8 5.9 %fusion = bf16[4,176,2048]{2,1,0:T(8,128)(2,1)} fusion(bf16[4,176,2048]{2,1,0:T(8,128)(2,1)} %collective-permute-done.41, bf16[4,2,176,2048]{3,2,1,0:T(8,128)(2,1)} %bitcast.214, s32[]{:T(128)S(6)} %select_n.214), kind=kLoop, calls=%fused_computation.4 | loop fusion | flops 5767168 | bytes 8650756 | tf_op jit(solution)/shard_map/convert_element_type | solution.py:160
  388.7 2.7 convolution_convert_fusion.3
  392.4 4.3 multiply_reduce_fusion.4
  397.4 2.9 collective-permute-done.42
  401.1 2.9 collective-permute-done.43
  404.8 3.2 shard_map.337
  408.3 4.1 collective-permute-start.45
  418.2 5.7 %convolution_convert_fusion.1 = bf16[2048,1536]{1,0:T(8,128)(2,1)} fusion(bf16[512,2048]{1,0:T(8,128)(2,1)S(1)} %copy-done.30, bf16[512,512]{1,0:T(8,128)(2,1)S(1)} %get-tuple-element.189, bf16[512,512]{1,0:T(8,128)(2,1)S(1)} %get-tuple-element.187, bf16[512,512]{1,0:T(8,128)(2,1)S(1)} %get-tuple-element.186), kind=kOutput, calls=%fused_computation.1 | convolution fusion | flops 3229089792 | bytes 9961472 | tf_op jit(solution)/shard_map/dot_general | solution.py:30
  425.2 7.8 %fusion.102 = (bf16[512,2048]{1,0:T(8,128)(2,1)S(1)}, f32[512,2048]{1,0:T(8,128)}) fusion(bf16[2048,1536]{1,0:T(8,128)(2,1)} %all-gather.4.cloned.1.call-done, bf16[512,512]{1,0:T(8,128)(2,1)S(1)} %copy-done.44, bf16[512,512]{1,0:T(8,128)(2,1)S(1)} %copy-done.48, bf16[512,512]{1,0:T(8,128)(2,1)S(1)} %copy-done.46), kind=kOutput, calls=%fused_computation.277 | convolution fusion | flops 3226992640 | bytes 14155776 | tf_op jit(solution)/shard_map/dot_general | solution.py:30
  435.1 2.6 collective-permute-start.47
  441.3 8.0 %collective-permute-done.49 = bf16[128,2048]{1,0:T(8,128)(2,1)S(1)} collective-permute-done((bf16[128,2048]{1,0:T(8,128)(2,1)}, bf16[128,2048]{1,0:T(8,128)(2,1)S(1)}, u32[]{:S(2)}, u32[]{:S(2)}) %collective-permute-start.49) | collective-permute-done | bytes 524320 | tf_op jit(solution)/shard_map/ppermute | solution.py:76
  449.7 23.4 %collective-permute-done.48 = bf16[128,2048]{1,0:T(8,128)(2,1)} collective-permute-done((bf16[128,2048]{1,0:T(8,128)(2,1)}, bf16[128,2048]{1,0:T(8,128)(2,1)}, u32[]{:S(2)}, u32[]{:S(2)}) %collective-permute-start.48) | collective-permute-done | bytes 524320 | tf_op jit(solution)/shard_map/ppermute | solution.py:76
  477.6 6.7 %collective-permute-done.51 = bf16[176,2048]{1,0:T(8,128)(2,1)} collective-permute-done((bf16[176,2048]{1,0:T(8,128)(2,1)}, bf16[176,2048]{1,0:T(8,128)(2,1)}, u32[]{:S(2)}, u32[]{:S(2)}) %collective-permute-start.51) | collective-permute-done | bytes 720928 | tf_op jit(solution)/shard_map/ppermute | solution.py:76
  484.3 3.5 multiply_reduce_fusion.2
  490.5 2.4 dynamic-slice_bitcast_fusion.4
  498.1 2.8 collective-permute-start.60
  500.9 2.2 collective-permute-start.61
  503.2 2.8 collective-permute-done.61
  522.2 5.3 multiply_subtract_fusion.2
  530.6 3.1 multiply_subtract_fusion.1
  533.7 13.6 %collective-permute-done.55.refs_3_ = bf16[64,2816]{1,0:T(8,128)(2,1)S(1)} collective-permute-done((bf16[64,2816]{1,0:T(8,128)(2,1)S(1)}, bf16[64,2816]{1,0:T(8,128)(2,1)S(1)}, u32[]{:S(2)}, u32[]{:S(2)}) %collective-permute-start.55) | collective-permute-done | bytes 360480 | tf_op jit(solution)/shard_map/ppermute | solution.py:76
  548.0 5.1 multiply_subtract_fusion
  (380 shorter events, 135.5 us)
Async XLA Ops:
  7.2 105.4 %all-gather.4.cloned.1.call-start = ((), (), s32[]{:S(2)}) async-start(), calls=%async_computation.3 | async-start | bytes 7077888 | tf_op jit(solution)/shard_map/all_gather | solution.py:454
  10.4 8.9 %collective-permute-start.10 = (bf16[64,1536]{1,0:T(8,128)(2,1)}, bf16[64,1536]{1,0:T(8,128)(2,1)S(1)}, u32[]{:S(2)}, u32[]{:S(2)}) collective-permute-start(bf16[64,1536]{1,0:T(8,128)(2,1)} %get-tuple-element.232), channel_id=1, source_target_pairs={{0,6},{2,4},{4,2},{6,0},{1,7},{3,5},{5,3},{7,1},{8,14},{10,12},{12... | collective-permute-start | bytes 589832 | tf_op jit(solution)/shard_map/ppermute | solution.py:76
  12.8 9.6 %collective-permute-start.9 = (bf16[64,1536]{1,0:T(8,128)(2,1)}, bf16[64,1536]{1,0:T(8,128)(2,1)}, u32[]{:S(2)}, u32[]{:S(2)}) collective-permute-start(bf16[64,1536]{1,0:T(8,128)(2,1)} %get-tuple-element.233), channel_id=1, source_target_pairs={{0,4},{2,6},{4,0},{6,2},{1,5},{3,7},{5,1},{7,3},{8,12},{10,14},{12... | collective-permute-start | bytes 589832 | tf_op jit(solution)/shard_map/ppermute | solution.py:76
  13.3 9.2 %collective-permute-start.8 = (bf16[64,1536]{1,0:T(8,128)(2,1)S(1)}, bf16[64,1536]{1,0:T(8,128)(2,1)}, u32[]{:S(2)}, u32[]{:S(2)}) collective-permute-start(bf16[64,1536]{1,0:T(8,128)(2,1)S(1)} %get-tuple-element.234), channel_id=1, source_target_pairs={{0,2},{2,0},{4,6},{6,4},{1,3},{3,1},{5,7},{7,5},{8,10},{10,8},{12,... | collective-permute-start | bytes 589832 | tf_op jit(solution)/shard_map/ppermute | solution.py:76
  14.7 26.0 %collective-permute-start.13 = (bf16[64,2816]{1,0:T(8,128)(2,1)S(1)}, bf16[64,2816]{1,0:T(8,128)(2,1)S(1)}, u32[]{:S(2)}, u32[]{:S(2)}) collective-permute-start(bf16[64,2816]{1,0:T(8,128)(2,1)S(1)} %get-tuple-element.218), channel_id=1, source_target_pairs={{0,24},{8,16},{16,8},{24,0},{1,25},{9,17},{17,9},{25,1},{2,26},{10... | collective-permute-start | bytes 1081352 | tf_op jit(solution)/shard_map/ppermute | solution.py:76
  16.3 30.0 %collective-permute-start.12 = (bf16[64,2816]{1,0:T(8,128)(2,1)S(1)}, bf16[64,2816]{1,0:T(8,128)(2,1)S(1)}, u32[]{:S(2)}, u32[]{:S(2)}) collective-permute-start(bf16[64,2816]{1,0:T(8,128)(2,1)S(1)} %get-tuple-element.219), channel_id=1, source_target_pairs={{0,16},{8,24},{16,0},{24,8},{1,17},{9,25},{17,1},{25,9},{2,18},{10... | collective-permute-start | bytes 1081352 | tf_op jit(solution)/shard_map/ppermute | solution.py:76
  19.3 27.0 %collective-permute-start.11 = (bf16[64,2816]{1,0:T(8,128)(2,1)S(1)}, bf16[64,2816]{1,0:T(8,128)(2,1)S(1)}, u32[]{:S(2)}, u32[]{:S(2)}) collective-permute-start(bf16[64,2816]{1,0:T(8,128)(2,1)S(1)} %get-tuple-element.220), channel_id=1, source_target_pairs={{0,8},{8,0},{16,24},{24,16},{1,9},{9,1},{17,25},{25,17},{2,10},{10... | collective-permute-start | bytes 1081352 | tf_op jit(solution)/shard_map/ppermute | solution.py:76
  48.0 161.6 %all-gather.6.cloned.1.call-start = ((), (), s32[]{:S(2)}) async-start(), calls=%async_computation.4 | async-start | bytes 12976128 | tf_op jit(solution)/shard_map/all_gather | solution.py:465
  48.3 4.0 collective-permute-start
  52.4 4.7 collective-permute-start.1
  62.2 4.0 collective-permute-start.4
  66.9 15.9 %collective-permute-start.7 = (bf16[128,2048]{1,0:T(8,128)(2,1)S(1)}, bf16[128,2048]{1,0:T(8,128)(2,1)S(1)}, u32[]{:S(2)}, u32[]{:S(2)}) collective-permute-start(bf16[128,2048]{1,0:T(8,128)(2,1)S(1)} %shard_map.331), channel_id=1, source_target_pairs={{0,6},{2,4},{4,2},{6,0},{1,7},{3,5},{5,3},{7,1},{8,14},{10,12},{12... | collective-permute-start | bytes 1572872 | tf_op jit(solution)/shard_map/ppermute | solution.py:76
  69.5 21.7 %collective-permute-start.6 = (bf16[128,2048]{1,0:T(8,128)(2,1)S(1)}, bf16[128,2048]{1,0:T(8,128)(2,1)S(1)}, u32[]{:S(2)}, u32[]{:S(2)}) collective-permute-start(bf16[128,2048]{1,0:T(8,128)(2,1)S(1)} %shard_map.331), channel_id=1, source_target_pairs={{0,4},{2,6},{4,0},{6,2},{1,5},{3,7},{5,1},{7,3},{8,12},{10,14},{12... | collective-permute-start | bytes 1572872 | tf_op jit(solution)/shard_map/ppermute | solution.py:76
  70.0 21.4 %collective-permute-start.5 = (bf16[128,2048]{1,0:T(8,128)(2,1)S(1)}, bf16[128,2048]{1,0:T(8,128)(2,1)S(1)}, u32[]{:S(2)}, u32[]{:S(2)}) collective-permute-start(bf16[128,2048]{1,0:T(8,128)(2,1)S(1)} %shard_map.331), channel_id=1, source_target_pairs={{0,2},{2,0},{4,6},{6,4},{1,3},{3,1},{5,7},{7,5},{8,10},{10,8},{12,... | collective-permute-start | bytes 1572872 | tf_op jit(solution)/shard_map/ppermute | solution.py:76
  112.7 151.7 %all-gather.8.cloned.1.call-start = ((), (), s32[]{:S(2)}) async-start(), calls=%async_computation.5 | async-start | bytes 6488064 | tf_op jit(solution)/shard_map/all_gather | solution.py:493
  112.7 14.0 %collective-permute-start.14 = (bf16[64,2048]{1,0:T(8,128)(2,1)S(1)}, bf16[64,2048]{1,0:T(8,128)(2,1)S(1)}, u32[]{:S(2)}, u32[]{:S(2)}) collective-permute-start(bf16[64,2048]{1,0:T(8,128)(2,1)S(1)} %convert_element_type.152), channel_id=1, source_target_pairs={{0,8},{8,0},{16,24},{24,16},{1,9},{9,1},{17,25},{25,17},{2,10},{10... | collective-permute-start | bytes 786440 | tf_op jit(solution)/shard_map/ppermute | solution.py:76
  115.5 13.2 %collective-permute-start.15 = (bf16[64,2048]{1,0:T(8,128)(2,1)S(1)}, bf16[64,2048]{1,0:T(8,128)(2,1)S(1)}, u32[]{:S(2)}, u32[]{:S(2)}) collective-permute-start(bf16[64,2048]{1,0:T(8,128)(2,1)S(1)} %convert_element_type.152), channel_id=1, source_target_pairs={{0,16},{8,24},{16,0},{24,8},{1,17},{9,25},{17,1},{25,9},{2,18},{10... | collective-permute-start | bytes 786440 | tf_op jit(solution)/shard_map/ppermute | solution.py:76
  128.8 7.6 %collective-permute-start.19 = (bf16[64,2048]{1,0:T(8,128)(2,1)S(1)}, bf16[64,2048]{1,0:T(8,128)(2,1)S(1)}, u32[]{:S(2)}, u32[]{:S(2)}) collective-permute-start(bf16[64,2048]{1,0:T(8,128)(2,1)S(1)} %collective-permute-done.15), channel_id=1, source_target_pairs={{0,8},{8,0},{16,24},{24,16},{1,9},{9,1},{17,25},{25,17},{2,10},{10... | collective-permute-start | bytes 786440 | tf_op jit(solution)/shard_map/ppermute | solution.py:76
  137.8 12.9 %collective-permute-start.20 = (bf16[4,64,2048]{2,1,0:T(8,128)(2,1)}, bf16[4,64,2048]{2,1,0:T(8,128)(2,1)}, u32[]{:S(2)}, u32[]{:S(2)}) collective-permute-start(bf16[4,64,2048]{2,1,0:T(8,128)(2,1)} %get-tuple-element.221), channel_id=1, source_target_pairs={{0,1},{1,0},{2,3},{3,2},{4,5},{5,4},{6,7},{7,6},{8,9},{9,8},{10,11... | collective-permute-start | bytes 3145736 | tf_op jit(solution)/shard_map/ppermute | solution.py:76
  144.0 5.8 %collective-permute-start.18 = (f32[2,512]{1,0:T(2,128)S(1)}, f32[2,512]{1,0:T(2,128)S(1)}, u32[]{:S(2)}, u32[]{:S(2)}) collective-permute-start(f32[2,512]{1,0:T(2,128)S(1)} %get-tuple-element.95), channel_id=1, source_target_pairs={{0,24},{8,16},{16,8},{24,0},{1,25},{9,17},{17,9},{25,1},{2,26},{10... | collective-permute-start | bytes 12296 | tf_op jit(solution)/shard_map/ppermute | solution.py:76
  145.2 4.7 collective-permute-start.17
  170.0 23.8 %collective-permute-start.25 = (bf16[128,2048]{1,0:T(8,128)(2,1)}, bf16[128,2048]{1,0:T(8,128)(2,1)}, u32[]{:S(2)}, u32[]{:S(2)}) collective-permute-start(bf16[128,2048]{1,0:T(8,128)(2,1)} %get-tuple-element.201), channel_id=1, source_target_pairs={{0,2},{2,0},{4,6},{6,4},{1,3},{3,1},{5,7},{7,5},{8,10},{10,8},{12,... | collective-permute-start | bytes 1572872 | tf_op jit(solution)/shard_map/ppermute | solution.py:76
  171.5 22.3 %collective-permute-start.24 = (bf16[128,2048]{1,0:T(8,128)(2,1)}, bf16[128,2048]{1,0:T(8,128)(2,1)}, u32[]{:S(2)}, u32[]{:S(2)}) collective-permute-start(bf16[128,2048]{1,0:T(8,128)(2,1)} %get-tuple-element.202), channel_id=1, source_target_pairs={{0,4},{2,6},{4,0},{6,2},{1,5},{3,7},{5,1},{7,3},{8,12},{10,14},{12... | collective-permute-start | bytes 1572872 | tf_op jit(solution)/shard_map/ppermute | solution.py:76
  173.0 32.1 %collective-permute-start.23 = (bf16[128,2048]{1,0:T(8,128)(2,1)}, bf16[128,2048]{1,0:T(8,128)(2,1)}, u32[]{:S(2)}, u32[]{:S(2)}) collective-permute-start(bf16[128,2048]{1,0:T(8,128)(2,1)} %get-tuple-element.200), channel_id=1, source_target_pairs={{0,6},{2,4},{4,2},{6,0},{1,7},{3,5},{5,3},{7,1},{8,14},{10,12},{12... | collective-permute-start | bytes 1572872 | tf_op jit(solution)/shard_map/ppermute | solution.py:76
  174.5 32.4 %collective-permute-start.26 = (bf16[128,2048]{1,0:T(8,128)(2,1)}, bf16[128,2048]{1,0:T(8,128)(2,1)S(1)}, u32[]{:S(2)}, u32[]{:S(2)}) collective-permute-start(bf16[128,2048]{1,0:T(8,128)(2,1)} %fusion.31), channel_id=1, source_target_pairs={{0,8},{8,0},{16,24},{24,16},{1,9},{9,1},{17,25},{25,17},{2,10},{10... | collective-permute-start | bytes 1572872 | tf_op jit(solution)/shard_map/ppermute | solution.py:76
  176.3 30.7 %collective-permute-start.27 = (bf16[128,2048]{1,0:T(8,128)(2,1)}, bf16[128,2048]{1,0:T(8,128)(2,1)S(1)}, u32[]{:S(2)}, u32[]{:S(2)}) collective-permute-start(bf16[128,2048]{1,0:T(8,128)(2,1)} %fusion.31), channel_id=1, source_target_pairs={{0,16},{8,24},{16,0},{24,8},{1,17},{9,25},{17,1},{25,9},{2,18},{10... | collective-permute-start | bytes 1572872 | tf_op jit(solution)/shard_map/ppermute | solution.py:76
  209.6 181.7 %reduce-scatter.6.cloned.1.call-start = ((), (), s32[]{:S(2)}) async-start(), calls=%async_computation.7 | async-start | bytes 12976128 | tf_op jit(solution)/shard_map/reduce_scatter | solution.py:512
  210.2 22.2 %collective-permute-start.28 = (bf16[128,2048]{1,0:T(8,128)(2,1)}, bf16[128,2048]{1,0:T(8,128)(2,1)S(1)}, u32[]{:S(2)}, u32[]{:S(2)}) collective-permute-start(bf16[128,2048]{1,0:T(8,128)(2,1)} %copy-done.4), channel_id=1, source_target_pairs={{0,8},{8,0},{16,24},{24,16},{1,9},{9,1},{17,25},{25,17},{2,10},{10... | collective-permute-start | bytes 1572872 | tf_op jit(solution)/shard_map/ppermute | solution.py:76
  210.8 24.8 %collective-permute-start.29 = (bf16[128,2048]{1,0:T(8,128)(2,1)}, bf16[128,2048]{1,0:T(8,128)(2,1)S(1)}, u32[]{:S(2)}, u32[]{:S(2)}) collective-permute-start(bf16[128,2048]{1,0:T(8,128)(2,1)} %copy-done.4), channel_id=1, source_target_pairs={{0,16},{8,24},{16,0},{24,8},{1,17},{9,25},{17,1},{25,9},{2,18},{10... | collective-permute-start | bytes 1572872 | tf_op jit(solution)/shard_map/ppermute | solution.py:76
  235.5 11.9 %collective-permute-start.30 = (bf16[128,2048]{1,0:T(8,128)(2,1)S(1)}, bf16[128,2048]{1,0:T(8,128)(2,1)S(1)}, u32[]{:S(2)}, u32[]{:S(2)}) collective-permute-start(bf16[128,2048]{1,0:T(8,128)(2,1)S(1)} %collective-permute-done.29), channel_id=1, source_target_pairs={{0,8},{8,0},{16,24},{24,16},{1,9},{9,1},{17,25},{25,17},{2,10},{10... | collective-permute-start | bytes 1572872 | tf_op jit(solution)/shard_map/ppermute | solution.py:76
  248.7 14.8 %collective-permute-start.31 = (bf16[128,2048]{1,0:T(8,128)(2,1)S(1)}, bf16[128,2048]{1,0:T(8,128)(2,1)S(1)}, u32[]{:S(2)}, u32[]{:S(2)}) collective-permute-start(bf16[128,2048]{1,0:T(8,128)(2,1)S(1)} %copy-done.52), channel_id=1, source_target_pairs={{0,8},{8,0},{16,24},{24,16},{1,9},{9,1},{17,25},{25,17},{2,10},{10... | collective-permute-start | bytes 1572872 | tf_op jit(solution)/shard_map/ppermute | solution.py:76
  285.3 207.5 %reduce-scatter.8.cloned.1.call-start = ((), (), s32[]{:S(2)}) async-start(), calls=%async_computation.8 | async-start | bytes 2359296 | tf_op jit(solution)/shard_map/reduce_scatter | solution.py:534
  295.5 19.1 %collective-permute-start.32 = (bf16[128,2048]{1,0:T(8,128)(2,1)S(1)}, bf16[128,2048]{1,0:T(8,128)(2,1)S(1)}, u32[]{:S(2)}, u32[]{:S(2)}) collective-permute-start(bf16[128,2048]{1,0:T(8,128)(2,1)S(1)} %get-tuple-element.198), channel_id=1, source_target_pairs={{0,8},{8,0},{16,24},{24,16},{1,9},{9,1},{17,25},{25,17},{2,10},{10... | collective-permute-start | bytes 1572872 | tf_op jit(solution)/shard_map/ppermute | solution.py:76
  296.6 31.2 %collective-permute-start.34 = (bf16[128,2048]{1,0:T(8,128)(2,1)S(1)}, bf16[128,2048]{1,0:T(8,128)(2,1)S(1)}, u32[]{:S(2)}, u32[]{:S(2)}) collective-permute-start(bf16[128,2048]{1,0:T(8,128)(2,1)S(1)} %get-tuple-element.199), channel_id=1, source_target_pairs={{0,8},{8,0},{16,24},{24,16},{1,9},{9,1},{17,25},{25,17},{2,10},{10... | collective-permute-start | bytes 1572872 | tf_op jit(solution)/shard_map/ppermute | solution.py:76
  314.7 18.0 %collective-permute-start.33 = (bf16[128,2048]{1,0:T(8,128)(2,1)S(1)}, bf16[128,2048]{1,0:T(8,128)(2,1)S(1)}, u32[]{:S(2)}, u32[]{:S(2)}) collective-permute-start(bf16[128,2048]{1,0:T(8,128)(2,1)S(1)} %fusion.26), channel_id=1, source_target_pairs={{0,16},{8,24},{16,0},{24,8},{1,17},{9,25},{17,1},{25,9},{2,18},{10... | collective-permute-start | bytes 1572872 | tf_op jit(solution)/shard_map/ppermute | solution.py:76
  327.8 55.0 %collective-permute-start.41 = (bf16[4,176,2048]{2,1,0:T(8,128)(2,1)}, bf16[4,176,2048]{2,1,0:T(8,128)(2,1)}, u32[]{:S(2)}, u32[]{:S(2)}) collective-permute-start(bf16[4,176,2048]{2,1,0:T(8,128)(2,1)} %dynamic-slice_bitcast_fusion), channel_id=1, source_target_pairs={{0,1},{1,0},{2,3},{3,2},{4,5},{5,4},{6,7},{7,6},{8,9},{9,8},{10,11... | collective-permute-start | bytes 8650760 | tf_op jit(solution)/shard_map/ppermute | solution.py:76
  338.8 13.2 %collective-permute-start.38 = (bf16[128,2048]{1,0:T(8,128)(2,1)S(1)}, bf16[128,2048]{1,0:T(8,128)(2,1)S(1)}, u32[]{:S(2)}, u32[]{:S(2)}) collective-permute-start(bf16[128,2048]{1,0:T(8,128)(2,1)S(1)} %get-tuple-element.196), channel_id=1, source_target_pairs={{0,8},{8,0},{16,24},{24,16},{1,9},{9,1},{17,25},{25,17},{2,10},{10... | collective-permute-start | bytes 1572872 | tf_op jit(solution)/shard_map/ppermute | solution.py:76
  341.9 17.1 %collective-permute-start.37 = (bf16[128,2048]{1,0:T(8,128)(2,1)}, bf16[128,2048]{1,0:T(8,128)(2,1)S(1)}, u32[]{:S(2)}, u32[]{:S(2)}) collective-permute-start(bf16[128,2048]{1,0:T(8,128)(2,1)} %convert_element_type.164), channel_id=1, source_target_pairs={{0,6},{2,4},{4,2},{6,0},{1,7},{3,5},{5,3},{7,1},{8,14},{10,12},{12... | collective-permute-start | bytes 1572872 | tf_op jit(solution)/shard_map/ppermute | solution.py:76
  342.6 25.7 %collective-permute-start.36 = (bf16[128,2048]{1,0:T(8,128)(2,1)}, bf16[128,2048]{1,0:T(8,128)(2,1)}, u32[]{:S(2)}, u32[]{:S(2)}) collective-permute-start(bf16[128,2048]{1,0:T(8,128)(2,1)} %convert_element_type.164), channel_id=1, source_target_pairs={{0,4},{2,6},{4,0},{6,2},{1,5},{3,7},{5,1},{7,3},{8,12},{10,14},{12... | collective-permute-start | bytes 1572872 | tf_op jit(solution)/shard_map/ppermute | solution.py:76
  344.0 24.3 %collective-permute-start.35 = (bf16[128,2048]{1,0:T(8,128)(2,1)}, bf16[128,2048]{1,0:T(8,128)(2,1)}, u32[]{:S(2)}, u32[]{:S(2)}) collective-permute-start(bf16[128,2048]{1,0:T(8,128)(2,1)} %convert_element_type.164), channel_id=1, source_target_pairs={{0,2},{2,0},{4,6},{6,4},{1,3},{3,1},{5,7},{7,5},{8,10},{10,8},{12,... | collective-permute-start | bytes 1572872 | tf_op jit(solution)/shard_map/ppermute | solution.py:76
  352.0 18.6 %collective-permute-start.40 = (bf16[128,2048]{1,0:T(8,128)(2,1)}, bf16[128,2048]{1,0:T(8,128)(2,1)}, u32[]{:S(2)}, u32[]{:S(2)}) collective-permute-start(bf16[128,2048]{1,0:T(8,128)(2,1)} %get-tuple-element.197), channel_id=1, source_target_pairs={{0,8},{8,0},{16,24},{24,16},{1,9},{9,1},{17,25},{25,17},{2,10},{10... | collective-permute-start | bytes 1572872 | tf_op jit(solution)/shard_map/ppermute | solution.py:76
  359.8 20.3 %collective-permute-start.39 = (bf16[128,2048]{1,0:T(8,128)(2,1)}, bf16[128,2048]{1,0:T(8,128)(2,1)}, u32[]{:S(2)}, u32[]{:S(2)}) collective-permute-start(bf16[128,2048]{1,0:T(8,128)(2,1)} %fusion.22), channel_id=1, source_target_pairs={{0,16},{8,24},{16,0},{24,8},{1,17},{9,25},{17,1},{25,9},{2,18},{10... | collective-permute-start | bytes 1572872 | tf_op jit(solution)/shard_map/ppermute | solution.py:76
  391.4 103.9 %reduce-scatter.4.cloned.1.call-start = ((), (), s32[]{:S(2)}) async-start(), calls=%async_computation.6 | async-start | bytes 7077888 | tf_op jit(solution)/shard_map/reduce_scatter | solution.py:569
  408.0 4.9 collective-permute-start.46
  408.3 5.8 %collective-permute-start.45 = (f32[2,512]{1,0:T(2,128)S(1)}, f32[2,512]{1,0:T(2,128)S(1)}, u32[]{:S(2)}, u32[]{:S(2)}) collective-permute-start(f32[2,512]{1,0:T(2,128)S(1)} %get-tuple-element.125), channel_id=1, source_target_pairs={{0,16},{8,24},{16,0},{24,8},{1,17},{9,25},{17,1},{25,9},{2,18},{10... | collective-permute-start | bytes 12296 | tf_op jit(solution)/shard_map/ppermute | solution.py:76
  434.2 15.1 %collective-permute-start.49 = (bf16[128,2048]{1,0:T(8,128)(2,1)}, bf16[128,2048]{1,0:T(8,128)(2,1)S(1)}, u32[]{:S(2)}, u32[]{:S(2)}) collective-permute-start(bf16[128,2048]{1,0:T(8,128)(2,1)} %get-tuple-element.194), channel_id=1, source_target_pairs={{0,2},{2,0},{4,6},{6,4},{1,3},{3,1},{5,7},{7,5},{8,10},{10,8},{12,... | collective-permute-start | bytes 1572872 | tf_op jit(solution)/shard_map/ppermute | solution.py:76
  434.6 38.5 %collective-permute-start.48 = (bf16[128,2048]{1,0:T(8,128)(2,1)}, bf16[128,2048]{1,0:T(8,128)(2,1)}, u32[]{:S(2)}, u32[]{:S(2)}) collective-permute-start(bf16[128,2048]{1,0:T(8,128)(2,1)} %get-tuple-element.195), channel_id=1, source_target_pairs={{0,4},{2,6},{4,0},{6,2},{1,5},{3,7},{5,1},{7,3},{8,12},{10,14},{12... | collective-permute-start | bytes 1572872 | tf_op jit(solution)/shard_map/ppermute | solution.py:76
  435.1 38.1 %collective-permute-start.47 = (bf16[128,2048]{1,0:T(8,128)(2,1)}, bf16[128,2048]{1,0:T(8,128)(2,1)}, u32[]{:S(2)}, u32[]{:S(2)}) collective-permute-start(bf16[128,2048]{1,0:T(8,128)(2,1)} %get-tuple-element.193), channel_id=1, source_target_pairs={{0,6},{2,4},{4,2},{6,0},{1,7},{3,5},{5,3},{7,1},{8,14},{10,12},{12... | collective-permute-start | bytes 1572872 | tf_op jit(solution)/shard_map/ppermute | solution.py:76
  439.1 38.6 %collective-permute-start.52 = (bf16[176,2048]{1,0:T(8,128)(2,1)}, bf16[176,2048]{1,0:T(8,128)(2,1)}, u32[]{:S(2)}, u32[]{:S(2)}) collective-permute-start(bf16[176,2048]{1,0:T(8,128)(2,1)} %get-tuple-element.191), channel_id=1, source_target_pairs={{0,6},{2,4},{4,2},{6,0},{1,7},{3,5},{5,3},{7,1},{8,14},{10,12},{12... | collective-permute-start | bytes 2162696 | tf_op jit(solution)/shard_map/ppermute | solution.py:76
  439.4 44.9 %collective-permute-start.51 = (bf16[176,2048]{1,0:T(8,128)(2,1)}, bf16[176,2048]{1,0:T(8,128)(2,1)}, u32[]{:S(2)}, u32[]{:S(2)}) collective-permute-start(bf16[176,2048]{1,0:T(8,128)(2,1)} %get-tuple-element.192), channel_id=1, source_target_pairs={{0,4},{2,6},{4,0},{6,2},{1,5},{3,7},{5,1},{7,3},{8,12},{10,14},{12... | collective-permute-start | bytes 2162696 | tf_op jit(solution)/shard_map/ppermute | solution.py:76
  449.3 35.1 %collective-permute-start.50 = (bf16[176,2048]{1,0:T(8,128)(2,1)}, bf16[176,2048]{1,0:T(8,128)(2,1)S(1)}, u32[]{:S(2)}, u32[]{:S(2)}) collective-permute-start(bf16[176,2048]{1,0:T(8,128)(2,1)} %get-tuple-element.190), channel_id=1, source_target_pairs={{0,2},{2,0},{4,6},{6,4},{1,3},{3,1},{5,7},{7,5},{8,10},{10,8},{12,... | collective-permute-start | bytes 2162696 | tf_op jit(solution)/shard_map/ppermute | solution.py:76
  498.1 5.0 collective-permute-start.60
  500.9 5.1 collective-permute-start.61
  503.1 3.9 collective-permute-start.59
  507.0 5.0 collective-permute-start.63
  508.5 4.8 collective-permute-start.64
  510.0 3.9 collective-permute-start.62
  510.6 23.1 %collective-permute-start.53 = (bf16[64,2816]{1,0:T(8,128)(2,1)}, bf16[64,2816]{1,0:T(8,128)(2,1)S(1)}, u32[]{:S(2)}, u32[]{:S(2)}) collective-permute-start(bf16[64,2816]{1,0:T(8,128)(2,1)} %get-tuple-element.131), channel_id=1, source_target_pairs={{0,8},{8,0},{16,24},{24,16},{1,9},{9,1},{17,25},{25,17},{2,10},{10... | collective-permute-start | bytes 1081352 | tf_op jit(solution)/shard_map/ppermute | solution.py:76
  511.1 22.5 %collective-permute-start.54 = (bf16[64,2816]{1,0:T(8,128)(2,1)}, bf16[64,2816]{1,0:T(8,128)(2,1)S(1)}, u32[]{:S(2)}, u32[]{:S(2)}) collective-permute-start(bf16[64,2816]{1,0:T(8,128)(2,1)} %get-tuple-element.132), channel_id=1, source_target_pairs={{0,16},{8,24},{16,0},{24,8},{1,17},{9,25},{17,1},{25,9},{2,18},{10... | collective-permute-start | bytes 1081352 | tf_op jit(solution)/shard_map/ppermute | solution.py:76
  513.9 4.1 collective-permute-start.65
  516.0 13.6 %collective-permute-start.56 = (bf16[64,1536]{1,0:T(8,128)(2,1)}, bf16[64,1536]{1,0:T(8,128)(2,1)S(1)}, u32[]{:S(2)}, u32[]{:S(2)}) collective-permute-start(bf16[64,1536]{1,0:T(8,128)(2,1)} %get-tuple-element.225), channel_id=1, source_target_pairs={{0,2},{2,0},{4,6},{6,4},{1,3},{3,1},{5,7},{7,5},{8,10},{10,8},{12,... | collective-permute-start | bytes 589832 | tf_op jit(solution)/shard_map/ppermute | solution.py:76
  517.0 12.8 %collective-permute-start.57 = (bf16[64,1536]{1,0:T(8,128)(2,1)}, bf16[64,1536]{1,0:T(8,128)(2,1)S(1)}, u32[]{:S(2)}, u32[]{:S(2)}) collective-permute-start(bf16[64,1536]{1,0:T(8,128)(2,1)} %get-tuple-element.224), channel_id=1, source_target_pairs={{0,4},{2,6},{4,0},{6,2},{1,5},{3,7},{5,1},{7,3},{8,12},{10,14},{12... | collective-permute-start | bytes 589832 | tf_op jit(solution)/shard_map/ppermute | solution.py:76
  518.1 11.7 %collective-permute-start.58 = (bf16[64,1536]{1,0:T(8,128)(2,1)S(1)}, bf16[64,1536]{1,0:T(8,128)(2,1)S(1)}, u32[]{:S(2)}, u32[]{:S(2)}) collective-permute-start(bf16[64,1536]{1,0:T(8,128)(2,1)S(1)} %get-tuple-element.223), channel_id=1, source_target_pairs={{0,6},{2,4},{4,2},{6,0},{1,7},{3,5},{5,3},{7,1},{8,14},{10,12},{12... | collective-permute-start | bytes 589832 | tf_op jit(solution)/shard_map/ppermute | solution.py:76
  529.6 17.7 %collective-permute-start.55 = (bf16[64,2816]{1,0:T(8,128)(2,1)S(1)}, bf16[64,2816]{1,0:T(8,128)(2,1)S(1)}, u32[]{:S(2)}, u32[]{:S(2)}) collective-permute-start(bf16[64,2816]{1,0:T(8,128)(2,1)S(1)} %copy-done.56), channel_id=1, source_target_pairs={{0,24},{8,16},{16,8},{24,0},{1,25},{9,17},{17,9},{25,1},{2,26},{10... | collective-permute-start | bytes 1081352 | tf_op jit(solution)/shard_map/ppermute | solution.py:76
  (77 other events, 583.7 us)
Sparse Core Ops, SparseCore 0:
  48.1 64.4 all-gather.3
  115.1 78.0 all-gather.5
  209.8 42.4 all-gather.7
  285.4 102.2 reduce-scatter.5
  391.5 32.3 reduce-scatter.7
  426.0 69.2 reduce-scatter.3
